TPU v7x, 32 devices: a whole 2x2x4 slice. The times are simulated.
32 devices in a mesh: dp: 2 (over x), tensor: 4 (over y, core), bucket: 4 (over z).
Axes of the slice: x: 2, y: 2, z: 4, core: 2. Of those that a mesh axis runs over, the one named last changes fastest.
Arguments:
- tokens: bfloat16 [8192, 2048], P(('dp', 'bucket')), may hold values from -6 to 6
- cotangent: bfloat16 [8192, 2048], P(('dp', 'bucket')), may hold values from -6 to 6
- lengths: int32 [8, 3], P(('dp', 'bucket')), may hold values from 1 to 768, 1024 in all within a row
- head_quarters: int32 [8192], P(('dp', 'bucket')), may hold values from 1 to 4
- buckets: int32 [8192, 1], P(('dp', 'bucket')), may hold values from 0 to 3, as said below
- ln1_gain: float32 [2048], replicated, may hold values from 0.5 to 1.5
- ln1_bias: float32 [2048], replicated, may hold values from -1.2 to 1.2
- w_qkv: bfloat16 [2048, 3, 2048], P(None, None, 'tensor'), may hold values from -0.125 to 0.125
- w_out: bfloat16 [2048, 2048], P('tensor'), may hold values from -0.5 to 0.5
- ln2_gain: float32 [2048], replicated, may hold values from 0.5 to 1.5
- ln2_bias: float32 [2048], replicated, may hold values from -1.2 to 1.2
- w_router: bfloat16 [2048, 4], replicated, may hold values from -0.09375 to 0.09375
- w_up: bfloat16 [2048, 4, 2048], P(None, 'bucket', 'tensor'), may hold values from -0.125 to 0.125
- w_down: bfloat16 [4, 2048, 2048], P('bucket', 'tensor'), may hold values from -0.25 to 0.25
Outputs:
- mixed: bfloat16 [8192, 2048], P(('dp', 'bucket'))
- tokens_grad: float32 [8192, 2048], P(('dp', 'bucket'))
- ln1_gain_grad: float32 [2048], P(('dp', 'bucket'))
- ln1_bias_grad: float32 [2048], P(('dp', 'bucket'))
- w_qkv_grad: float32 [2048, 3, 2048], P(('dp', 'bucket'), None, 'tensor')
- w_out_grad: float32 [2048, 2048], P('tensor', ('dp', 'bucket'))
- ln2_gain_grad: float32 [2048], P(('dp', 'bucket'))
- ln2_bias_grad: float32 [2048], P(('dp', 'bucket'))
- w_router_grad: float32 [2048, 4], P(('dp', 'bucket'))
- w_up_grad: float32 [2048, 4, 2048], P('dp', 'bucket', 'tensor')
- w_down_grad: float32 [4, 2048, 2048], P('bucket', 'tensor', 'dp')
Inputs may be any that keep to these rules, and one draw needn't show every extreme that they name: `lengths`: each row sums to 1024. `buckets`: a token uses the hidden units of levels 0 to its level.
All inputs are finite; a program needn't handle non-finite values.
Results may differ from a plain program's by a relative error of at most 0.018.
Values may be sent and summed in bfloat16 or wider, within the bound.
A program may use at most 320 MiB of HBM per device.

v0:
```python
import math

import jax
import jax.numpy as jnp
from jax import lax
from jax.sharding import PartitionSpec as P

HEAD_DIM = 128
QBLOCK = 512


EPS = 1e-05
HIGH = lax.Precision.HIGHEST
NEGATIVE = -1e30


def norm_forward(values, gain, shift):
    centred = values - jnp.mean(values, -1, keepdims=True)
    inverse = lax.rsqrt(jnp.mean(centred * centred, -1, keepdims=True) + EPS)
    normed = centred * inverse
    return (normed * gain + shift, normed, inverse)


def norm_backward(grad_in, normed, inverse, gain):
    scaled = grad_in * gain
    inner = (
        scaled
        - jnp.mean(scaled, -1, keepdims=True)
        - normed * jnp.mean(scaled * normed, -1, keepdims=True)
    )
    return (inverse * inner, jnp.sum(grad_in * normed, 0), jnp.sum(grad_in, 0))


def softmax(scores):
    row_max = jnp.max(scores, -1, keepdims=True)
    expo = jnp.exp(scores - row_max)
    return expo / jnp.sum(expo, -1, keepdims=True)


def layout(lengths_row, tok_rows):
    ends = jnp.cumsum(lengths_row)
    starts = ends - lengths_row
    tok_index = jnp.arange(tok_rows, dtype=jnp.int32)
    segments = jnp.sum((tok_index[:, None] >= ends[None, :]).astype(jnp.int32), 1)
    chosen = segments[:, None] == jnp.arange(lengths_row.shape[0], dtype=jnp.int32)[None, :]
    positions = tok_index - jnp.sum(jnp.where(chosen, starts[None, :], 0), 1)
    return (positions, segments)


def tables(positions):
    half_dim = HEAD_DIM // 2
    freq = jnp.exp(jnp.arange(half_dim, dtype=jnp.float32) * (-math.log(10000.0) / half_dim))
    angle = positions.astype(jnp.float32)[:, None] * freq[None, :]
    return (jnp.cos(angle)[:, None, :], jnp.sin(angle)[:, None, :])


def rotate(values, cosine, sine):
    half_dim = values.shape[-1] // 2
    first_half, second_half = (values[..., :half_dim], values[..., half_dim:])
    return jnp.concatenate(
        [first_half * cosine - second_half * sine, second_half * cosine + first_half * sine], -1
    )


def rotate_back(grads, cosine, sine):
    half_dim = grads.shape[-1] // 2
    first_half, second_half = (grads[..., :half_dim], grads[..., half_dim:])
    return jnp.concatenate(
        [first_half * cosine + second_half * sine, second_half * cosine - first_half * sine], -1
    )


def local(
    tokens,
    cotangent,
    lengths,
    head_quarters,
    buckets,
    ln1_gain,
    ln1_bias,
    w_qkv,
    w_out,
    ln2_gain,
    ln2_bias,
    w_router,
    w_up,
    w_down,
):
    tok_rows, model_width = tokens.shape
    splits = lax.axis_size("tensor")
    owners = lax.axis_size("bucket")
    share_rows = tok_rows // splits
    tensor_rank = lax.axis_index("tensor")
    local_heads = w_qkv.shape[2] // HEAD_DIM
    scale = HEAD_DIM ** (-0.5)
    inputs = tokens.astype(jnp.float32)
    positions, segments = layout(lengths[0], tok_rows)
    tok_index = jnp.arange(tok_rows, dtype=jnp.int32)
    levels_tok = buckets[:, 0]
    head_keep = (tensor_rank < head_quarters).astype(jnp.bfloat16)[:, None]
    normed1, hat1, inverse1 = norm_forward(inputs, ln1_gain, ln1_bias)
    normed1_low = normed1.astype(jnp.bfloat16)
    qkv_flat = w_qkv.reshape(model_width, -1)
    projected = jnp.dot(normed1_low, qkv_flat, preferred_element_type=jnp.float32).reshape(
        tok_rows, 3, local_heads, HEAD_DIM
    )
    cosine, sine = tables(positions)
    queries = rotate(projected[:, 0], cosine, sine).astype(jnp.bfloat16)
    key_heads = rotate(projected[:, 1], cosine, sine).astype(jnp.bfloat16)
    value_heads = projected[:, 2].astype(jnp.bfloat16)
    blocks = tok_rows // QBLOCK
    query_blocks = queries.reshape(blocks, QBLOCK, local_heads, HEAD_DIM)
    segment_blocks = segments.reshape(blocks, QBLOCK)
    index_blocks = tok_index.reshape(blocks, QBLOCK)

    def block_scores(query_block, segment_block, index_block):
        allowed = (segment_block[:, None] == segments[None, :]) & (
            tok_index[None, :] <= index_block[:, None]
        )
        scores = (
            jnp.einsum("qhd,khd->hqk", query_block, key_heads, preferred_element_type=jnp.float32)
            * scale
        )
        return jnp.where(allowed[None], scores, NEGATIVE)

    def forward_block(block_item):
        query_block, segment_block, index_block = block_item
        scores = block_scores(query_block, segment_block, index_block)
        row_max = jnp.max(scores, -1, keepdims=True)
        expo = jnp.exp(scores - row_max)
        row_total = jnp.sum(expo, -1, keepdims=True)
        weights = (expo / row_total).astype(jnp.bfloat16)
        heads_out = jnp.einsum(
            "hqk,khd->qhd", weights, value_heads, preferred_element_type=jnp.float32
        )
        return (heads_out, (row_max + jnp.log(row_total))[..., 0])

    head_blocks, log_totals = lax.map(forward_block, (query_blocks, segment_blocks, index_blocks))
    heads_low = head_blocks.reshape(tok_rows, -1).astype(jnp.bfloat16) * head_keep
    attention = lax.psum(jnp.dot(heads_low, w_out, preferred_element_type=jnp.float32), "tensor")
    middle = inputs + attention
    normed2, hat2, inverse2 = norm_forward(middle, ln2_gain, ln2_bias)
    normed2_low = normed2.astype(jnp.bfloat16)
    logits = jnp.dot(normed2_low, w_router, preferred_element_type=jnp.float32)
    router_probs = softmax(logits)
    onehot = (levels_tok[:, None] == jnp.arange(owners, dtype=jnp.int32)[None, :]).astype(
        jnp.float32
    )
    gate_tok = jnp.sum(router_probs * onehot, -1)
    up_flat = w_up.reshape(model_width, -1)
    down_flat = w_down.reshape(-1, model_width)
    active = levels_tok.reshape(splits, 1, share_rows) >= jnp.arange(
        owners, dtype=jnp.int32
    ).reshape(1, owners, 1)
    outgoing = jnp.where(
        active[..., None],
        normed2_low.reshape(splits, 1, share_rows, model_width),
        jnp.zeros((), jnp.bfloat16),
    )
    arrived = lax.all_to_all(outgoing, "bucket", split_axis=1, concat_axis=1, tiled=True).reshape(
        -1, model_width
    )
    up_act = jnp.dot(arrived, up_flat, preferred_element_type=jnp.float32)
    hidden = jnp.square(jnp.maximum(up_act, 0.0)).astype(jnp.bfloat16)
    terms = jnp.dot(hidden, down_flat, preferred_element_type=jnp.float32)
    summed = lax.psum_scatter(terms, ("tensor", "bucket"), scatter_dimension=0, tiled=True).astype(
        jnp.bfloat16
    )
    branch = lax.all_gather(summed, "tensor", axis=0, tiled=True).astype(jnp.float32)
    mixed = (middle + gate_tok[:, None] * branch).astype(jnp.bfloat16)
    grad_output = cotangent.astype(jnp.float32)
    grad_branch = (gate_tok[:, None] * grad_output).astype(jnp.bfloat16)
    grad_gate = jnp.sum(grad_output * branch, -1)
    grad_logits = (grad_gate * gate_tok)[:, None] * (onehot - router_probs)
    grad_router = jnp.dot(
        normed2_low.T, grad_logits, precision=HIGH, preferred_element_type=jnp.float32
    )
    grad_norm2 = jnp.dot(
        grad_logits,
        w_router.astype(jnp.float32).T,
        precision=HIGH,
        preferred_element_type=jnp.float32,
    )
    grad_share = lax.dynamic_slice_in_dim(grad_branch, tensor_rank * share_rows, share_rows, 0)
    grad_arrived = lax.all_gather(grad_share, ("tensor", "bucket"), axis=0, tiled=True)
    grad_hidden = jnp.dot(grad_arrived, down_flat.T, preferred_element_type=jnp.float32)
    grad_up_act = (grad_hidden * 2.0 * jnp.maximum(up_act, 0.0)).astype(jnp.bfloat16)
    grad_down_local = jnp.dot(hidden.T, grad_arrived, preferred_element_type=jnp.float32)
    grad_up_local = jnp.dot(arrived.T, grad_up_act, preferred_element_type=jnp.float32)
    returned = lax.psum_scatter(
        jnp.dot(grad_up_act, up_flat.T, preferred_element_type=jnp.float32),
        ("tensor", "bucket"),
        scatter_dimension=0,
        tiled=True,
    ).astype(jnp.bfloat16)
    grad_norm2 = grad_norm2 + lax.all_gather(returned, "tensor", axis=0, tiled=True).astype(
        jnp.float32
    )
    grad_up_part, grad_down_part = (
        lax.psum_scatter(
            grad_up_local.reshape(model_width, 1, -1), "dp", scatter_dimension=0, tiled=True
        ),
        lax.psum_scatter(
            grad_down_local.reshape(1, -1, model_width), "dp", scatter_dimension=2, tiled=True
        ),
    )
    grad_norm_in2, grad_ln2_gain, grad_ln2_bias = norm_backward(
        grad_norm2, hat2, inverse2, ln2_gain
    )
    grad_middle = grad_output + grad_norm_in2
    grad_attention = grad_middle.astype(jnp.bfloat16)
    grad_w_out = jnp.dot(heads_low.T, grad_attention, preferred_element_type=jnp.float32)
    grad_heads = (
        jnp.dot(grad_attention, w_out.T, preferred_element_type=jnp.float32).astype(jnp.bfloat16)
        * head_keep
    )
    grad_head_blocks = grad_heads.reshape(blocks, QBLOCK, local_heads, HEAD_DIM)

    def backward_block(carry, block_item):
        grad_keys, grad_values = carry
        query_block, grad_block, log_block, segment_block, index_block = block_item
        scores = block_scores(query_block, segment_block, index_block)
        probs = jnp.exp(scores - log_block[..., None])
        grad_probs = jnp.einsum(
            "qhd,khd->hqk", grad_block, value_heads, preferred_element_type=jnp.float32
        )
        grad_scores = (
            probs * (grad_probs - jnp.sum(probs * grad_probs, -1, keepdims=True))
        ).astype(jnp.bfloat16)
        grad_query = (
            jnp.einsum("hqk,khd->qhd", grad_scores, key_heads, preferred_element_type=jnp.float32)
            * scale
        )
        grad_keys = (
            grad_keys
            + jnp.einsum(
                "hqk,qhd->khd", grad_scores, query_block, preferred_element_type=jnp.float32
            )
            * scale
        )
        grad_values = grad_values + jnp.einsum(
            "hqk,qhd->khd",
            probs.astype(jnp.bfloat16),
            grad_block,
            preferred_element_type=jnp.float32,
        )
        return ((grad_keys, grad_values), grad_query)

    zero_heads = jnp.zeros((tok_rows, local_heads, HEAD_DIM), jnp.float32)
    (grad_keys, grad_values), grad_queries = lax.scan(
        backward_block,
        (zero_heads, zero_heads),
        (query_blocks, grad_head_blocks, log_totals, segment_blocks, index_blocks),
    )
    grad_queries = grad_queries.reshape(tok_rows, local_heads, HEAD_DIM)
    grad_q_raw = rotate_back(grad_queries.astype(jnp.bfloat16), cosine, sine).astype(jnp.bfloat16)
    grad_k_raw = rotate_back(grad_keys.astype(jnp.bfloat16), cosine, sine).astype(jnp.bfloat16)
    grad_projected = jnp.stack(
        [grad_q_raw, grad_k_raw, grad_values.astype(jnp.bfloat16)], 1
    ).reshape(tok_rows, -1)
    grad_w_qkv = jnp.dot(normed1_low.T, grad_projected, preferred_element_type=jnp.float32).reshape(
        model_width, 3, -1
    )
    grad_norm1 = lax.psum(
        jnp.dot(grad_projected, qkv_flat.T, preferred_element_type=jnp.float32), "tensor"
    )
    grad_norm_in1, grad_ln1_gain, grad_ln1_bias = norm_backward(
        grad_norm1, hat1, inverse1, ln1_gain
    )
    tokens_grad = grad_middle + grad_norm_in1
    reduced = (
        lax.psum_scatter(grad_w_qkv, ("dp", "bucket"), scatter_dimension=0, tiled=True),
        lax.psum_scatter(grad_w_out, ("dp", "bucket"), scatter_dimension=1, tiled=True),
        lax.psum_scatter(grad_router, ("dp", "bucket"), scatter_dimension=0, tiled=True),
        lax.psum_scatter(grad_ln1_gain, ("dp", "bucket"), scatter_dimension=0, tiled=True),
        lax.psum_scatter(grad_ln1_bias, ("dp", "bucket"), scatter_dimension=0, tiled=True),
        lax.psum_scatter(grad_ln2_gain, ("dp", "bucket"), scatter_dimension=0, tiled=True),
        lax.psum_scatter(grad_ln2_bias, ("dp", "bucket"), scatter_dimension=0, tiled=True),
    )
    return (
        mixed,
        tokens_grad,
        reduced[3],
        reduced[4],
        reduced[0],
        reduced[1],
        reduced[5],
        reduced[6],
        reduced[2],
        grad_up_part,
        grad_down_part,
    )


def solution(mesh):
    placed = (
        P(("dp", "bucket"), None),
        P(("dp", "bucket"), None),
        P(("dp", "bucket"), None),
        P(("dp", "bucket")),
        P(("dp", "bucket"), None),
        P(),
        P(),
        P(None, None, "tensor"),
        P("tensor", None),
        P(),
        P(),
        P(),
        P(None, "bucket", "tensor"),
        P("bucket", "tensor", None),
    )
    return jax.shard_map(
        local,
        mesh=mesh,
        in_specs=placed,
        out_specs=(
            P(("dp", "bucket"), None),
            P(("dp", "bucket"), None),
            P(("dp", "bucket")),
            P(("dp", "bucket")),
            P(("dp", "bucket"), None, "tensor"),
            P("tensor", ("dp", "bucket")),
            P(("dp", "bucket")),
            P(("dp", "bucket")),
            P(("dp", "bucket"), None),
            P("dp", "bucket", "tensor"),
            P("bucket", "tensor", "dp"),
        ),
        check_vma=False,
    )
```

profile of v0, /device:TPU:0, one launch (start us, length us, event | category | flops | bytes accessed | tf_op | source)
XLA Modules:
  0.0 2160.0 jit_solution(13665125081042234562)
XLA Ops:
  10.3 3.4 fusion.51
  13.7 8.9 copy.83
  22.6 10.5 fusion.55
  38.3 4.0 subtract_convert_fusion
  53.8 3.1 pad_maximum_fusion.1
  58.0 21.0 while.28
  59.1 2.9 fusion.152
  64.4 3.3 fusion.154
  69.4 2.9 fusion.152
  74.7 3.3 fusion.154
  82.4 7.4 fusion.86
  89.9 6.5 convert_element_type.138
  96.4 149.1 %all-reduce.8.cloned.1.call-done = f32[1024,2048]{1,0:T(8,128)} async-done(((f32[1024,2048]{1,0:T(8,128)}), f32[1024,2048]{1,0:T(8,128)}) %all-reduce.8.cloned.1.call-update) | async-done | bytes 8388624 | tf_op jit(solution)/shard_map/psum | solution.py:140
  245.6 5.5 fusion.106
  260.6 4.5 broadcast_select_fusion
  265.1 468.0 %all_to_all.5 = bf16[4,4,256,2048]{3,2,0,1:T(8,128)(2,1)S(1)} all-to-all(bf16[4,4,256,2048]{3,2,0,1:T(8,128)(2,1)S(1)} %broadcast_select_fusion), channel_id=1, replica_groups=mesh['dp'=2,'tensor'=4,'bucket'=4] {'bucket'}, dimensions={1} | all-to-all | bytes 33554432 | tf_op jit(solution)/shard_map/all_to_all | solution.py:160
  733.2 6.5 copy.89
  739.7 14.5 fusion.65
  754.2 18.8 fusion.61
  773.0 15.8 multiply_convert_fusion.1
  791.1 20.7 fusion.63
  811.9 292.6 %reduce-scatter.10.cloned.1.call-done = f32[256,2048]{1,0:T(8,128)} async-done(((f32[4096,2048]{1,0:T(8,128)}), f32[256,2048]{1,0:T(8,128)}) %reduce-scatter.10.cloned.1.call-update) | async-done | bytes 2097168 | tf_op jit(solution)/shard_map/reduce_scatter | solution.py:166
  1107.2 333.1 %reduce-scatter.12.cloned.1.call-done = f32[256,2048]{1,0:T(8,128)} async-done(((f32[4096,2048]{1,0:T(8,128)}), f32[256,2048]{1,0:T(8,128)}) %reduce-scatter.12.cloned.1.call-update) | async-done | bytes 2097168 | tf_op jit(solution)/shard_map/reduce_scatter | solution.py:190
  1443.1 15.3 convolution_bitcast_fusion.1
  1458.8 16.6 all-gather.4.cloned.1.call-done
  1475.4 4.8 fusion.54
  1480.1 5.6 fusion.95
  1486.2 25.6 %all-gather.8.cloned.1.call-done = bf16[1024,2048]{1,0:T(8,128)(2,1)} async-done(((bf16[256,2048]{1,0:T(8,128)(2,1)}), bf16[1024,2048]{1,0:T(8,128)(2,1)}) %all-gather.8.cloned.1.call-update) | async-done | bytes 4194320 | tf_op jit(solution)/shard_map/all_gather | solution.py:196
  1511.9 12.2 multiply_reduce_fusion.1
  1524.1 11.2 multiply_add_fusion
  1535.3 3.4 copy-done.8
  1538.7 5.0 fusion.74
  1547.0 34.9 %while.29 = (s32[]{:T(128)}, f32[1024,4,128]{0,2,1:T(8,128)S(1)}, f32[1024,4,128]{0,2,1:T(8,128)}, bf16[2,512,4,128]{3,1,2,0:T(8,128)(2,1)}, bf16[2,512,4,128]{3...) while((s32[]{:T(128)}, f32[1024,4,128]{0,2,1:T(8,128)S(1)}, ...), condition=%wide.region_22.23_spmd.clone, body=%wide.region_20.22_spmd.clone.sunk | while | flops 2720266240 | bytes 97591584 | solution.py:250
  1551.4 3.8 bitcast_add_fusion.5
  1555.2 3.5 multiply_reduce_fusion.7
  1568.1 5.1 bitcast_add_fusion.5
  1573.2 3.5 multiply_reduce_fusion.7
  1592.3 9.5 fusion.108
  1601.9 16.3 convolution_bitcast_fusion
  1618.4 7.8 fusion.67
  1626.4 14.8 fusion.57
  1643.1 5.2 copy.95
  1649.8 140.4 %all-reduce.10.cloned.1.call-done = f32[1024,2048]{1,0:T(8,128)} async-done(((f32[1024,2048]{1,0:T(8,128)}), f32[1024,2048]{1,0:T(8,128)}) %all-reduce.10.cloned.1.call-update) | async-done | bytes 8388624 | tf_op jit(solution)/shard_map/psum | solution.py:264
  1790.2 6.5 fusion.50
  1796.8 38.1 %all-reduce.4 = (f32[2048]{0:T(1024)S(1)}, f32[2048]{0:T(1024)S(1)}, f32[2048]{0:T(1024)S(1)}, f32[2048]{0:T(1024)S(1)}) all-reduce(f32[2048]{0:T(1024)S(1)} %get-tuple-element.361, f32[2048]{0:T(1024)S(1)} %get-tuple-element.366, f32[2048]{0:T(1024)S(1)} %copy-done.42, ...), channel_id=4, replica_groups=mesh['dp'=2,'tensor'=4,'bucket'=4] {'dp','bucket'}, use_global_device_ids=true, to_apply=%region_27.28.clone | all-reduce | flops 8192 | bytes 65536
  1837.4 12.2 fusion.49
  1849.6 91.5 %reduce-scatter.16.cloned.1.call-done = f32[512,256]{1,0:T(8,128)} async-done(((f32[512,2048]{1,0:T(8,128)}), f32[512,256]{1,0:T(8,128)}) %reduce-scatter.16.cloned.1.call-update) | async-done | bytes 524304 | tf_op jit(solution)/shard_map/reduce_scatter | solution.py:273
  1941.1 211.6 %reduce-scatter.14.cloned.1.call-done = f32[256,3,512]{2,0,1:T(8,128)} async-done(((f32[2048,3,512]{2,0,1:T(8,128)}), f32[256,3,512]{2,0,1:T(8,128)}) %reduce-scatter.14.cloned.1.call-update) | async-done | bytes 1572880 | tf_op jit(solution)/shard_map/reduce_scatter | solution.py:272
  (236 shorter events, 88.2 us)
Async XLA Ops:
  7.2 747.0 %copy-start = (bf16[1,512,2048]{2,1,0:T(8,128)(2,1)S(1)}, bf16[1,512,2048]{2,1,0:T(8,128)(2,1)}, u32[]{:S(2)}) copy-start(bf16[1,512,2048]{2,1,0:T(8,128)(2,1)} %param.31) | copy-start | bytes 6291460
  7.2 238.4 %all-reduce.8.cloned.1.call-start = ((), (), s32[]{:S(2)}) async-start(), calls=%async_computation.8 | async-start | bytes 16777216 | tf_op jit(solution)/shard_map/psum | solution.py:140
  10.2 12.4 copy-start.30
  10.2 12.3 copy-start.39
  10.2 12.3 copy-start.48
  13.7 8.9 copy-start.36
  58.0 23.4 %copy-start.45 = (s32[1024]{0:T(1024)S(1)}, s32[1024]{0:T(1024)}, u32[]{:S(2)}) copy-start(s32[1024]{0:T(1024)} %param.21) | copy-start | bytes 12292
  59.1 5.4 copy-start.10
  59.1 5.4 copy-start.16
  69.3 5.4 copy-start.10
  69.4 5.4 copy-start.16
  79.0 10.8 copy-start.3
  79.0 10.8 copy-start.22
  79.0 10.9 copy-start.24
  79.0 10.9 copy-start.26
  79.0 10.9 copy-start.28
  89.9 683.1 %all-gather.6.cloned.1.call-start = ((), (), s32[]{:S(2)}) async-start(), calls=%async_computation.11 | async-start | bytes 17825792 | tf_op jit(solution)/shard_map/all_gather | solution.py:185
  259.4 845.1 %reduce-scatter.10.cloned.1.call-start = ((), (), s32[]{:S(2)}) async-start(), calls=%async_computation.9 | async-start | bytes 35651584 | tf_op jit(solution)/shard_map/reduce_scatter | solution.py:166
  733.2 6.5 copy-start.46
  773.0 667.4 %reduce-scatter.12.cloned.1.call-start = ((), (), s32[]{:S(2)}) async-start(), calls=%async_computation.12 | async-start | bytes 35651584 | tf_op jit(solution)/shard_map/reduce_scatter | solution.py:190
  773.0 18.1 copy-start.47
  811.8 663.6 %all-gather.4.cloned.1.call-start = ((), (), s32[]{:S(2)}) async-start(), calls=%async_computation.10 | async-start | bytes 5242880 | tf_op jit(solution)/shard_map/all_gather | solution.py:169
  1107.2 404.7 %all-gather.8.cloned.1.call-start = ((), (), s32[]{:S(2)}) async-start(), calls=%async_computation.13 | async-start | bytes 5242880 | tf_op jit(solution)/shard_map/all_gather | solution.py:196
  1443.1 200.0 %reduce-scatter.18.cloned.1.call-start = ((), (), s32[]{:S(2)}) async-start(), calls=%async_computation.17 | async-start | bytes 6291456 | tf_op jit(solution)/shard_map/reduce_scatter | solution.py:200
  1458.4 189.8 %reduce-scatter.22.cloned.1.call-start = ((), (), s32[]{:S(2)}) async-start(), calls=%async_computation.19 | async-start | bytes 1179648
  1485.7 304.5 %all-reduce.10.cloned.1.call-start = ((), (), s32[]{:S(2)}) async-start(), calls=%async_computation.14 | async-start | bytes 16777216 | tf_op jit(solution)/shard_map/psum | solution.py:264
  1511.9 12.2 copy-start.9
  1524.1 14.6 copy-start.33
  1538.7 8.3 copy-start.4
  1538.7 8.3 copy-start.23
  1538.7 8.3 copy-start.25
  1538.7 8.3 copy-start.27
  1538.7 8.3 copy-start.29
  1568.1 5.1 copy-start.11
  1581.9 6.2 copy-start.20
  1586.1 6.3 slice-start
  1601.9 16.5 copy-start.13
  1601.9 16.5 copy-start.34
  1601.9 247.7 %reduce-scatter.20.cloned.1.call-start = ((), (), s32[]{:S(2)}) async-start(), calls=%async_computation.18 | async-start | bytes 6291456 | tf_op jit(solution)/shard_map/reduce_scatter | solution.py:203
  1618.3 8.0 copy-start.31
  1618.3 8.0 copy-start.37
  1618.3 8.0 copy-start.40
  1618.3 8.0 copy-start.49
  1618.4 322.7 %reduce-scatter.16.cloned.1.call-start = ((), (), s32[]{:S(2)}) async-start(), calls=%async_computation.16 | async-start | bytes 4718592 | tf_op jit(solution)/shard_map/reduce_scatter | solution.py:273
  1626.3 526.4 %reduce-scatter.14.cloned.1.call-start = ((), (), s32[]{:S(2)}) async-start(), calls=%async_computation.15 | async-start | bytes 14155776 | tf_op jit(solution)/shard_map/reduce_scatter | solution.py:272
  1643.0 153.7 %copy-start.42 = (f32[2048]{0:T(1024)S(1)}, f32[2048]{0:T(1024)}, u32[]{:S(2)}) copy-start(f32[2048]{0:T(1024)} %get-tuple-element.359) | copy-start | bytes 24580
  1643.0 153.7 %copy-start.43 = (f32[2048]{0:T(1024)S(1)}, f32[2048]{0:T(1024)}, u32[]{:S(2)}) copy-start(f32[2048]{0:T(1024)} %get-tuple-element.365) | copy-start | bytes 24580
  1837.4 315.3 %copy-start.1 = (bf16[1,512,2048]{2,1,0:T(8,128)(2,1)S(1)}, bf16[1,512,2048]{2,1,0:T(8,128)(2,1)}, u32[]{:S(2)}) copy-start(bf16[1,512,2048]{2,1,0:T(8,128)(2,1)} %param.31) | copy-start | bytes 6291460
  (26 other events, 64.7 us)
Sparse Core Ops, SparseCore 0:
  90.0 155.5 all-reduce.7
  259.5 276.4 all-gather.5
  773.1 331.2 reduce-scatter.9
  1108.5 331.7 reduce-scatter.11
  1441.8 33.5 all-gather.3
  1477.4 34.4 all-gather.7
  1514.2 54.2 reduce-scatter.17
  1572.3 63.4 reduce-scatter.21
  1638.3 151.8 all-reduce.9
  1792.9 55.1 reduce-scatter.19
  1852.7 88.2 reduce-scatter.15
  1945.1 207.5 reduce-scatter.13
where the time goes:
time: 2170 us; the launch traced here: 2160 us
  waiting for transfers between devices  1260 us (58%)
  blocking collectives  506 us (23%)
  matrix products  214 us (10%)
  other arithmetic  94.9 us (4%)
  local copies, waits for them, and re-layouts  66.1 us (3%)
    all_to_all x1, blocking collectives, local(): lax.all_to_all(outgoing, 'bucket', split_axis=1, concat_axis=1, tiled=True)  468 us
    reduce_scatter x1, waiting for transfers between devices, local(): lax.psum_scatter(jnp.dot(grad_up_act, up_flat.T, preferred_element_type=j...  333 us
    reduce_scatter x1, waiting for transfers between devices, local(): lax.psum_scatter(terms, ('tensor', 'bucket'), scatter_dimension=0, tiled=...  293 us
    reduce_scatter x1, waiting for transfers between devices, local(): lax.psum_scatter(grad_w_qkv, ('dp', 'bucket'), scatter_dimension=0, tiled...  212 us
    psum x1, waiting for transfers between devices, local(): lax.psum(jnp.dot(heads_low, w_out, preferred_element_type=jnp.float32), '...  149 us
    psum x1, waiting for transfers between devices, local(): lax.psum(jnp.dot(grad_projected, qkv_flat.T, preferred_element_type=jnp.f...  140 us
    reduce_scatter x1, waiting for transfers between devices, local(): lax.psum_scatter(grad_w_out, ('dp', 'bucket'), scatter_dimension=1, tiled...  91.5 us
  transfers between devices with their start and end apart: 12, of which 8 were waited for; matrix products, arithmetic and copies ran while one was open for 13% of the time, Pallas kernels for 0%

commit v1 on v0

v1 whole, which is shorter than its diff:
```python
import functools
import math

import jax
import jax.numpy as jnp
from jax import lax
from jax.experimental import pallas as pl
from jax.experimental.pallas import tpu as pltpu
from jax.sharding import PartitionSpec as P

HEAD_DIM = 128
QBLOCK = 256
EPS = 1e-05
HIGH = lax.Precision.HIGHEST
NEGATIVE = -1e30
F32 = jnp.float32
BF16 = jnp.bfloat16


def norm_parts(values):
    centred = values - jnp.mean(values, -1, keepdims=True)
    inverse = lax.rsqrt(jnp.mean(centred * centred, -1, keepdims=True) + EPS)
    return centred * inverse, inverse


def norm_backward(grad_in, normed, inverse, gain):
    scaled = grad_in * gain
    inner = (
        scaled
        - jnp.mean(scaled, -1, keepdims=True)
        - normed * jnp.mean(scaled * normed, -1, keepdims=True)
    )
    return inverse * inner, jnp.sum(grad_in * normed, 0), jnp.sum(grad_in, 0)


def softmax(scores):
    expo = jnp.exp(scores - jnp.max(scores, -1, keepdims=True))
    return expo / jnp.sum(expo, -1, keepdims=True)


def layout(lengths_row, tok_rows):
    ends = jnp.cumsum(lengths_row)
    starts = ends - lengths_row
    tok_index = jnp.arange(tok_rows, dtype=jnp.int32)
    segments = jnp.sum((tok_index[:, None] >= ends[None, :]).astype(jnp.int32), 1)
    chosen = segments[:, None] == jnp.arange(lengths_row.shape[0], dtype=jnp.int32)[None, :]
    first = jnp.sum(jnp.where(chosen, starts[None, :], 0), 1)
    return tok_index - first, first


def tables(positions):
    half_dim = HEAD_DIM // 2
    freq = jnp.exp(jnp.arange(half_dim, dtype=F32) * (-math.log(10000.0) / half_dim))
    angle = positions.astype(F32)[:, None] * freq[None, :]
    cosine, sine = jnp.cos(angle), jnp.sin(angle)
    return jnp.concatenate([cosine, cosine], -1), jnp.concatenate([-sine, sine], -1)


def dot(left, right, dims):
    return lax.dot_general(left, right, (dims, ((), ())), preferred_element_type=F32)


NN = ((1,), (0,))
NT = ((1,), (1,))
TN = ((0,), (0,))


def qkv_kernel(x_ref, gain_ref, bias_ref, w_ref, cos_ref, sin_ref, n_ref, q_ref, k_ref, v_ref):
    values = x_ref[...].astype(F32)
    normed, _ = norm_parts(values)
    low = (normed * gain_ref[...] + bias_ref[...]).astype(BF16)
    n_ref[...] = low
    cosine, sine = cos_ref[...], sin_ref[...]
    width = w_ref.shape[2]
    for part, out_ref in enumerate((q_ref, k_ref, v_ref)):
        projected = dot(low, w_ref[part], NN)
        if part == 2:
            out_ref[...] = projected.astype(BF16)
            continue
        for at in range(0, width, HEAD_DIM):
            head = projected[:, at : at + HEAD_DIM]
            turned = head * cosine + pltpu.roll(head, HEAD_DIM // 2, 1) * sine
            out_ref[:, at : at + HEAD_DIM] = turned.astype(BF16)


def qkv_call(tokens, gain, bias, w3, cosine, sine):
    rows, width = tokens.shape
    own = w3.shape[2]
    wide = pl.BlockSpec((QBLOCK, width), lambda i: (i, 0))
    row = pl.BlockSpec((1, width), lambda i: (0, 0))
    table = pl.BlockSpec((QBLOCK, HEAD_DIM), lambda i: (i, 0))
    out = pl.BlockSpec((QBLOCK, own), lambda i: (i, 0))
    return pl.pallas_call(
        qkv_kernel,
        grid=(rows // QBLOCK,),
        in_specs=[wide, row, row, pl.BlockSpec(w3.shape, lambda i: (0, 0, 0)), table, table],
        out_specs=[wide, out, out, out],
        out_shape=[jax.ShapeDtypeStruct((rows, width), BF16)]
        + [jax.ShapeDtypeStruct((rows, own), BF16)] * 3,
        compiler_params=pltpu.CompilerParams(vmem_limit_bytes=40 << 20),
        cost_estimate=pl.CostEstimate(
            flops=6 * rows * width * own, bytes_accessed=2 * (2 * rows * width + 3 * width * own + 3 * rows * own), transcendentals=0
        ),
        name="qkv",
    )(tokens, gain.reshape(1, -1), bias.reshape(1, -1), w3, cosine, sine)


def masked_scores(query, keys, first, block, length):
    scores = dot(query, keys, NT) * HEAD_DIM**-0.5
    key_at = lax.broadcasted_iota(jnp.int32, (QBLOCK, length), 1)
    row_at = lax.broadcasted_iota(jnp.int32, (QBLOCK, length), 0) + block * QBLOCK
    allowed = (key_at >= first) & (key_at <= row_at)
    return jnp.where(allowed, scores, NEGATIVE)


def attend_kernel(q_ref, k_ref, v_ref, first_ref, keep_ref, o_ref, log_ref):
    for block in range(pl.num_programs(1)):

        @pl.when(pl.program_id(1) == block)
        def _():
            length = (block + 1) * QBLOCK
            scores = masked_scores(q_ref[...], k_ref[:length], first_ref[...], block, length)
            most = jnp.max(scores, -1, keepdims=True)
            expo = jnp.exp(scores - most)
            total = jnp.sum(expo, -1, keepdims=True)
            weights = (expo * (1.0 / total)).astype(BF16)
            out = dot(weights, v_ref[:length], NN)
            o_ref[...] = (out * keep_ref[...]).astype(BF16)
            log_ref[0] = most + jnp.log(total)


def attend_call(queries, keys, values, first, keep):
    rows, own = queries.shape
    heads, blocks = own // HEAD_DIM, rows // QBLOCK
    part = pl.BlockSpec((QBLOCK, HEAD_DIM), lambda h, i: (i, h))
    whole = pl.BlockSpec((rows, HEAD_DIM), lambda h, i: (0, h))
    column = pl.BlockSpec((QBLOCK, 1), lambda h, i: (i, 0))
    return pl.pallas_call(
        attend_kernel,
        grid=(heads, blocks),
        in_specs=[part, whole, whole, column, column],
        out_specs=[part, pl.BlockSpec((1, QBLOCK, 1), lambda h, i: (h, i, 0))],
        out_shape=[
            jax.ShapeDtypeStruct((rows, own), BF16),
            jax.ShapeDtypeStruct((heads, rows, 1), F32),
        ],
        compiler_params=pltpu.CompilerParams(vmem_limit_bytes=40 << 20),
        cost_estimate=pl.CostEstimate(
            flops=4 * rows * rows * own, bytes_accessed=8 * rows * own, transcendentals=heads * rows * rows
        ),
        name="attend",
    )(queries, keys, values, first, keep)


def attend_back_kernel(
    q_ref, k_ref, v_ref, go_ref, first_ref, log_ref, cos_ref, sin_ref, g_ref, dk_ref, dv_ref
):
    head, step = pl.program_id(0), pl.program_id(1)
    blocks = pl.num_programs(1)
    own = q_ref.shape[1] * pl.num_programs(0)

    @pl.when(step == 0)
    def _():
        dk_ref[...] = jnp.zeros_like(dk_ref)
        dv_ref[...] = jnp.zeros_like(dv_ref)

    def place(part):
        return pl.ds(pl.multiple_of(part * own + head * HEAD_DIM, HEAD_DIM), HEAD_DIM)

    def turn_back(grad, rows):
        grad = grad.astype(BF16).astype(F32)
        back = grad * cos_ref[rows] - pltpu.roll(grad, HEAD_DIM // 2, 1) * sin_ref[rows]
        return back.astype(BF16)

    for block in range(blocks):

        @pl.when(step == block)
        def _():
            length = (block + 1) * QBLOCK
            rows = slice(block * QBLOCK, length)
            query, keys, grad = q_ref[...], k_ref[:length], go_ref[...]
            scores = masked_scores(query, keys, first_ref[...], block, length)
            probs = jnp.exp(scores - log_ref[0])
            grad_probs = dot(grad, v_ref[:length], NT)
            inner = jnp.sum(probs * grad_probs, -1, keepdims=True)
            grad_scores = (probs * (grad_probs - inner)).astype(BF16)
            dq = dot(grad_scores, keys, NN) * HEAD_DIM**-0.5
            g_ref[rows, place(0)] = turn_back(dq, rows)
            dk_ref[:length] += dot(grad_scores, query, TN)
            dv_ref[:length] += dot(probs.astype(BF16), grad, TN)

    @pl.when(step == blocks - 1)
    def _():
        g_ref[:, place(1)] = turn_back(dk_ref[...] * HEAD_DIM**-0.5, slice(None))
        g_ref[:, place(2)] = dv_ref[...].astype(BF16)


def attend_back_call(queries, keys, values, grads, first, logs, cosine, sine):
    rows, own = queries.shape
    heads, blocks = own // HEAD_DIM, rows // QBLOCK
    part = pl.BlockSpec((QBLOCK, HEAD_DIM), lambda h, i: (i, h))
    whole = pl.BlockSpec((rows, HEAD_DIM), lambda h, i: (0, h))
    column = pl.BlockSpec((QBLOCK, 1), lambda h, i: (i, 0))
    table = pl.BlockSpec((rows, HEAD_DIM), lambda h, i: (0, 0))
    return pl.pallas_call(
        attend_back_kernel,
        grid=(heads, blocks),
        in_specs=[
            part,
            whole,
            whole,
            part,
            column,
            pl.BlockSpec((1, QBLOCK, 1), lambda h, i: (h, i, 0)),
            table,
            table,
        ],
        out_specs=pl.BlockSpec((rows, 3 * own), lambda h, i: (0, 0)),
        out_shape=jax.ShapeDtypeStruct((rows, 3 * own), BF16),
        scratch_shapes=[pltpu.VMEM((rows, HEAD_DIM), F32)] * 2,
        compiler_params=pltpu.CompilerParams(vmem_limit_bytes=40 << 20),
        cost_estimate=pl.CostEstimate(
            flops=10 * rows * rows * own, bytes_accessed=14 * rows * own, transcendentals=heads * rows * rows
        ),
        name="attend_back",
    )(queries, keys, values, grads, first, logs, cosine, sine)


def qkv_back_kernel(g_ref, w_ref, o_ref):
    own = w_ref.shape[2]
    total = dot(g_ref[:, :own], w_ref[0], NT)
    total += dot(g_ref[:, own : 2 * own], w_ref[1], NT)
    total += dot(g_ref[:, 2 * own :], w_ref[2], NT)
    o_ref[...] = total.astype(BF16)


def qkv_back_call(grads, w3):
    rows = grads.shape[0]
    width, own = w3.shape[1], w3.shape[2]
    return pl.pallas_call(
        qkv_back_kernel,
        grid=(rows // QBLOCK,),
        in_specs=[
            pl.BlockSpec((QBLOCK, 3 * own), lambda i: (i, 0)),
            pl.BlockSpec(w3.shape, lambda i: (0, 0, 0)),
        ],
        out_specs=pl.BlockSpec((QBLOCK, width), lambda i: (i, 0)),
        out_shape=jax.ShapeDtypeStruct((rows, width), BF16),
        compiler_params=pltpu.CompilerParams(vmem_limit_bytes=40 << 20),
        cost_estimate=pl.CostEstimate(
            flops=6 * rows * width * own, bytes_accessed=2 * (rows * width + 3 * width * own + 3 * rows * own), transcendentals=0
        ),
        name="qkv_back",
    )(grads, w3)


def swap(values, axis, bit):
    pairs = [(i, i ^ bit) for i in range(lax.axis_size(axis))]
    return lax.ppermute(values, axis, pairs)


def local(
    tokens,
    cotangent,
    lengths,
    head_quarters,
    buckets,
    ln1_gain,
    ln1_bias,
    w_qkv,
    w_out,
    ln2_gain,
    ln2_bias,
    w_router,
    w_up,
    w_down,
):
    tok_rows, model_width = tokens.shape
    owners = lax.axis_size("bucket")
    splits = lax.axis_size("tensor")
    copies = lax.axis_size("dp")
    share = tok_rows // splits
    t, z, x = lax.axis_index("tensor"), lax.axis_index("bucket"), lax.axis_index("dp")
    up_own = w_up.reshape(model_width, -1)
    down_own = w_down.reshape(-1, model_width)
    hidden_width = up_own.shape[1]

    def fetch(weights):
        rows = weights.shape[0] // copies
        piece = swap(lax.dynamic_slice_in_dim(weights, x * rows, rows, 0), "bucket", 2)
        return lax.all_gather(piece, "dp", axis=0, tiled=True)

    up_other, down_other = fetch(up_own), fetch(down_own)
    levels = buckets[:, 0].astype(F32).reshape(-1, HEAD_DIM)
    near_levels = swap(levels, "bucket", 1)
    near_cotangent = swap(cotangent, "bucket", 1)

    def shard(values, bit):
        return lax.dynamic_slice_in_dim(values, (t ^ bit) * share, share, 0)

    ORDER = (0, 2, 1, 3)

    def arranged(values):
        return jnp.concatenate([shard(values, bit) for bit in ORDER], 0)

    inputs = tokens.astype(F32)
    positions, first = layout(lengths[0], tok_rows)
    first = first[:, None]
    keep = (t < head_quarters).astype(F32)[:, None]
    cosine, sine = tables(positions)
    w3 = jnp.transpose(w_qkv, (1, 0, 2))
    normed1, queries, keys, values = qkv_call(tokens, ln1_gain, ln1_bias, w3, cosine, sine)
    heads_low, logs = attend_call(queries, keys, values, first, keep)

    def gather_sum(away, kept):
        both = kept + swap(away.astype(BF16), "tensor", 1).astype(F32)
        half = both.shape[0] // 2
        return both[:half] + swap(both[half:].astype(BF16), "tensor", 2).astype(F32)

    def spread(piece):
        both = jnp.concatenate([piece, swap(piece, "tensor", 2)], 0)
        return jnp.concatenate([both, swap(both, "tensor", 1)], 0)

    def natural(piece, dtype):
        whole = jnp.zeros((tok_rows, model_width), dtype)
        for at, bit in enumerate(ORDER):
            part = lax.slice_in_dim(piece, at * share, (at + 1) * share).astype(dtype)
            whole = lax.dynamic_update_slice_in_dim(whole, part, (t ^ bit) * share, 0)
        return whole

    heads_kept = jnp.concatenate([shard(heads_low, 0), shard(heads_low, 2)], 0)
    heads_away = jnp.concatenate([shard(heads_low, 1), shard(heads_low, 3)], 0)
    attention = gather_sum(dot(heads_away, w_out, NN).astype(BF16), dot(heads_kept, w_out, NN))
    inputs_own = shard(tokens, 0).astype(F32)
    middle = inputs_own + attention
    hat2, inverse2 = norm_parts(middle)
    normed2 = (hat2 * ln2_gain + ln2_bias).astype(BF16)

    near = swap(normed2, "bucket", 1)
    n2 = jnp.concatenate([spread(normed2), spread(near)], 0)

    def gate_of(rows, tok_levels):
        probs = softmax(dot(rows, w_router, NN))
        onehot = (tok_levels[:, None] == jnp.arange(owners, dtype=F32)[None, :]).astype(F32)
        return jnp.sum(probs * onehot, -1), probs, onehot

    level_all = jnp.concatenate(
        [arranged(levels.reshape(-1)), arranged(near_levels.reshape(-1))], 0
    )
    gate_all, _, _ = gate_of(n2, level_all)
    grad_all = jnp.concatenate([arranged(cotangent), arranged(near_cotangent)], 0)
    grad_branch = (gate_all[:, None] * grad_all.astype(F32)).astype(BF16)
    kept_own = (level_all >= z.astype(F32))[:, None]
    kept_other = (level_all >= (z ^ 2).astype(F32))[:, None]

    def forward(up, kept):
        act = jnp.where(kept, jnp.maximum(dot(n2, up, NN), 0.0), 0.0)
        return act.astype(BF16), jnp.square(act).astype(BF16)

    act_own, hid_own = forward(up_own, kept_own)
    act_other, hid_other = forward(up_other, kept_other)
    parts = 2 * splits

    def scatter_sum(total):
        blocks = total.astype(BF16).reshape(2, 2, 2, share, model_width)
        kept, away = blocks[:, 0], blocks[:, 1]
        both = kept.astype(F32) + swap(away, "tensor", 1).astype(F32)
        one = both[:, 0] + swap(both[:, 1].astype(BF16), "tensor", 2).astype(F32)
        return one[0] + swap(one[1].astype(BF16), "bucket", 1).astype(F32)

    branch_sum = scatter_sum(dot(hid_own, down_own, NN) + dot(hid_other, down_other, NN))

    def backward(act, down):
        grad = dot(grad_branch, down, NT)
        return (grad * 2.0 * act.astype(F32)).astype(BF16)

    gu_own, gu_other = backward(act_own, down_own), backward(act_other, down_other)
    returned = scatter_sum(dot(gu_own, up_own, NT) + dot(gu_other, up_other, NT))

    def reduce_dp(grad, dim):
        return lax.psum_scatter(grad.astype(BF16), "dp", scatter_dimension=dim, tiled=True)

    def owner_sum(own, other):
        return own.astype(F32) + swap(other, "bucket", 2).astype(F32)

    grad_down = owner_sum(
        reduce_dp(dot(grad_branch, hid_own, TN), 0), reduce_dp(dot(grad_branch, hid_other, TN), 0)
    ).T
    grad_up = owner_sum(
        reduce_dp(dot(n2, gu_own, TN), 0), reduce_dp(dot(n2, gu_other, TN), 0)
    )

    branch = branch_sum.astype(BF16).astype(F32)
    level_own = shard(levels.reshape(-1), 0)
    gate, probs, onehot = gate_of(normed2, level_own)
    mixed_own = (middle + gate[:, None] * branch).astype(BF16)
    mixed = natural(spread(mixed_own), BF16)
    grad_output = shard(cotangent, 0).astype(F32)
    grad_gate = jnp.sum(grad_output * branch, -1)
    grad_logits = (grad_gate * gate)[:, None] * (onehot - probs)
    grad_router = dot(normed2.astype(F32), grad_logits, TN)
    grad_norm2 = returned.astype(BF16).astype(F32) + dot(grad_logits, w_router.astype(F32), NT)
    grad_in2, grad_ln2_gain, grad_ln2_bias = norm_backward(grad_norm2, hat2, inverse2, ln2_gain)
    grad_middle = grad_output + grad_in2
    grad_attention = natural(spread(grad_middle.astype(BF16)), BF16)

    def reduce_all(grad):
        return lax.psum_scatter(
            grad.astype(BF16), ("dp", "bucket"), scatter_dimension=0, tiled=True
        ).astype(F32)

    grad_w_out = reduce_all(dot(grad_attention, heads_low, TN)).T
    grad_heads = (dot(grad_attention, w_out, NT).astype(BF16).astype(F32) * keep).astype(BF16)
    grad_projected = attend_back_call(
        queries, keys, values, grad_heads, first, logs, cosine, sine
    )
    partial = qkv_back_call(grad_projected, w3)
    grad_w_qkv = reduce_all(dot(normed1, grad_projected, TN)).reshape(-1, 3, w3.shape[2])
    away = jnp.concatenate([shard(partial, 1), shard(partial, 3)], 0)
    kept = jnp.concatenate([shard(partial, 0), shard(partial, 2)], 0).astype(F32)
    grad_norm1 = gather_sum(away, kept)
    hat1, inverse1 = norm_parts(inputs_own)
    grad_in1, grad_ln1_gain, grad_ln1_bias = norm_backward(grad_norm1, hat1, inverse1, ln1_gain)
    tokens_grad = natural(spread((grad_middle + grad_in1).astype(BF16)), F32)

    def reduce_small(*grads):
        stacked = jnp.stack(grads, 0)
        total = lax.psum(stacked, ("dp", "tensor", "bucket"))
        width = model_width // (copies * owners)
        return lax.dynamic_slice_in_dim(total, (x * owners + z) * width, width, 1)

    small = reduce_small(grad_ln2_gain, grad_ln2_bias, *(grad_router[:, i] for i in range(owners)))
    last = reduce_small(grad_ln1_gain, grad_ln1_bias)
    return (
        mixed,
        tokens_grad,
        last[0],
        last[1],
        grad_w_qkv,
        grad_w_out,
        small[0],
        small[1],
        small[2:].T,
        grad_up.reshape(-1, 1, hidden_width),
        grad_down.reshape(1, hidden_width, -1),
    )


def solution(mesh):
    placed = (
        P(("dp", "bucket"), None),
        P(("dp", "bucket"), None),
        P(("dp", "bucket"), None),
        P(("dp", "bucket")),
        P(("dp", "bucket"), None),
        P(),
        P(),
        P(None, None, "tensor"),
        P("tensor", None),
        P(),
        P(),
        P(),
        P(None, "bucket", "tensor"),
        P("bucket", "tensor", None),
    )
    return jax.shard_map(
        local,
        mesh=mesh,
        in_specs=placed,
        out_specs=(
            P(("dp", "bucket"), None),
            P(("dp", "bucket"), None),
            P(("dp", "bucket")),
            P(("dp", "bucket")),
            P(("dp", "bucket"), None, "tensor"),
            P("tensor", ("dp", "bucket")),
            P(("dp", "bucket")),
            P(("dp", "bucket")),
            P(("dp", "bucket"), None),
            P("dp", "bucket", "tensor"),
            P("bucket", "tensor", "dp"),
        ),
        check_vma=False,
    )
```

time: 2170 us -> 1020 us (0.47)
  waiting for transfers between devices: 1260 us -> 595 us
  blocking collectives: 506 us -> 0 us
  matrix products: 214 us -> 133 us
  Pallas kernels: 0 us -> 48.8 us
  local copies, waits for them, and re-layouts: 66.1 us -> 104 us
  starting transfers between devices: 1.22 us -> 35.7 us
    reduce_scatter x6, waiting for transfers between devices: 929 us -> 179 us  [the longest x2 179 us: reduce_all(): lax.psum_scatter(grad.astype(BF16), ('dp', 'bucket'), scatter_dimension=0...]
    all_to_all x1 -> x0, blocking collectives: 468 us -> none  [local(): lax.all_to_all(outgoing, 'bucket', split_axis=1, concat_axis=1, tiled=True)]
    ppermute x0 -> x27, waiting for transfers between devices: none -> 354 us  [swap(): return lax.ppermute(values, axis, pairs)]
    psum x2 -> x1, waiting for transfers between devices: 290 us -> 62 us  [reduce_small(): total = lax.psum(stacked, ('dp', 'tensor', 'bucket'))]
    dot_general x28 -> x21, matrix products: 208 us -> 133 us  [dot(): lax.dot_general(left, right, (dims, ((), ())), preferred_element_type=F32)]
    pallas_call x0 -> x4, Pallas kernels: none -> 48.8 us  [the longest x1 16.5 us: attend_back_call(): pl.pallas_call(attend_back_kernel, grid=(heads, blocks), in_specs=[part,...]
    all_gather x3 -> x2, waiting for transfers between devices: 42.3 us -> 0.01 us  [fetch(): return lax.all_gather(piece, 'dp', axis=0, tiled=True)]
    unnamed x1 -> x0, blocking collectives: 38.1 us -> none
  transfers between devices with their start and end apart: 12 -> 36, of which waited for: 8 -> 16; matrix products, arithmetic and copies ran while one was open for 13% -> 26% of each run, Pallas kernels for 0% -> 2%
where the time goes in v1:
time: 1020 us; the launch traced here: 1010 us
  waiting for transfers between devices  595 us (58%)
  matrix products  133 us (13%)
  local copies, waits for them, and re-layouts  104 us (10%)
  other arithmetic  76.3 us (7%)
  Pallas kernels  48.8 us (5%)
  starting transfers between devices  35.7 us (4%)
  between operations  15.3 us (2%)
    ppermute x27, waiting for transfers between devices, swap(): return lax.ppermute(values, axis, pairs)  354 us
    reduce_scatter x2, waiting for transfers between devices, reduce_all(): lax.psum_scatter(grad.astype(BF16), ('dp', 'bucket'), scatter_dimension=0...  179 us
    dot_general x21, matrix products, dot(): lax.dot_general(left, right, (dims, ((), ())), preferred_element_type=F32)  133 us
    psum x1, waiting for transfers between devices, reduce_small(): total = lax.psum(stacked, ('dp', 'tensor', 'bucket'))  62 us
    unnamed x174, local copies, waits for them, and re-layouts  55.6 us
    ppermute x27, starting transfers between devices, swap(): return lax.ppermute(values, axis, pairs)  22.9 us
  transfers between devices with their start and end apart: 36, of which 16 were waited for; matrix products, arithmetic and copies ran while one was open for 26% of the time, Pallas kernels for 2%

profile of v1, /device:TPU:0, one launch (start us, length us, event | category | flops | bytes accessed | tf_op | source)
XLA Modules:
  0.0 1008.0 jit_solution(16545910336470765155)
XLA Ops:
  10.6 3.2 fusion.46
  18.2 12.3 %qkv.1 = (bf16[1024,2048]{1,0:T(8,128)(2,1)S(1)}, bf16[1024,512]{1,0:T(8,128)(2,1)S(1)}, bf16[1024,512]{1,0:T(8,128)(2,1)S(1)}, bf16[1024,512]{1,0:T(8,128)(2,1)S(1)}) custom-call(bf16[1024,2048]{1,0:T(8,128)(2,1)S(1)} %copy-done.2, f32[1,2048]{1,0:T(1,128)S(1)} %bitcast.141, f32[1,2048]{1,0:T(1,128)S(1)} %bitcast.146, bf16[3,2048,512]{2,1,0:T(8,128)(2,1)} %bitcast.142, ...), custom_call_target="tpu_custom_call" | custom-call | flops 6442450944 | bytes 17825792 | tf_op jit(solution)/shard_map/qkv/pallas_call | solution.py:93
  30.6 12.6 %attend.1 = (bf16[1024,512]{1,0:T(8,128)(2,1)S(1)}, f32[4,1024,1]{2,1,0:T(8,128)S(1)}) custom-call(bf16[1024,512]{1,0:T(8,128)(2,1)S(1)} %get-tuple-element.17.q_ref, bf16[1024,512]{1,0:T(8,128)(2,1)S(1)} %get-tuple-element.18.k_ref, bf16[1024,512]{1,0:T(8,128)(2,1)S(1)} %get-tuple-element.19.v_ref, s32[1024,1]{1,0:T(8,128)S(1)} %copy.41.first_ref, ...), custom_call_target="tpu_custom_call" | custom-call | flops 2147483648 | bytes 4194304 | tf_op jit(solution)/shard_map/attend/pallas_call | solution.py:138
  45.2 3.8 collective-permute-done
  66.2 13.0 %collective-permute-done.1 = bf16[256,2048]{1,0:T(8,128)(2,1)} collective-permute-done((bf16[256,2048]{1,0:T(8,128)(2,1)}, bf16[256,2048]{1,0:T(8,128)(2,1)}, u32[]{:S(2)}, u32[]{:S(2)}) %collective-permute-start.1) | collective-permute-done | bytes 1048608 | tf_op jit(solution)/shard_map/ppermute | solution.py:259
  79.2 3.5 fusion.65
  89.3 82.0 %collective-permute-done.8 = bf16[1024,512]{1,0:T(8,128)(2,1)} collective-permute-done((bf16[1024,512]{1,0:T(8,128)(2,1)}, bf16[1024,512]{1,0:T(8,128)(2,1)}, u32[]{:S(2)}, u32[]{:S(2)}) %collective-permute-start.8) | collective-permute-done | bytes 1048608 | tf_op jit(solution)/shard_map/ppermute | solution.py:259
  171.3 3.4 collective-permute-start.9
  179.4 37.1 %collective-permute-done.5 = bf16[256,2048]{1,0:T(8,128)(2,1)} collective-permute-done((bf16[256,2048]{1,0:T(8,128)(2,1)}, bf16[256,2048]{1,0:T(8,128)(2,1)}, u32[]{:S(2)}, u32[]{:S(2)}) %collective-permute-start.5) | collective-permute-done | bytes 1048608 | tf_op jit(solution)/shard_map/ppermute | solution.py:259
  222.7 17.8 %collective-permute-done.6 = bf16[256,2048]{1,0:T(8,128)(2,1)S(1)} collective-permute-done((bf16[256,2048]{1,0:T(8,128)(2,1)}, bf16[256,2048]{1,0:T(8,128)(2,1)S(1)}, u32[]{:S(2)}, u32[]{:S(2)}) %collective-permute-start.6) | collective-permute-done | bytes 1048608 | tf_op jit(solution)/shard_map/ppermute | solution.py:259
  244.4 12.0 %reduce-scatter.17.cloned.1.call-start = ((), (), s32[]{:S(2)}) async-start(), calls=%async_computation.13 | async-start | bytes 3145728 | tf_op jit(solution)/shard_map/reduce_scatter | solution.py:381
  274.0 4.5 fusion.33
  280.9 8.2 fusion.27
  289.2 10.5 %fusion.72 = f32[2048,512]{1,0:T(8,128)} fusion(bf16[2048,2048]{1,0:T(8,128)(2,1)} %copy-done.32, bf16[2048,512]{1,0:T(8,128)(2,1)} %all-gather.3.cloned.1.call-done), kind=kOutput, calls=%fused_computation.211 | convolution fusion | flops 4294967296 | bytes 14680064 | tf_op jit(solution)/shard_map/dot_general | solution.py:60
  299.7 10.0 add_convert_fusion.1
  315.8 7.7 multiply_convert_fusion.2
  323.6 8.5 fusion.31
  332.1 6.9 multiply_convert_fusion.1
  338.9 10.8 %add_convert_fusion = bf16[2048,2048]{1,0:T(8,128)(2,1)} fusion(f32[2048,2048]{1,0:T(8,128)} %fusion.31, bf16[2048,512]{1,0:T(8,128)(2,1)} %multiply_convert_fusion.1, bf16[2048,512]{1,0:T(8,128)(2,1)S(1)} %copy-done.58), kind=kOutput, calls=%fused_computation | convolution fusion | flops 4303355904 | bytes 29360128 | tf_op jit(solution)/shard_map/dot_general | solution.py:60
  349.7 5.6 fusion.66
  358.3 3.6 convert_add_fusion.1
  364.2 6.6 convert_add_fusion
  375.2 11.1 %convolution_convert_fusion.2 = bf16[2048,512]{1,0:T(8,128)(2,1)} fusion(f32[2048,512]{1,0:T(8,128)} %fusion.72, pred[2048]{0:T(1024)(128)(4,1)S(1)} %get-tuple-element.100, bf16[2048,2048]{1,0:T(8,128)(2,1)} %dynamic-slice_dynamic-update-slice_fusion, f32[2048]{0:T(1024)S(1)} %fusion.47), kind=kOutput, calls=%fused_computation.30 | convolution fusion | flops 4312793088 | bytes 14690304 | tf_op jit(solution)/shard_map/dot_general | solution.py:60
  386.4 26.1 %collective-permute-done.11 = bf16[2,256,2048]{2,1,0:T(8,128)(2,1)S(1)} collective-permute-done((bf16[2,256,2048]{2,1,0:T(8,128)(2,1)}, bf16[2,256,2048]{2,1,0:T(8,128)(2,1)S(1)}, u32[]{:S(2)}, u32[]{:S(2)}) %collective-permute-start.11) | collective-permute-done | bytes 2097184 | tf_op jit(solution)/shard_map/ppermute | solution.py:259
  416.7 40.0 %collective-permute-done.17 = bf16[2,256,2048]{2,1,0:T(8,128)(2,1)} collective-permute-done((bf16[2,256,2048]{2,1,0:T(8,128)(2,1)}, bf16[2,256,2048]{2,1,0:T(8,128)(2,1)}, u32[]{:S(2)}, u32[]{:S(2)}) %collective-permute-start.17) | collective-permute-done | bytes 2097184 | tf_op jit(solution)/shard_map/ppermute | solution.py:259
  461.4 6.0 convolution_convert_fusion.4
  470.4 14.5 %collective-permute-done.18 = bf16[256,2048]{1,0:T(8,128)(2,1)} collective-permute-done((bf16[256,2048]{1,0:T(8,128)(2,1)}, bf16[256,2048]{1,0:T(8,128)(2,1)}, u32[]{:S(2)}, u32[]{:S(2)}) %collective-permute-start.18) | collective-permute-done | bytes 1048608 | tf_op jit(solution)/shard_map/ppermute | solution.py:259
  487.9 3.8 constant_dynamic-update-slice_fusion.8
  494.1 22.9 %collective-permute-done.19 = bf16[256,2048]{1,0:T(8,128)(2,1)S(1)} collective-permute-done((bf16[256,2048]{1,0:T(8,128)(2,1)S(1)}, bf16[256,2048]{1,0:T(8,128)(2,1)S(1)}, u32[]{:S(2)}, u32[]{:S(2)}) %collective-permute-start.19) | collective-permute-done | bytes 1048608 | tf_op jit(solution)/shard_map/ppermute | solution.py:259
  518.5 7.0 convolution_convert_fusion.3
  531.8 4.7 multiply_convert_fusion.5.go_ref
  536.6 16.5 %attend_back.1.g_ref = bf16[1024,1536]{1,0:T(8,128)(2,1)S(1)} custom-call(bf16[1024,512]{1,0:T(8,128)(2,1)S(1)} %copy-done.14, bf16[1024,512]{1,0:T(8,128)(2,1)S(1)} %copy-done.16, bf16[1024,512]{1,0:T(8,128)(2,1)S(1)} %copy-done.18, bf16[1024,512]{1,0:T(8,128)(2,1)S(1)} %multiply_convert_fusion.5.go_ref, s32[1024,1]{1,0:T(8,128)S(1)} %copy.41.first_ref, ...), custom_call_target="tpu_custom_call" | custom-call | flops 5368709120 | bytes 7340032 | tf_op jit(solution)/shard_map/attend_back/pallas_call | solution.py:205
  553.2 7.3 qkv_back.1
  564.3 9.4 convolution_convert_fusion.5
  581.1 22.8 %collective-permute-done.22 = bf16[256,2048]{1,0:T(8,128)(2,1)S(1)} collective-permute-done((bf16[256,2048]{1,0:T(8,128)(2,1)S(1)}, bf16[256,2048]{1,0:T(8,128)(2,1)S(1)}, u32[]{:S(2)}, u32[]{:S(2)}) %collective-permute-start.22) | collective-permute-done | bytes 1048608 | tf_op jit(solution)/shard_map/ppermute | solution.py:259
  607.6 5.9 convolution_convert_fusion.1
  613.8 11.5 %convolution_convert_fusion = bf16[2048,1536]{1,0:T(8,128)(2,1)} fusion(bf16[1024,2048]{1,0:T(8,128)(2,1)} %copy-done.20, bf16[1024,1536]{1,0:T(8,128)(2,1)} %copy-done.19), kind=kOutput, calls=%fused_computation.5 | convolution fusion | flops 6445596672 | bytes 13631488 | tf_op jit(solution)/shard_map/dot_general | solution.py:60
  629.6 3.2 constant_dynamic-update-slice_fusion.10
  636.4 21.3 %collective-permute-done.13 = bf16[256,2048]{1,0:T(8,128)(2,1)S(1)} collective-permute-done((bf16[256,2048]{1,0:T(8,128)(2,1)}, bf16[256,2048]{1,0:T(8,128)(2,1)S(1)}, u32[]{:S(2)}, u32[]{:S(2)}) %collective-permute-start.13) | collective-permute-done | bytes 1048608 | tf_op jit(solution)/shard_map/ppermute | solution.py:259
  657.8 3.4 pad_maximum_fusion.2
  664.0 3.1 convert_dynamic-update-slice_fusion.3
  667.2 3.4 copy-done.38
  671.4 33.5 %collective-permute-done.26 = bf16[1024,512]{1,0:T(8,128)(2,1)} collective-permute-done((bf16[1024,512]{1,0:T(8,128)(2,1)}, bf16[1024,512]{1,0:T(8,128)(2,1)}, u32[]{:S(2)}, u32[]{:S(2)}) %collective-permute-start.26) | collective-permute-done | bytes 1048608 | tf_op jit(solution)/shard_map/ppermute | solution.py:259
  708.6 18.7 %collective-permute-done.25 = bf16[1024,512]{1,0:T(8,128)(2,1)} collective-permute-done((bf16[1024,512]{1,0:T(8,128)(2,1)}, bf16[1024,512]{1,0:T(8,128)(2,1)}, u32[]{:S(2)}, u32[]{:S(2)}) %collective-permute-start.25) | collective-permute-done | bytes 1048608 | tf_op jit(solution)/shard_map/ppermute | solution.py:259
  729.1 3.5 copy.51
  740.0 62.0 %all-reduce.3.cloned.1.call-done = (f32[2,2048]{1,0:T(2,128)}, f32[6,2048]{1,0:T(8,128)}) async-done(((f32[2,2048]{1,0:T(2,128)}, f32[6,2048]{1,0:T(8,128)}), (f32[2,2048]{1,0:T(2,128)}, f32[6,2048]{1,0:T(8,128)})) %all-reduce.3.cloned.1.call-update) | async-done | bytes 65552 | tf_op jit(solution)/shard_map/psum | solution.py:428
  806.2 68.9 %reduce-scatter.9.cloned.1.call-done = bf16[256,512]{1,0:T(8,128)(2,1)} async-done(((bf16[2048,512]{1,0:T(8,128)(2,1)}), bf16[256,512]{1,0:T(8,128)(2,1)}) %reduce-scatter.9.cloned.1.call-update) | async-done | bytes 262160 | tf_op jit(solution)/shard_map/reduce_scatter | solution.py:408
  885.6 110.0 %reduce-scatter.7.cloned.1.call-done = bf16[256,1536]{1,0:T(8,128)(2,1)} async-done(((bf16[2048,1536]{1,0:T(8,128)(2,1)}), bf16[256,1536]{1,0:T(8,128)(2,1)}) %reduce-scatter.7.cloned.1.call-update) | async-done | bytes 786448 | tf_op jit(solution)/shard_map/reduce_scatter | solution.py:408
  (321 shorter events, 168.6 us)
Async XLA Ops:
  7.2 79.5 %copy-start = (bf16[1,512,2048]{2,1,0:T(8,128)(2,1)S(1)}, bf16[1,512,2048]{2,1,0:T(8,128)(2,1)}, u32[]{:S(2)}) copy-start(bf16[1,512,2048]{2,1,0:T(8,128)(2,1)} %param.27) | copy-start | bytes 6291460
  7.2 281.9 %all-gather.3.cloned.1.call-start = ((), (), s32[]{:S(2)}) async-start(), calls=%async_computation.6 | async-start | bytes 3145728 | tf_op jit(solution)/shard_map/all_gather | solution.py:291
  44.6 4.3 collective-permute-start
  52.6 26.7 %collective-permute-start.1 = (bf16[256,2048]{1,0:T(8,128)(2,1)}, bf16[256,2048]{1,0:T(8,128)(2,1)}, u32[]{:S(2)}, u32[]{:S(2)}) collective-permute-start(bf16[256,2048]{1,0:T(8,128)(2,1)} %slice.217), channel_id=1, source_target_pairs={{0,8},{4,12},{8,0},{12,4},{1,9},{5,13},{9,1},{13,5},{2,10},{6,14},... | collective-permute-start | bytes 3145736 | tf_op jit(solution)/shard_map/ppermute | solution.py:259
  55.5 166.9 %collective-permute-start.2 = (f32[8,128]{1,0:T(8,128)S(1)}, f32[8,128]{1,0:T(8,128)S(1)}, u32[]{:S(2)}, u32[]{:S(2)}) collective-permute-start(f32[8,128]{1,0:T(8,128)S(1)} %bitcast.167), channel_id=1, source_target_pairs={{0,1},{1,0},{2,3},{3,2},{4,5},{5,4},{6,7},{7,6},{8,9},{9,8},{10,11... | collective-permute-start | bytes 12296 | tf_op jit(solution)/shard_map/ppermute | solution.py:259
  57.0 201.6 %collective-permute-start.15 = (bf16[1024,2048]{1,0:T(8,128)(2,1)}, bf16[1024,2048]{1,0:T(8,128)(2,1)}, u32[]{:S(2)}, u32[]{:S(2)}) collective-permute-start(bf16[1024,2048]{1,0:T(8,128)(2,1)} %param.15), channel_id=1, source_target_pairs={{0,1},{1,0},{2,3},{3,2},{4,5},{5,4},{6,7},{7,6},{8,9},{9,8},{10,11... | collective-permute-start | bytes 12582920 | tf_op jit(solution)/shard_map/ppermute | solution.py:259
  59.7 111.5 %collective-permute-start.8 = (bf16[1024,512]{1,0:T(8,128)(2,1)}, bf16[1024,512]{1,0:T(8,128)(2,1)}, u32[]{:S(2)}, u32[]{:S(2)}) collective-permute-start(bf16[1024,512]{1,0:T(8,128)(2,1)} %dynamic-slice_bitcast_fusion.1), channel_id=1, source_target_pairs={{0,2},{1,3},{2,0},{3,1},{4,6},{5,7},{6,4},{7,5},{8,10},{9,11},{10,... | collective-permute-start | bytes 3145736 | tf_op jit(solution)/shard_map/ppermute | solution.py:259
  84.9 131.7 %collective-permute-start.5 = (bf16[256,2048]{1,0:T(8,128)(2,1)}, bf16[256,2048]{1,0:T(8,128)(2,1)}, u32[]{:S(2)}, u32[]{:S(2)}) collective-permute-start(bf16[256,2048]{1,0:T(8,128)(2,1)} %get-tuple-element.74), channel_id=1, source_target_pairs={{0,1},{1,0},{2,3},{3,2},{4,5},{5,4},{6,7},{7,6},{8,9},{9,8},{10,11... | collective-permute-start | bytes 3145736 | tf_op jit(solution)/shard_map/ppermute | solution.py:259
  87.7 131.5 %collective-permute-start.3 = (bf16[256,2048]{1,0:T(8,128)(2,1)}, bf16[256,2048]{1,0:T(8,128)(2,1)}, u32[]{:S(2)}, u32[]{:S(2)}) collective-permute-start(bf16[256,2048]{1,0:T(8,128)(2,1)} %get-tuple-element.74), channel_id=1, source_target_pairs={{0,8},{4,12},{8,0},{12,4},{1,9},{5,13},{9,1},{13,5},{2,10},{6,14},... | collective-permute-start | bytes 3145736 | tf_op jit(solution)/shard_map/ppermute | solution.py:259
  171.3 73.1 %collective-permute-start.9 = (bf16[256,2048]{1,0:T(8,128)(2,1)}, bf16[256,2048]{1,0:T(8,128)(2,1)}, u32[]{:S(2)}, u32[]{:S(2)}) collective-permute-start(bf16[256,2048]{1,0:T(8,128)(2,1)} %dynamic-slice_bitcast_fusion), channel_id=1, source_target_pairs={{0,2},{1,3},{2,0},{3,1},{4,6},{5,7},{6,4},{7,5},{8,10},{9,11},{10,... | collective-permute-start | bytes 3145736 | tf_op jit(solution)/shard_map/ppermute | solution.py:259
  174.7 125.0 %all-gather.5.cloned.1.call-start = ((), (), s32[]{:S(2)}) async-start(), calls=%async_computation.7 | async-start | bytes 3145728 | tf_op jit(solution)/shard_map/all_gather | solution.py:291
  216.5 23.9 %collective-permute-start.6 = (bf16[256,2048]{1,0:T(8,128)(2,1)}, bf16[256,2048]{1,0:T(8,128)(2,1)S(1)}, u32[]{:S(2)}, u32[]{:S(2)}) collective-permute-start(bf16[256,2048]{1,0:T(8,128)(2,1)} %collective-permute-done.5), channel_id=1, source_target_pairs={{0,8},{4,12},{8,0},{12,4},{1,9},{5,13},{9,1},{13,5},{2,10},{6,14},... | collective-permute-start | bytes 3145736 | tf_op jit(solution)/shard_map/ppermute | solution.py:259
  222.4 46.6 %collective-permute-start.4 = (bf16[512,2048]{1,0:T(8,128)(2,1)}, bf16[512,2048]{1,0:T(8,128)(2,1)}, u32[]{:S(2)}, u32[]{:S(2)}) collective-permute-start(bf16[512,2048]{1,0:T(8,128)(2,1)} %pad_maximum_fusion), channel_id=1, source_target_pairs={{0,4},{4,0},{8,12},{12,8},{1,5},{5,1},{9,13},{13,9},{2,6},{6,2},{1... | collective-permute-start | bytes 6291464 | tf_op jit(solution)/shard_map/ppermute | solution.py:259
  244.3 27.9 %collective-permute-start.7 = (bf16[512,2048]{1,0:T(8,128)(2,1)}, bf16[512,2048]{1,0:T(8,128)(2,1)}, u32[]{:S(2)}, u32[]{:S(2)}) collective-permute-start(bf16[512,2048]{1,0:T(8,128)(2,1)} %pad_maximum_fusion.1), channel_id=1, source_target_pairs={{0,4},{4,0},{8,12},{12,8},{1,5},{5,1},{9,13},{13,9},{2,6},{6,2},{1... | collective-permute-start | bytes 6291464 | tf_op jit(solution)/shard_map/ppermute | solution.py:259
  244.4 389.1 %reduce-scatter.17.cloned.1.call-start = ((), (), s32[]{:S(2)}) async-start(), calls=%async_computation.13 | async-start | bytes 3145728 | tf_op jit(solution)/shard_map/reduce_scatter | solution.py:381
  314.6 43.7 %collective-permute-start.10 = (bf16[2,2,256,2048]{3,2,0,1:T(8,128)(2,1)}, bf16[2,2,256,2048]{3,2,0,1:T(8,128)(2,1)}, u32[]{:S(2)}, u32[]{:S(2)}) collective-permute-start(bf16[2,2,256,2048]{3,2,0,1:T(8,128)(2,1)} %bitcast.140), channel_id=1, source_target_pairs={{0,4},{4,0},{8,12},{12,8},{1,5},{5,1},{9,13},{13,9},{2,6},{6,2},{1... | collective-permute-start | bytes 12582920 | tf_op jit(solution)/shard_map/ppermute | solution.py:259
  355.7 8.5 collective-permute-start.16
  363.8 48.7 %collective-permute-start.11 = (bf16[2,256,2048]{2,1,0:T(8,128)(2,1)}, bf16[2,256,2048]{2,1,0:T(8,128)(2,1)S(1)}, u32[]{:S(2)}, u32[]{:S(2)}) collective-permute-start(bf16[2,256,2048]{2,1,0:T(8,128)(2,1)} %fusion.19), channel_id=1, source_target_pairs={{0,8},{4,12},{8,0},{12,4},{1,9},{5,13},{9,1},{13,5},{2,10},{6,14},... | collective-permute-start | bytes 6291464 | tf_op jit(solution)/shard_map/ppermute | solution.py:259
  374.8 81.8 %collective-permute-start.17 = (bf16[2,256,2048]{2,1,0:T(8,128)(2,1)}, bf16[2,256,2048]{2,1,0:T(8,128)(2,1)}, u32[]{:S(2)}, u32[]{:S(2)}) collective-permute-start(bf16[2,256,2048]{2,1,0:T(8,128)(2,1)} %fusion.20), channel_id=1, source_target_pairs={{0,8},{4,12},{8,0},{12,4},{1,9},{5,13},{9,1},{13,5},{2,10},{6,14},... | collective-permute-start | bytes 6291464 | tf_op jit(solution)/shard_map/ppermute | solution.py:259
  386.3 247.2 %reduce-scatter.13.cloned.1.call-start = ((), (), s32[]{:S(2)}) async-start(), calls=%async_computation.11 | async-start | bytes 3145728 | tf_op jit(solution)/shard_map/reduce_scatter | solution.py:381
  386.4 70.3 %copy-start.26 = (f32[2,2,256,2048]{3,2,0,1:T(8,128)S(1)}, f32[2,2,256,2048]{3,2,0,1:T(8,128)}, u32[]{:S(2)}) copy-start(f32[2,2,256,2048]{3,2,0,1:T(8,128)} %copy-done.25) | copy-start | bytes 25165828
  412.5 49.0 %slice-start.2 = ((s8[8388608]{0:T(1024)(128)(4,1)}), s8[4194304]{0:T(1024)(128)(4,1)S(1)}, s32[]{:S(2)}) async-start(s8[8388608]{0:T(1024)(128)(4,1)} %bitcast.147), calls=%async_computation.17 | async-start | bytes 8388608
  415.4 43.7 %copy-start.29 = (f32[2,256,2048]{2,1,0:T(8,128)}, f32[2,256,2048]{2,1,0:T(8,128)S(1)}, u32[]{:S(2)}) copy-start(f32[2,256,2048]{2,1,0:T(8,128)S(1)} %fusion.1) | copy-start | bytes 12582916
  416.6 44.8 %slice-start.3 = ((s8[8388608]{0:T(1024)(128)(4,1)}), s8[4194304]{0:T(1024)(128)(4,1)S(1)}, s32[]{:S(2)}) async-start(s8[8388608]{0:T(1024)(128)(4,1)} %bitcast.147), calls=%async_computation.18 | async-start | bytes 8388608
  416.7 44.8 %copy-start.66 = (bf16[2048,512]{1,0:T(8,128)(2,1)S(1)}, bf16[2048,512]{1,0:T(8,128)(2,1)}, u32[]{:S(2)}) copy-start(bf16[2048,512]{1,0:T(8,128)(2,1)} %multiply_convert_fusion.1) | copy-start | bytes 6291460
  416.7 50.9 %collective-permute-start.12 = (bf16[256,2048]{1,0:T(8,128)(2,1)}, bf16[256,2048]{1,0:T(8,128)(2,1)}, u32[]{:S(2)}, u32[]{:S(2)}) collective-permute-start(bf16[256,2048]{1,0:T(8,128)(2,1)} %fusion.35), channel_id=1, source_target_pairs={{0,1},{1,0},{2,3},{3,2},{4,5},{5,4},{6,7},{7,6},{8,9},{9,8},{10,11... | collective-permute-start | bytes 3145736 | tf_op jit(solution)/shard_map/ppermute | solution.py:259
  460.3 24.6 %collective-permute-start.18 = (bf16[256,2048]{1,0:T(8,128)(2,1)}, bf16[256,2048]{1,0:T(8,128)(2,1)}, u32[]{:S(2)}, u32[]{:S(2)}) collective-permute-start(bf16[256,2048]{1,0:T(8,128)(2,1)} %fusion.36), channel_id=1, source_target_pairs={{0,1},{1,0},{2,3},{3,2},{4,5},{5,4},{6,7},{7,6},{8,9},{9,8},{10,11... | collective-permute-start | bytes 3145736 | tf_op jit(solution)/shard_map/ppermute | solution.py:259
  467.5 203.9 %reduce-scatter.15.cloned.1.call-start = ((), (), s32[]{:S(2)}) async-start(), calls=%async_computation.12 | async-start | bytes 3145728 | tf_op jit(solution)/shard_map/reduce_scatter | solution.py:381
  487.4 31.1 %slice-start.6 = ((s8[8388608]{0:T(1024)(128)(4,1)}), s8[4194304]{0:T(1024)(128)(4,1)S(1)}, s32[]{:S(2)}) async-start(s8[8388608]{0:T(1024)(128)(4,1)} %bitcast.155), calls=%async_computation.21 | async-start | bytes 8388608
  487.9 30.6 %slice-start.7 = ((s8[8388608]{0:T(1024)(128)(4,1)}), s8[4194304]{0:T(1024)(128)(4,1)S(1)}, s32[]{:S(2)}) async-start(s8[8388608]{0:T(1024)(128)(4,1)} %bitcast.155), calls=%async_computation.22 | async-start | bytes 8388608
  493.7 24.8 %copy-start.63 = (f32[2048,512]{1,0:T(8,128)S(1)}, f32[2048,512]{1,0:T(8,128)}, u32[]{:S(2)}) copy-start(f32[2048,512]{1,0:T(8,128)} %copy-done.61) | copy-start | bytes 12582916
  493.7 23.3 %collective-permute-start.19 = (bf16[256,2048]{1,0:T(8,128)(2,1)S(1)}, bf16[256,2048]{1,0:T(8,128)(2,1)S(1)}, u32[]{:S(2)}, u32[]{:S(2)}) collective-permute-start(bf16[256,2048]{1,0:T(8,128)(2,1)S(1)} %get-tuple-element.69), channel_id=1, source_target_pairs={{0,8},{4,12},{8,0},{12,4},{1,9},{5,13},{9,1},{13,5},{2,10},{6,14},... | collective-permute-start | bytes 3145736 | tf_op jit(solution)/shard_map/ppermute | solution.py:259
  518.5 8.5 collective-permute-start.20
  525.5 183.1 %reduce-scatter.11.cloned.1.call-start = ((), (), s32[]{:S(2)}) async-start(), calls=%async_computation.10 | async-start | bytes 3145728 | tf_op jit(solution)/shard_map/reduce_scatter | solution.py:381
  563.4 10.4 %collective-permute-start.21 = (bf16[512,2048]{1,0:T(8,128)(2,1)}, bf16[512,2048]{1,0:T(8,128)(2,1)}, u32[]{:S(2)}, u32[]{:S(2)}) collective-permute-start(bf16[512,2048]{1,0:T(8,128)(2,1)} %pad_maximum_fusion.4), channel_id=1, source_target_pairs={{0,4},{4,0},{8,12},{12,8},{1,5},{5,1},{9,13},{13,9},{2,6},{6,2},{1... | collective-permute-start | bytes 6291464 | tf_op jit(solution)/shard_map/ppermute | solution.py:259
  573.7 228.3 %all-reduce.3.cloned.1.call-start = ((), (), s32[]{:S(2)}) async-start(), calls=%async_computation.14 | async-start | bytes 163840 | tf_op jit(solution)/shard_map/psum | solution.py:428
  573.8 30.1 %copy-start.52 = (f32[256]{0:T(256)S(1)}, f32[256]{0:T(256)}, u32[]{:S(2)}) copy-start(f32[256]{0:T(256)} %copy-done.51) | copy-start | bytes 3076
  578.2 29.4 %copy-start.4 = (bf16[1024,512]{1,0:T(8,128)(2,1)S(1)}, bf16[1024,512]{1,0:T(8,128)(2,1)}, u32[]{:S(2)}) copy-start(bf16[1024,512]{1,0:T(8,128)(2,1)} %copy-done.3) | copy-start | bytes 3145732
  578.4 25.6 %collective-permute-start.22 = (bf16[256,2048]{1,0:T(8,128)(2,1)S(1)}, bf16[256,2048]{1,0:T(8,128)(2,1)S(1)}, u32[]{:S(2)}, u32[]{:S(2)}) collective-permute-start(bf16[256,2048]{1,0:T(8,128)(2,1)S(1)} %slice.216), channel_id=1, source_target_pairs={{0,8},{4,12},{8,0},{12,4},{1,9},{5,13},{9,1},{13,5},{2,10},{6,14},... | collective-permute-start | bytes 3145736 | tf_op jit(solution)/shard_map/ppermute | solution.py:259
  607.6 267.5 %reduce-scatter.9.cloned.1.call-start = ((), (), s32[]{:S(2)}) async-start(), calls=%async_computation.9 | async-start | bytes 2359296 | tf_op jit(solution)/shard_map/reduce_scatter | solution.py:408
  613.5 382.1 %reduce-scatter.7.cloned.1.call-start = ((), (), s32[]{:S(2)}) async-start(), calls=%async_computation.8 | async-start | bytes 7077888 | tf_op jit(solution)/shard_map/reduce_scatter | solution.py:408
  632.8 24.9 %collective-permute-start.13 = (bf16[256,2048]{1,0:T(8,128)(2,1)}, bf16[256,2048]{1,0:T(8,128)(2,1)S(1)}, u32[]{:S(2)}, u32[]{:S(2)}) collective-permute-start(bf16[256,2048]{1,0:T(8,128)(2,1)} %get-tuple-element.72), channel_id=1, source_target_pairs={{0,8},{4,12},{8,0},{12,4},{1,9},{5,13},{9,1},{13,5},{2,10},{6,14},... | collective-permute-start | bytes 3145736 | tf_op jit(solution)/shard_map/ppermute | solution.py:259
  633.5 71.4 %collective-permute-start.26 = (bf16[1024,512]{1,0:T(8,128)(2,1)}, bf16[1024,512]{1,0:T(8,128)(2,1)}, u32[]{:S(2)}, u32[]{:S(2)}) collective-permute-start(bf16[1024,512]{1,0:T(8,128)(2,1)} %reduce-scatter.17.cloned.1.call-done), channel_id=1, source_target_pairs={{0,2},{1,3},{2,0},{3,1},{4,6},{5,7},{6,4},{7,5},{8,10},{9,11},{10,... | collective-permute-start | bytes 3145736 | tf_op jit(solution)/shard_map/ppermute | solution.py:259
  633.5 93.7 %collective-permute-start.25 = (bf16[1024,512]{1,0:T(8,128)(2,1)}, bf16[1024,512]{1,0:T(8,128)(2,1)}, u32[]{:S(2)}, u32[]{:S(2)}) collective-permute-start(bf16[1024,512]{1,0:T(8,128)(2,1)} %reduce-scatter.13.cloned.1.call-done), channel_id=1, source_target_pairs={{0,2},{1,3},{2,0},{3,1},{4,6},{5,7},{6,4},{7,5},{8,10},{9,11},{10,... | collective-permute-start | bytes 3145736 | tf_op jit(solution)/shard_map/ppermute | solution.py:259
  661.1 74.2 %collective-permute-start.14 = (bf16[512,2048]{1,0:T(8,128)(2,1)}, bf16[512,2048]{1,0:T(8,128)(2,1)}, u32[]{:S(2)}, u32[]{:S(2)}) collective-permute-start(bf16[512,2048]{1,0:T(8,128)(2,1)} %pad_maximum_fusion.2), channel_id=1, source_target_pairs={{0,4},{4,0},{8,12},{12,8},{1,5},{5,1},{9,13},{13,9},{2,6},{6,2},{1... | collective-permute-start | bytes 6291464 | tf_op jit(solution)/shard_map/ppermute | solution.py:259
  670.6 63.0 %collective-permute-start.23 = (bf16[256,2048]{1,0:T(8,128)(2,1)}, bf16[256,2048]{1,0:T(8,128)(2,1)}, u32[]{:S(2)}, u32[]{:S(2)}) collective-permute-start(bf16[256,2048]{1,0:T(8,128)(2,1)} %get-tuple-element.67), channel_id=1, source_target_pairs={{0,8},{4,12},{8,0},{12,4},{1,9},{5,13},{9,1},{13,5},{2,10},{6,14},... | collective-permute-start | bytes 3145736 | tf_op jit(solution)/shard_map/ppermute | solution.py:259
  735.3 144.6 %collective-permute-start.24 = (bf16[512,2048]{1,0:T(8,128)(2,1)S(1)}, bf16[512,2048]{1,0:T(8,128)(2,1)}, u32[]{:S(2)}, u32[]{:S(2)}) collective-permute-start(bf16[512,2048]{1,0:T(8,128)(2,1)S(1)} %pad_maximum_fusion.5), channel_id=1, source_target_pairs={{0,4},{4,0},{8,12},{12,8},{1,5},{5,1},{9,13},{13,9},{2,6},{6,2},{1... | collective-permute-start | bytes 6291464 | tf_op jit(solution)/shard_map/ppermute | solution.py:259
  879.9 121.3 %copy-start.1 = (bf16[1,512,2048]{2,1,0:T(8,128)(2,1)S(1)}, bf16[1,512,2048]{2,1,0:T(8,128)(2,1)}, u32[]{:S(2)}) copy-start(bf16[1,512,2048]{2,1,0:T(8,128)(2,1)} %param.27) | copy-start | bytes 6291460
  (63 other events, 512.4 us)
Sparse Core Ops, SparseCore 0:
  174.8 33.3 all-gather.2
  244.5 30.5 all-gather.4
  386.4 30.1 reduce-scatter.16
  467.6 29.4 reduce-scatter.12
  525.6 29.2 reduce-scatter.14
  573.8 29.6 reduce-scatter.10
  609.8 192.2 all-reduce.2
  805.6 69.4 reduce-scatter.8
  878.7 116.8 reduce-scatter.6

commit v2 on v1

--- a/solution.py
+++ b/solution.py
@@ -65,91 +65,12 @@
 TN = ((0,), (0,))
 
 
-def qkv_kernel(x_ref, gain_ref, bias_ref, w_ref, cos_ref, sin_ref, n_ref, q_ref, k_ref, v_ref):
-    values = x_ref[...].astype(F32)
-    normed, _ = norm_parts(values)
-    low = (normed * gain_ref[...] + bias_ref[...]).astype(BF16)
-    n_ref[...] = low
-    cosine, sine = cos_ref[...], sin_ref[...]
-    width = w_ref.shape[2]
-    for part, out_ref in enumerate((q_ref, k_ref, v_ref)):
-        projected = dot(low, w_ref[part], NN)
-        if part == 2:
-            out_ref[...] = projected.astype(BF16)
-            continue
-        for at in range(0, width, HEAD_DIM):
-            head = projected[:, at : at + HEAD_DIM]
-            turned = head * cosine + pltpu.roll(head, HEAD_DIM // 2, 1) * sine
-            out_ref[:, at : at + HEAD_DIM] = turned.astype(BF16)
-
-
-def qkv_call(tokens, gain, bias, w3, cosine, sine):
-    rows, width = tokens.shape
-    own = w3.shape[2]
-    wide = pl.BlockSpec((QBLOCK, width), lambda i: (i, 0))
-    row = pl.BlockSpec((1, width), lambda i: (0, 0))
-    table = pl.BlockSpec((QBLOCK, HEAD_DIM), lambda i: (i, 0))
-    out = pl.BlockSpec((QBLOCK, own), lambda i: (i, 0))
-    return pl.pallas_call(
-        qkv_kernel,
-        grid=(rows // QBLOCK,),
-        in_specs=[wide, row, row, pl.BlockSpec(w3.shape, lambda i: (0, 0, 0)), table, table],
-        out_specs=[wide, out, out, out],
-        out_shape=[jax.ShapeDtypeStruct((rows, width), BF16)]
-        + [jax.ShapeDtypeStruct((rows, own), BF16)] * 3,
-        compiler_params=pltpu.CompilerParams(vmem_limit_bytes=40 << 20),
-        cost_estimate=pl.CostEstimate(
-            flops=6 * rows * width * own, bytes_accessed=2 * (2 * rows * width + 3 * width * own + 3 * rows * own), transcendentals=0
-        ),
-        name="qkv",
-    )(tokens, gain.reshape(1, -1), bias.reshape(1, -1), w3, cosine, sine)
-
-
 def masked_scores(query, keys, first, block, length):
     scores = dot(query, keys, NT) * HEAD_DIM**-0.5
     key_at = lax.broadcasted_iota(jnp.int32, (QBLOCK, length), 1)
     row_at = lax.broadcasted_iota(jnp.int32, (QBLOCK, length), 0) + block * QBLOCK
     allowed = (key_at >= first) & (key_at <= row_at)
     return jnp.where(allowed, scores, NEGATIVE)
-
-
-def attend_kernel(q_ref, k_ref, v_ref, first_ref, keep_ref, o_ref, log_ref):
-    for block in range(pl.num_programs(1)):
-
-        @pl.when(pl.program_id(1) == block)
-        def _():
-            length = (block + 1) * QBLOCK
-            scores = masked_scores(q_ref[...], k_ref[:length], first_ref[...], block, length)
-            most = jnp.max(scores, -1, keepdims=True)
-            expo = jnp.exp(scores - most)
-            total = jnp.sum(expo, -1, keepdims=True)
-            weights = (expo * (1.0 / total)).astype(BF16)
-            out = dot(weights, v_ref[:length], NN)
-            o_ref[...] = (out * keep_ref[...]).astype(BF16)
-            log_ref[0] = most + jnp.log(total)
-
-
-def attend_call(queries, keys, values, first, keep):
-    rows, own = queries.shape
-    heads, blocks = own // HEAD_DIM, rows // QBLOCK
-    part = pl.BlockSpec((QBLOCK, HEAD_DIM), lambda h, i: (i, h))
-    whole = pl.BlockSpec((rows, HEAD_DIM), lambda h, i: (0, h))
-    column = pl.BlockSpec((QBLOCK, 1), lambda h, i: (i, 0))
-    return pl.pallas_call(
-        attend_kernel,
-        grid=(heads, blocks),
-        in_specs=[part, whole, whole, column, column],
-        out_specs=[part, pl.BlockSpec((1, QBLOCK, 1), lambda h, i: (h, i, 0))],
-        out_shape=[
-            jax.ShapeDtypeStruct((rows, own), BF16),
-            jax.ShapeDtypeStruct((heads, rows, 1), F32),
-        ],
-        compiler_params=pltpu.CompilerParams(vmem_limit_bytes=40 << 20),
-        cost_estimate=pl.CostEstimate(
-            flops=4 * rows * rows * own, bytes_accessed=8 * rows * own, transcendentals=heads * rows * rows
-        ),
-        name="attend",
-    )(queries, keys, values, first, keep)
 
 
 def attend_back_kernel(
@@ -226,6 +147,233 @@
     )(queries, keys, values, grads, first, logs, cosine, sine)
 
 
+class Copies:
+    def __init__(self, send_sems, recv_sems):
+        self.send_sems, self.recv_sems, self.used = send_sems, recv_sems, 0
+
+    def make(self, source, target, device):
+        slot = self.used
+        self.used += 1
+        return pltpu.make_async_remote_copy(
+            src_ref=source,
+            dst_ref=target,
+            send_sem=self.send_sems.at[slot],
+            recv_sem=self.recv_sems.at[slot],
+            device_id=device,
+            device_id_type=pl.DeviceIdType.MESH,
+        )
+
+    def start(self, source, target, device):
+        copy = self.make(source, target, device)
+        copy.start()
+        return copy
+
+
+def meet(devices):
+    barrier = pltpu.get_barrier_semaphore()
+    for device in devices:
+        pl.semaphore_signal(barrier, inc=1, device_id=device, device_id_type=pl.DeviceIdType.MESH)
+    pl.semaphore_wait(barrier, len(devices))
+
+
+def front_kernel(
+    copies,
+    tokens_ref,
+    gain1_ref,
+    bias1_ref,
+    w_ref,
+    cos_ref,
+    sin_ref,
+    first_ref,
+    keep_ref,
+    w_out_ref,
+    gain2_ref,
+    bias2_ref,
+    up_ref,
+    down_ref,
+    cot_ref,
+    n1_ref,
+    q_ref,
+    k_ref,
+    v_ref,
+    heads_ref,
+    log_ref,
+    middle_ref,
+    n2_ref,
+    up_other_ref,
+    down_other_ref,
+    near_cot_ref,
+    away_ref,
+    got_core_ref,
+    pass_ref,
+    got_y_ref,
+    own_ref,
+    send_sems,
+    recv_sems,
+    local_sem,
+):
+    t, z, x = lax.axis_index("tensor"), lax.axis_index("bucket"), lax.axis_index("dp")
+    rows, own = q_ref.shape
+    share = own_ref.shape[0]
+    heads = own // HEAD_DIM
+    core, y_side = {"tensor": t ^ 1}, {"tensor": t ^ 2}
+    near, far = {"bucket": z ^ 1}, {"bucket": z ^ 2}
+    twins = [{"dp": lax.rem(x + d, copies)} for d in range(1, copies)]
+    meet([core, y_side, near, far] + twins)
+    links = Copies(send_sems, recv_sems)
+
+    def piece(ref, of):
+        size = ref.shape[0] // copies
+        return ref.at[pl.ds(pl.multiple_of(of * size, 16), size)]
+
+    def shard(ref, index):
+        return ref.at[pl.ds(pl.multiple_of(index * share, share), share)]
+
+    up_piece = links.start(piece(up_ref, x), piece(up_other_ref, x), far)
+    parity = lax.rem(t, 2)
+    cots = [
+        links.start(shard(cot_ref, parity + i), shard(near_cot_ref, parity + i), near)
+        for i in (0, 2)
+    ]
+    down_piece = links.start(piece(down_ref, x), piece(down_other_ref, x), far)
+
+    def project(i, carry):
+        at = pl.ds(pl.multiple_of(i * QBLOCK, QBLOCK), QBLOCK)
+        normed, _ = norm_parts(tokens_ref[at, :].astype(F32))
+        low = (normed * gain1_ref[...] + bias1_ref[...]).astype(BF16)
+        n1_ref[at, :] = low
+        cosine, sine = cos_ref[at, :], sin_ref[at, :]
+        for part, out_ref in enumerate((q_ref, k_ref, v_ref)):
+            projected = dot(low, w_ref[part], NN)
+            if part == 2:
+                out_ref[at, :] = projected.astype(BF16)
+                continue
+            for lane in range(0, own, HEAD_DIM):
+                head = projected[:, lane : lane + HEAD_DIM]
+                turned = head * cosine + pltpu.roll(head, HEAD_DIM // 2, 1) * sine
+                out_ref[at, lane : lane + HEAD_DIM] = turned.astype(BF16)
+        return carry
+
+    lax.fori_loop(0, rows // QBLOCK, project, 0)
+
+    for head in range(heads):
+        lanes = slice(head * HEAD_DIM, (head + 1) * HEAD_DIM)
+        for block in range(rows // QBLOCK):
+            length = (block + 1) * QBLOCK
+            at = slice(block * QBLOCK, length)
+            scores = masked_scores(
+                q_ref[at, lanes], k_ref[:length, lanes], first_ref[at], block, length
+            )
+            most = jnp.max(scores, -1, keepdims=True)
+            expo = jnp.exp(scores - most)
+            total = jnp.sum(expo, -1, keepdims=True)
+            weights = (expo * (1.0 / total)).astype(BF16)
+            out = dot(weights, v_ref[:length, lanes], NN)
+            heads_ref[at, lanes] = (out * keep_ref[at]).astype(BF16)
+            log_ref[at, head : head + 1] = most + jnp.log(total)
+
+    def attended(index):
+        at = pl.ds(pl.multiple_of(index * share, share), share)
+        return dot(heads_ref[at, :], w_out_ref[...], NN)
+
+    away_ref[1] = attended(t ^ 3).astype(BF16)
+    to_core1 = links.start(away_ref.at[1], got_core_ref.at[1], core)
+    away_ref[0] = attended(t ^ 1).astype(BF16)
+    to_core0 = links.start(away_ref.at[0], got_core_ref.at[0], core)
+    passed = attended(t ^ 2)
+    to_core1.wait_recv()
+    pass_ref[...] = (passed + got_core_ref[1].astype(F32)).astype(BF16)
+    to_y = links.start(pass_ref, got_y_ref, y_side)
+    middle = attended(t)
+    middle += tokens_ref[pl.ds(pl.multiple_of(t * share, share), share), :].astype(F32)
+    to_core0.wait_recv()
+    middle_ref[...] = middle + got_core_ref[0].astype(F32)
+
+    onward = []
+
+    def pass_on(copy, ref, devices):
+        copy.wait_recv()
+        onward.extend(links.start(ref, ref, device) for device in devices)
+
+    for i, copy in zip((0, 2), cots):
+        pass_on(copy, shard(near_cot_ref, parity + i), [core])
+    pass_on(up_piece, piece(up_other_ref, x), twins)
+    to_y.wait_recv()
+    total = middle_ref[...] + got_y_ref[...].astype(F32)
+    middle_ref[...] = total
+    normed, _ = norm_parts(total)
+    own_ref[...] = (normed * gain2_ref[...] + bias2_ref[...]).astype(BF16)
+    keep_own = pltpu.make_async_copy(own_ref, n2_ref.at[0, t], local_sem)
+    keep_own.start()
+    to_near = links.start(own_ref, n2_ref.at[1, t], near)
+    own_y = links.start(own_ref, n2_ref.at[0, t], y_side)
+    own_core = links.start(own_ref, n2_ref.at[0, t], core)
+    own_y.wait_recv()
+    y_core = links.start(n2_ref.at[0, t ^ 2], n2_ref.at[0, t ^ 2], core)
+    to_near.wait_recv()
+    near_y = links.start(n2_ref.at[1, t], n2_ref.at[1, t], y_side)
+    near_core = links.start(n2_ref.at[1, t], n2_ref.at[1, t], core)
+    near_y.wait_recv()
+    near_y_core = links.start(n2_ref.at[1, t ^ 2], n2_ref.at[1, t ^ 2], core)
+    pass_on(down_piece, piece(down_other_ref, x), twins)
+    keep_own.wait()
+    for copy in (own_core, y_core, near_core, near_y_core, *onward):
+        copy.wait_recv()
+    for copy in (
+        up_piece, *cots, down_piece, to_core1, to_core0, to_y,
+        to_near, own_y, own_core, y_core, near_y, near_core, near_y_core, *onward,
+    ):
+        copy.wait_send()
+
+
+def front_call(tokens, ln1, w3, tables_, first, keep, w_out, ln2, up, down, cotangent):
+    rows, width = tokens.shape
+    own = w3.shape[2]
+    splits, copies = lax.axis_size("tensor"), lax.axis_size("dp")
+    share = rows // splits
+    inside = pl.BlockSpec(memory_space=pltpu.VMEM)
+    outside = pl.BlockSpec(memory_space=pl.ANY)
+    shape = jax.ShapeDtypeStruct
+    total = 14 + 2 * copies
+    return pl.pallas_call(
+        functools.partial(front_kernel, copies),
+        in_specs=[inside] * 11 + [outside] * 3,
+        out_specs=[inside] * 7 + [outside] * 4,
+        out_shape=[
+            shape((rows, width), BF16),
+            shape((rows, own), BF16),
+            shape((rows, own), BF16),
+            shape((rows, own), BF16),
+            shape((rows, own), BF16),
+            shape((rows, own // HEAD_DIM), F32),
+            shape((share, width), F32),
+            shape((2, splits, share, width), BF16),
+            shape(up.shape, BF16),
+            shape(down.shape, BF16),
+            shape(cotangent.shape, BF16),
+        ],
+        scratch_shapes=[
+            pltpu.VMEM((2, share, width), BF16),
+            pltpu.VMEM((2, share, width), BF16),
+            pltpu.VMEM((share, width), BF16),
+            pltpu.VMEM((share, width), BF16),
+            pltpu.VMEM((share, width), BF16),
+            pltpu.SemaphoreType.DMA((total,)),
+            pltpu.SemaphoreType.DMA((total,)),
+            pltpu.SemaphoreType.DMA,
+        ],
+        compiler_params=pltpu.CompilerParams(
+            vmem_limit_bytes=56 << 20, collective_id=0, has_side_effects=True
+        ),
+        cost_estimate=pl.CostEstimate(
+            flops=8 * rows * width * own + 4 * rows * rows * own,
+            bytes_accessed=60 << 20,
+            transcendentals=rows * rows * own // HEAD_DIM,
+        ),
+        name="front",
+    )(tokens, *ln1, w3, *tables_, first, keep, w_out, *ln2, up, down, cotangent)
+
+
 def qkv_back_kernel(g_ref, w_ref, o_ref):
     own = w_ref.shape[2]
     total = dot(g_ref[:, :own], w_ref[0], NT)
@@ -285,32 +433,47 @@
     down_own = w_down.reshape(-1, model_width)
     hidden_width = up_own.shape[1]
 
-    def fetch(weights):
-        rows = weights.shape[0] // copies
-        piece = swap(lax.dynamic_slice_in_dim(weights, x * rows, rows, 0), "bucket", 2)
-        return lax.all_gather(piece, "dp", axis=0, tiled=True)
-
-    up_other, down_other = fetch(up_own), fetch(down_own)
     levels = buckets[:, 0].astype(F32).reshape(-1, HEAD_DIM)
     near_levels = swap(levels, "bucket", 1)
-    near_cotangent = swap(cotangent, "bucket", 1)
 
     def shard(values, bit):
         return lax.dynamic_slice_in_dim(values, (t ^ bit) * share, share, 0)
 
     ORDER = (0, 2, 1, 3)
 
-    def arranged(values):
-        return jnp.concatenate([shard(values, bit) for bit in ORDER], 0)
-
-    inputs = tokens.astype(F32)
     positions, first = layout(lengths[0], tok_rows)
     first = first[:, None]
     keep = (t < head_quarters).astype(F32)[:, None]
     cosine, sine = tables(positions)
     w3 = jnp.transpose(w_qkv, (1, 0, 2))
-    normed1, queries, keys, values = qkv_call(tokens, ln1_gain, ln1_bias, w3, cosine, sine)
-    heads_low, logs = attend_call(queries, keys, values, first, keep)
+    (
+        normed1,
+        queries,
+        keys,
+        values,
+        heads_low,
+        logs,
+        middle,
+        n2,
+        up_other,
+        down_other,
+        near_cotangent,
+    ) = front_call(
+        tokens,
+        (ln1_gain.reshape(1, -1), ln1_bias.reshape(1, -1)),
+        w3,
+        (cosine, sine),
+        first,
+        keep,
+        w_out,
+        (ln2_gain.reshape(1, -1), ln2_bias.reshape(1, -1)),
+        up_own,
+        down_own,
+        cotangent,
+    )
+    logs = logs.T[:, :, None]
+    normed2 = lax.dynamic_index_in_dim(n2[0], t, 0, False)
+    n2 = n2.reshape(-1, model_width)
 
     def gather_sum(away, kept):
         both = kept + swap(away.astype(BF16), "tensor", 1).astype(F32)
@@ -328,27 +491,17 @@
             whole = lax.dynamic_update_slice_in_dim(whole, part, (t ^ bit) * share, 0)
         return whole
 
-    heads_kept = jnp.concatenate([shard(heads_low, 0), shard(heads_low, 2)], 0)
-    heads_away = jnp.concatenate([shard(heads_low, 1), shard(heads_low, 3)], 0)
-    attention = gather_sum(dot(heads_away, w_out, NN).astype(BF16), dot(heads_kept, w_out, NN))
     inputs_own = shard(tokens, 0).astype(F32)
-    middle = inputs_own + attention
     hat2, inverse2 = norm_parts(middle)
-    normed2 = (hat2 * ln2_gain + ln2_bias).astype(BF16)
-
-    near = swap(normed2, "bucket", 1)
-    n2 = jnp.concatenate([spread(normed2), spread(near)], 0)
 
     def gate_of(rows, tok_levels):
         probs = softmax(dot(rows, w_router, NN))
         onehot = (tok_levels[:, None] == jnp.arange(owners, dtype=F32)[None, :]).astype(F32)
         return jnp.sum(probs * onehot, -1), probs, onehot
 
-    level_all = jnp.concatenate(
-        [arranged(levels.reshape(-1)), arranged(near_levels.reshape(-1))], 0
-    )
+    level_all = jnp.concatenate([levels.reshape(-1), near_levels.reshape(-1)], 0)
     gate_all, _, _ = gate_of(n2, level_all)
-    grad_all = jnp.concatenate([arranged(cotangent), arranged(near_cotangent)], 0)
+    grad_all = jnp.concatenate([cotangent, near_cotangent], 0)
     grad_branch = (gate_all[:, None] * grad_all.astype(F32)).astype(BF16)
     kept_own = (level_all >= z.astype(F32))[:, None]
     kept_other = (level_all >= (z ^ 2).astype(F32))[:, None]
@@ -359,12 +512,13 @@
 
     act_own, hid_own = forward(up_own, kept_own)
     act_other, hid_other = forward(up_other, kept_other)
-    parts = 2 * splits
 
     def scatter_sum(total):
-        blocks = total.astype(BF16).reshape(2, 2, 2, share, model_width)
-        kept, away = blocks[:, 0], blocks[:, 1]
-        both = kept.astype(F32) + swap(away, "tensor", 1).astype(F32)
+        blocks = total.astype(BF16).reshape(2, splits, share, model_width)
+        pick = lambda bits: jnp.stack(
+            [lax.dynamic_index_in_dim(blocks, t ^ bit, 1, False) for bit in bits], 1
+        )
+        both = pick((0, 2)).astype(F32) + swap(pick((1, 3)), "tensor", 1).astype(F32)
         one = both[:, 0] + swap(both[:, 1].astype(BF16), "tensor", 2).astype(F32)
         return one[0] + swap(one[1].astype(BF16), "bucket", 1).astype(F32)
 

time: 1020 us -> 810 us (0.79)
  waiting for transfers between devices: 595 us -> 293 us
  Pallas kernels: 48.8 us -> 197 us
  starting transfers between devices: 35.7 us -> 12.8 us
  local copies, waits for them, and re-layouts: 104 us -> 88.7 us
  other arithmetic: 76.3 us -> 65.7 us
    pallas_call x2 -> x1, Pallas kernels: 24.9 us -> 173 us  [front_call(): pl.pallas_call(functools.partial(front_kernel, copies), in_specs=[inside]...]
    reduce_scatter x2, waiting for transfers between devices: 179 us -> 31.3 us  [reduce_all(): lax.psum_scatter(grad.astype(BF16), ('dp', 'bucket'), scatter_dimension=0...]
    ppermute x27 -> x17, waiting for transfers between devices: 354 us -> 208 us  [swap(): return lax.ppermute(values, axis, pairs)]
    unnamed x174 -> x128, local copies, waits for them, and re-layouts: 55.6 us -> 42.8 us
    reduce_scatter x4, starting transfers between devices: 12.5 us -> 0.75 us  [reduce_dp(): lax.psum_scatter(grad.astype(BF16), 'dp', scatter_dimension=dim, tiled=True)]
    ppermute x27 -> x17, starting transfers between devices: 22.9 us -> 11.8 us  [swap(): return lax.ppermute(values, axis, pairs)]
    dot_general x21 -> x19, matrix products: 133 us -> 131 us  [dot(): lax.dot_general(left, right, (dims, ((), ())), preferred_element_type=F32)]
  transfers between devices with their start and end apart: 36 -> 24, of which waited for: 16 -> 10; matrix products, arithmetic and copies ran while one was open for 26% -> 27% of each run, Pallas kernels for 2% -> 24%
where the time goes in v2:
time: 810 us; the launch traced here: 805 us
  waiting for transfers between devices  293 us (36%)
  Pallas kernels  197 us (24%)
  matrix products  131 us (16%)
  local copies, waits for them, and re-layouts  88.7 us (11%)
  other arithmetic  65.7 us (8%)
  between operations  16.6 us (2%)
  starting transfers between devices  12.8 us (2%)
    ppermute x17, waiting for transfers between devices, swap(): return lax.ppermute(values, axis, pairs)  208 us
    pallas_call x1, Pallas kernels, front_call(): pl.pallas_call(functools.partial(front_kernel, copies), in_specs=[inside]...  173 us
    dot_general x19, matrix products, dot(): lax.dot_general(left, right, (dims, ((), ())), preferred_element_type=F32)  131 us
    psum x1, waiting for transfers between devices, reduce_small(): total = lax.psum(stacked, ('dp', 'tensor', 'bucket'))  53.4 us
    unnamed x128, local copies, waits for them, and re-layouts  42.8 us
    reduce_scatter x2, waiting for transfers between devices, reduce_all(): lax.psum_scatter(grad.astype(BF16), ('dp', 'bucket'), scatter_dimension=0...  31.3 us
    pallas_call x1, Pallas kernels, attend_back_call(): pl.pallas_call(attend_back_kernel, grid=(heads, blocks), in_specs=[part,...  16.3 us
  transfers between devices with their start and end apart: 24, of which 10 were waited for; matrix products, arithmetic and copies ran while one was open for 27% of the time, Pallas kernels for 24%

profile of v2, /device:TPU:0, one launch (start us, length us, event | category | flops | bytes accessed | tf_op | source)
XLA Modules:
  0.0 804.9 jit_solution(2863230475466030418)
XLA Ops:
  8.8 3.0 collective-permute-start
  19.5 173.5 %front.1 = (bf16[1024,2048]{1,0:T(8,128)(2,1)}, bf16[1024,512]{1,0:T(8,128)(2,1)}, bf16[1024,512]{1,0:T(8,128)(2,1)}, bf16[1024,512]{1,0:T(8,128)(2,1)}, bf16[10...) custom-call(bf16[1024,2048]{1,0:T(8,128)(2,1)} %tokens_ref.1, ...), custom_call_target="tpu_custom_call" | custom-call | flops 10737418240 | bytes 62914560 | tf_op jit(solution)/shard_map/front/pallas_call | solution.py:338
  193.0 9.8 %fusion.51 = f32[2048,512]{1,0:T(8,128)} fusion(bf16[2048,2048]{1,0:T(8,128)(2,1)} %bitcast.146, bf16[2048,1,512]{2,0,1:T(8,128)(2,1)S(1)} %copy-done.42), kind=kOutput, calls=%fused_computation.165 | convolution fusion | flops 4294967296 | bytes 14680064 | tf_op jit(solution)/shard_map/dot_general | solution.py:60
  205.1 6.0 fusion.61
  211.3 13.3 %fusion.47 = f32[2048,2048]{1,0:T(8,128)} fusion(bf16[1,512,2048]{2,1,0:T(8,128)(2,1)} %param.27, f32[2048,512]{1,0:T(8,128)} %fusion.51, pred[2048]{0:T(1024)(128)(4,1)S(1)} %get-tuple-element.106), kind=kOutput, calls=%fused_computation.161 | convolution fusion | flops 4299161600 | bytes 23070720 | tf_op jit(solution)/shard_map/dot_general | solution.py:60
  224.6 7.5 multiply_convert_fusion.2
  232.2 7.3 multiply_convert_fusion.1
  239.4 8.8 %add_convert_fusion.1 = bf16[2048,2048]{1,0:T(8,128)(2,1)S(1)} fusion(f32[2048,2048]{1,0:T(8,128)} %fusion.47, bf16[512,2048]{1,0:T(8,128)(2,1)} %get-tuple-element.25, f32[2048,512]{1,0:T(8,128)S(1)} %copy-done.45, pred[2048]{0:T(1024)(128)(4,1)S(1)} %get-tuple-element.105), kind=kOutput, calls=%fused_computation.2 | convolution fusion | flops 4307550208 | bytes 31459328 | tf_op jit(solution)/shard_map/dot_general | solution.py:60
  248.3 2.9 dynamic-slice_bitcast_fusion.7
  254.9 8.3 %fusion.49 = f32[2048,2048]{1,0:T(8,128)} fusion(bf16[2048,512]{1,0:T(8,128)(2,1)S(1)} %copy-done.49, bf16[2048,1,512]{2,0,1:T(8,128)(2,1)S(1)} %copy-done.43), kind=kOutput, calls=%fused_computation.163 | convolution fusion | flops 4294967296 | bytes 20971520 | tf_op jit(solution)/shard_map/dot_general | solution.py:60
  263.2 11.3 %add_convert_fusion = bf16[2048,2048]{1,0:T(8,128)(2,1)} fusion(f32[2048,2048]{1,0:T(8,128)} %fusion.49, bf16[2048,512]{1,0:T(8,128)(2,1)S(1)} %copy-done.51, bf16[2048,512]{1,0:T(8,128)(2,1)} %get-tuple-element.24), kind=kOutput, calls=%fused_computation | convolution fusion | flops 4303355904 | bytes 29360128 | tf_op jit(solution)/shard_map/dot_general | solution.py:60
  274.5 6.7 dynamic-slice_bitcast_fusion.3
  283.6 4.9 slice.83
  290.9 3.6 convert_add_fusion.1
  299.9 3.3 convert_add_fusion
  304.8 3.6 copy-done.13
  309.5 6.8 convolution_convert_fusion.2
  316.6 28.4 %collective-permute-done.2 = bf16[2,256,2048]{2,1,0:T(8,128)(2,1)} collective-permute-done((bf16[2,256,2048]{2,1,0:T(8,128)(2,1)}, bf16[2,256,2048]{2,1,0:T(8,128)(2,1)}, u32[]{:S(2)}, u32[]{:S(2)}) %collective-permute-start.2) | collective-permute-done | bytes 2097184 | tf_op jit(solution)/shard_map/ppermute | solution.py:407
  345.0 3.6 fusion.1
  351.7 37.6 %collective-permute-done.7 = bf16[2,256,2048]{2,1,0:T(8,128)(2,1)} collective-permute-done((bf16[2,256,2048]{2,1,0:T(8,128)(2,1)}, bf16[2,256,2048]{2,1,0:T(8,128)(2,1)}, u32[]{:S(2)}, u32[]{:S(2)}) %collective-permute-start.7) | collective-permute-done | bytes 2097184 | tf_op jit(solution)/shard_map/ppermute | solution.py:407
  394.9 5.8 convolution_convert_fusion.4
  400.8 2.8 fusion.18
  403.6 16.2 %collective-permute-done.8 = bf16[256,2048]{1,0:T(8,128)(2,1)} collective-permute-done((bf16[256,2048]{1,0:T(8,128)(2,1)}, bf16[256,2048]{1,0:T(8,128)(2,1)}, u32[]{:S(2)}, u32[]{:S(2)}) %collective-permute-start.8) | collective-permute-done | bytes 1048608 | tf_op jit(solution)/shard_map/ppermute | solution.py:407
  422.8 3.5 constant_dynamic-update-slice_fusion.1
  428.8 8.5 %copy.60.log_ref = f32[4,1024,1]{2,1,0:T(8,128)S(1)} copy(f32[4,1024,1]{0,1,2:T(8,128)} %bitcast.158) | data formatting | bytes 32768 | tf_op jit(solution)/shard_map/broadcast_in_dim | solution.py:474
  437.4 14.7 %collective-permute-done.9 = bf16[256,2048]{1,0:T(8,128)(2,1)} collective-permute-done((bf16[256,2048]{1,0:T(8,128)(2,1)S(1)}, bf16[256,2048]{1,0:T(8,128)(2,1)}, u32[]{:S(2)}, u32[]{:S(2)}) %collective-permute-start.9) | collective-permute-done | bytes 1048608 | tf_op jit(solution)/shard_map/ppermute | solution.py:407
  452.1 2.7 pad_maximum_fusion.3
  454.9 10.1 %convolution_convert_fusion.3 = bf16[2048,512]{1,0:T(8,128)(2,1)} fusion(f32[2048,512]{1,0:T(8,128)} %fusion.51, pred[2048]{0:T(1024)(128)(4,1)S(1)} %get-tuple-element.106, bf16[1024,2048]{1,0:T(8,128)(2,1)} %get-tuple-element.26, bf16[1024,2048]{1,0:T(8,128)(2,1)S(1)} %copy-done.36, f32[2048]{0:T(1024)S(1)} %fusion.34), kind=kOutput, calls=%fused_computation.25 | convolution fusion | flops 4325376000 | bytes 14690304 | tf_op jit(solution)/shard_map/dot_general | solution.py:60
  472.7 4.8 multiply_convert_fusion.5.go_ref
  477.5 16.3 %attend_back.1.g_ref = bf16[1024,1536]{1,0:T(8,128)(2,1)S(1)} custom-call(bf16[1024,512]{1,0:T(8,128)(2,1)S(1)} %copy-done.6, bf16[1024,512]{1,0:T(8,128)(2,1)S(1)} %copy-done.7, bf16[1024,512]{1,0:T(8,128)(2,1)S(1)} %copy-done.8, bf16[1024,512]{1,0:T(8,128)(2,1)S(1)} %multiply_convert_fusion.5.go_ref, s32[1024,1]{1,0:T(8,128)S(1)} %copy-done.3, ...), custom_call_target="tpu_custom_call" | custom-call | flops 5368709120 | bytes 7340032 | tf_op jit(solution)/shard_map/attend_back/pallas_call | solution.py:126
  493.9 7.3 qkv_back.1
  505.2 5.7 convolution_convert_fusion.5
  522.3 20.2 %collective-permute-done.12 = bf16[256,2048]{1,0:T(8,128)(2,1)S(1)} collective-permute-done((bf16[256,2048]{1,0:T(8,128)(2,1)S(1)}, bf16[256,2048]{1,0:T(8,128)(2,1)S(1)}, u32[]{:S(2)}, u32[]{:S(2)}) %collective-permute-start.12) | collective-permute-done | bytes 1048608 | tf_op jit(solution)/shard_map/ppermute | solution.py:407
  542.5 3.4 fusion.14
  546.6 6.4 convolution_convert_fusion.1
  553.3 11.0 %convolution_convert_fusion = bf16[2048,1536]{1,0:T(8,128)(2,1)} fusion(bf16[1024,2048]{1,0:T(8,128)(2,1)} %get-tuple-element.31, bf16[1024,1536]{1,0:T(8,128)(2,1)S(1)} %copy-done.5), kind=kOutput, calls=%fused_computation.5 | convolution fusion | flops 6445596672 | bytes 13631488 | tf_op jit(solution)/shard_map/dot_general | solution.py:60
  564.3 2.7 broadcast.103.clone
  572.1 4.4 collective-permute-start.16
  576.5 19.6 %collective-permute-done.4 = bf16[256,2048]{1,0:T(8,128)(2,1)S(1)} collective-permute-done((bf16[256,2048]{1,0:T(8,128)(2,1)}, bf16[256,2048]{1,0:T(8,128)(2,1)S(1)}, u32[]{:S(2)}, u32[]{:S(2)}) %collective-permute-start.4) | collective-permute-done | bytes 1048608 | tf_op jit(solution)/shard_map/ppermute | solution.py:407
  596.1 3.2 pad_maximum_fusion.2
  604.6 3.4 copy-done.22
  608.9 43.6 %collective-permute-done.16 = bf16[1024,512]{1,0:T(8,128)(2,1)} collective-permute-done((bf16[1024,512]{1,0:T(8,128)(2,1)}, bf16[1024,512]{1,0:T(8,128)(2,1)}, u32[]{:S(2)}, u32[]{:S(2)}) %collective-permute-start.16) | collective-permute-done | bytes 1048608 | tf_op jit(solution)/shard_map/ppermute | solution.py:407
  656.2 27.5 %collective-permute-done.15 = bf16[1024,512]{1,0:T(8,128)(2,1)} collective-permute-done((bf16[1024,512]{1,0:T(8,128)(2,1)}, bf16[1024,512]{1,0:T(8,128)(2,1)}, u32[]{:S(2)}, u32[]{:S(2)}) %collective-permute-start.15) | collective-permute-done | bytes 1048608 | tf_op jit(solution)/shard_map/ppermute | solution.py:407
  685.6 3.5 copy.64
  690.1 2.7 pad_maximum_fusion.5
  697.4 53.4 %all-reduce.3.cloned.1.call-done = (f32[2,2048]{1,0:T(2,128)}, f32[6,2048]{1,0:T(8,128)}) async-done(((f32[2,2048]{1,0:T(2,128)}, f32[6,2048]{1,0:T(8,128)}), (f32[2,2048]{1,0:T(2,128)}, f32[6,2048]{1,0:T(8,128)})) %all-reduce.3.cloned.1.call-update) | async-done | bytes 65552 | tf_op jit(solution)/shard_map/psum | solution.py:582
  757.0 2.8 convert_dynamic-update-slice_fusion.2
  763.0 31.3 %reduce-scatter.7.cloned.1.call-done = bf16[256,1536]{1,0:T(8,128)(2,1)} async-done(((bf16[2048,1536]{1,0:T(8,128)(2,1)}), bf16[256,1536]{1,0:T(8,128)(2,1)}) %reduce-scatter.7.cloned.1.call-update) | async-done | bytes 786448 | tf_op jit(solution)/shard_map/reduce_scatter | solution.py:562
  (238 shorter events, 100.3 us)
Async XLA Ops:
  8.0 194.7 %copy-start = (bf16[2048,4]{0,1:T(4,128)(2,1)S(1)}, bf16[2048,4]{0,1:T(4,128)(2,1)}, u32[]{:S(2)}) copy-start(bf16[2048,4]{0,1:T(4,128)(2,1)} %param.25) | copy-start | bytes 49156
  8.0 564.0 %reduce-scatter.17.cloned.1.call-start = ((), (), s32[]{:S(2)}) async-start(), calls=%async_computation.11 | async-start | bytes 3145728 | tf_op jit(solution)/shard_map/reduce_scatter | solution.py:535
  8.8 202.4 %collective-permute-start = (f32[8,128]{1,0:T(8,128)S(1)}, f32[8,128]{1,0:T(8,128)S(1)}, u32[]{:S(2)}, u32[]{:S(2)}) collective-permute-start(f32[8,128]{1,0:T(8,128)S(1)} %bitcast.159), channel_id=1, source_target_pairs={{0,1},{1,0},{2,3},{3,2},{4,5},{5,4},{6,7},{7,6},{8,9},{9,8},{10,11... | collective-permute-start | bytes 12296 | tf_op jit(solution)/shard_map/ppermute | solution.py:407
  14.2 178.8 %copy-start.39 = (f32[1024]{0:T(1024)}, f32[1024]{0:T(1024)S(1)}, u32[]{:S(2)}) copy-start(f32[1024]{0:T(1024)S(1)} %compare_convert_fusion) | copy-start | bytes 12292
  19.5 173.5 %copy-start.42 = (bf16[2048,1,512]{2,0,1:T(8,128)(2,1)S(1)}, bf16[2048,1,512]{2,0,1:T(8,128)(2,1)}, u32[]{:S(2)}) copy-start(bf16[2048,1,512]{2,0,1:T(8,128)(2,1)} %param.26) | copy-start | bytes 6291460
  193.0 9.8 %copy-start.11 = (bf16[2,4,256,2048]{3,2,1,0:T(8,128)(2,1)S(1)}, bf16[2,4,256,2048]{3,2,1,0:T(8,128)(2,1)}, u32[]{:S(2)}) copy-start(bf16[2,4,256,2048]{3,2,1,0:T(8,128)(2,1)} %get-tuple-element.23) | copy-start | bytes 25165828
  211.2 13.4 %copy-start.34 = (bf16[1024,2048]{1,0:T(8,128)(2,1)S(1)}, bf16[1024,2048]{1,0:T(8,128)(2,1)}, u32[]{:S(2)}) copy-start(bf16[1024,2048]{1,0:T(8,128)(2,1)} %cot_ref.1) | copy-start | bytes 12582916
  211.2 13.4 %copy-start.41 = (bf16[1,512,2048]{2,1,0:T(8,128)(2,1)S(1)}, bf16[1,512,2048]{2,1,0:T(8,128)(2,1)}, u32[]{:S(2)}) copy-start(bf16[1,512,2048]{2,1,0:T(8,128)(2,1)} %param.27) | copy-start | bytes 6291460
  211.3 13.4 %copy-start.47 = (f32[2048,512]{1,0:T(8,128)S(1)}, f32[2048,512]{1,0:T(8,128)}, u32[]{:S(2)}) copy-start(f32[2048,512]{1,0:T(8,128)} %fusion.51) | copy-start | bytes 12582916
  253.6 9.6 %copy-start.51 = (bf16[2048,512]{1,0:T(8,128)(2,1)S(1)}, bf16[2048,512]{1,0:T(8,128)(2,1)}, u32[]{:S(2)}) copy-start(bf16[2048,512]{1,0:T(8,128)(2,1)} %multiply_convert_fusion.1) | copy-start | bytes 6291460
  253.6 37.3 %collective-permute-start.1 = (bf16[2,2,256,2048]{3,2,0,1:T(8,128)(2,1)}, bf16[2,2,256,2048]{3,2,0,1:T(8,128)(2,1)}, u32[]{:S(2)}, u32[]{:S(2)}) collective-permute-start(bf16[2,2,256,2048]{3,2,0,1:T(8,128)(2,1)} %pad_maximum_fusion), channel_id=1, source_target_pairs={{0,4},{4,0},{8,12},{12,8},{1,5},{5,1},{9,13},{13,9},{2,6},{6,2},{1... | collective-permute-start | bytes 12582920 | tf_op jit(solution)/shard_map/ppermute | solution.py:407
  283.6 12.6 %collective-permute-start.6 = (bf16[2,2,256,2048]{3,2,0,1:T(8,128)(2,1)}, bf16[2,2,256,2048]{3,2,0,1:T(8,128)(2,1)}, u32[]{:S(2)}, u32[]{:S(2)}) collective-permute-start(bf16[2,2,256,2048]{3,2,0,1:T(8,128)(2,1)} %pad_maximum_fusion.1), channel_id=1, source_target_pairs={{0,4},{4,0},{8,12},{12,8},{1,5},{5,1},{9,13},{13,9},{2,6},{6,2},{1... | collective-permute-start | bytes 12582920 | tf_op jit(solution)/shard_map/ppermute | solution.py:407
  294.5 8.6 %copy-start.12 = (f32[2,2,256,2048]{3,2,0,1:T(8,128)}, f32[2,2,256,2048]{3,2,0,1:T(8,128)S(1)}, u32[]{:S(2)}) copy-start(f32[2,2,256,2048]{3,2,0,1:T(8,128)S(1)} %convert_add_fusion.1) | copy-start | bytes 25165828
  296.2 48.8 %collective-permute-start.2 = (bf16[2,256,2048]{2,1,0:T(8,128)(2,1)}, bf16[2,256,2048]{2,1,0:T(8,128)(2,1)}, u32[]{:S(2)}, u32[]{:S(2)}) collective-permute-start(bf16[2,256,2048]{2,1,0:T(8,128)(2,1)} %fusion.19), channel_id=1, source_target_pairs={{0,8},{4,12},{8,0},{12,4},{1,9},{5,13},{9,1},{13,5},{2,10},{6,14},... | collective-permute-start | bytes 6291464 | tf_op jit(solution)/shard_map/ppermute | solution.py:407
  299.9 8.6 %copy-start.54 = (bf16[1024,2048]{1,0:T(8,128)(2,1)S(1)}, bf16[1024,2048]{1,0:T(8,128)(2,1)}, u32[]{:S(2)}) copy-start(bf16[1024,2048]{1,0:T(8,128)(2,1)} %get-tuple-element.26) | copy-start | bytes 12582916
  308.4 80.9 %collective-permute-start.7 = (bf16[2,256,2048]{2,1,0:T(8,128)(2,1)}, bf16[2,256,2048]{2,1,0:T(8,128)(2,1)}, u32[]{:S(2)}, u32[]{:S(2)}) collective-permute-start(bf16[2,256,2048]{2,1,0:T(8,128)(2,1)} %fusion.20), channel_id=1, source_target_pairs={{0,8},{4,12},{8,0},{12,4},{1,9},{5,13},{9,1},{13,5},{2,10},{6,14},... | collective-permute-start | bytes 6291464 | tf_op jit(solution)/shard_map/ppermute | solution.py:407
  316.3 260.1 %reduce-scatter.13.cloned.1.call-start = ((), (), s32[]{:S(2)}) async-start(), calls=%async_computation.9 | async-start | bytes 3145728 | tf_op jit(solution)/shard_map/reduce_scatter | solution.py:535
  316.6 72.8 %copy-start.14 = (f32[2,2,256,2048]{3,2,0,1:T(8,128)S(1)}, f32[2,2,256,2048]{3,2,0,1:T(8,128)}, u32[]{:S(2)}) copy-start(f32[2,2,256,2048]{3,2,0,1:T(8,128)} %copy-done.13) | copy-start | bytes 25165828
  345.0 49.9 %slice-start.2 = ((s8[8388608]{0:T(1024)(128)(4,1)}), s8[4194304]{0:T(1024)(128)(4,1)S(1)}, s32[]{:S(2)}) async-start(s8[8388608]{0:T(1024)(128)(4,1)} %bitcast.149), calls=%async_computation.15 | async-start | bytes 8388608
  351.7 43.2 %slice-start.3 = ((s8[8388608]{0:T(1024)(128)(4,1)}), s8[4194304]{0:T(1024)(128)(4,1)S(1)}, s32[]{:S(2)}) async-start(s8[8388608]{0:T(1024)(128)(4,1)} %bitcast.149), calls=%async_computation.16 | async-start | bytes 8388608
  351.7 43.2 %copy-start.52 = (bf16[2048,512]{1,0:T(8,128)(2,1)S(1)}, bf16[2048,512]{1,0:T(8,128)(2,1)}, u32[]{:S(2)}) copy-start(bf16[2048,512]{1,0:T(8,128)(2,1)} %multiply_convert_fusion.1) | copy-start | bytes 6291460
  351.7 49.1 %collective-permute-start.3 = (bf16[256,2048]{1,0:T(8,128)(2,1)}, bf16[256,2048]{1,0:T(8,128)(2,1)S(1)}, u32[]{:S(2)}, u32[]{:S(2)}) collective-permute-start(bf16[256,2048]{1,0:T(8,128)(2,1)} %fusion.25), channel_id=1, source_target_pairs={{0,1},{1,0},{2,3},{3,2},{4,5},{5,4},{6,7},{7,6},{8,9},{9,8},{10,11... | collective-permute-start | bytes 3145736 | tf_op jit(solution)/shard_map/ppermute | solution.py:407
  394.9 24.9 %collective-permute-start.8 = (bf16[256,2048]{1,0:T(8,128)(2,1)}, bf16[256,2048]{1,0:T(8,128)(2,1)}, u32[]{:S(2)}, u32[]{:S(2)}) collective-permute-start(bf16[256,2048]{1,0:T(8,128)(2,1)} %fusion.26), channel_id=1, source_target_pairs={{0,1},{1,0},{2,3},{3,2},{4,5},{5,4},{6,7},{7,6},{8,9},{9,8},{10,11... | collective-permute-start | bytes 3145736 | tf_op jit(solution)/shard_map/ppermute | solution.py:407
  400.7 19.1 %copy-start.38 = (f32[2048]{0:T(1024)S(1)}, f32[2048]{0:T(1024)}, u32[]{:S(2)}) copy-start(f32[2048]{0:T(1024)} %param.23) | copy-start | bytes 24580
  400.8 208.1 %reduce-scatter.15.cloned.1.call-start = ((), (), s32[]{:S(2)}) async-start(), calls=%async_computation.10 | async-start | bytes 3145728 | tf_op jit(solution)/shard_map/reduce_scatter | solution.py:535
  400.8 19.0 %copy-start.20 = (f32[2,256,2048]{2,1,0:T(8,128)S(1)}, f32[2,256,2048]{2,1,0:T(8,128)}, u32[]{:S(2)}) copy-start(f32[2,256,2048]{2,1,0:T(8,128)} %copy-done.19) | copy-start | bytes 12582916
  400.8 21.5 %copy-start.29 = (bf16[256,2048]{1,0:T(8,128)(2,1)}, bf16[256,2048]{1,0:T(8,128)(2,1)S(1)}, u32[]{:S(2)}) copy-start(bf16[256,2048]{1,0:T(8,128)(2,1)S(1)} %collective-permute-done.3) | copy-start | bytes 3145732
  428.4 23.8 %collective-permute-start.9 = (bf16[256,2048]{1,0:T(8,128)(2,1)S(1)}, bf16[256,2048]{1,0:T(8,128)(2,1)}, u32[]{:S(2)}, u32[]{:S(2)}) collective-permute-start(bf16[256,2048]{1,0:T(8,128)(2,1)S(1)} %get-tuple-element.79), channel_id=1, source_target_pairs={{0,8},{4,12},{8,0},{12,4},{1,9},{5,13},{9,1},{13,5},{2,10},{6,14},... | collective-permute-start | bytes 3145736 | tf_op jit(solution)/shard_map/ppermute | solution.py:407
  437.4 17.5 %copy-start.36 = (bf16[1024,2048]{1,0:T(8,128)(2,1)S(1)}, bf16[1024,2048]{1,0:T(8,128)(2,1)}, u32[]{:S(2)}) copy-start(bf16[1024,2048]{1,0:T(8,128)(2,1)} %cot_ref.1) | copy-start | bytes 12582916
  454.9 13.1 %collective-permute-start.10 = (bf16[512,2048]{1,0:T(8,128)(2,1)}, bf16[512,2048]{1,0:T(8,128)(2,1)}, u32[]{:S(2)}, u32[]{:S(2)}) collective-permute-start(bf16[512,2048]{1,0:T(8,128)(2,1)} %pad_maximum_fusion.3), channel_id=1, source_target_pairs={{0,4},{4,0},{8,12},{12,8},{1,5},{5,1},{9,13},{13,9},{2,6},{6,2},{1... | collective-permute-start | bytes 6291464 | tf_op jit(solution)/shard_map/ppermute | solution.py:407
  465.0 191.2 %reduce-scatter.11.cloned.1.call-start = ((), (), s32[]{:S(2)}) async-start(), calls=%async_computation.8 | async-start | bytes 3145728 | tf_op jit(solution)/shard_map/reduce_scatter | solution.py:535
  472.6 21.2 %slice-start = ((s8[6291456]{0:T(1024)(128)(4,1)}), s8[4194304]{0:T(1024)(128)(4,1)S(1)}, s32[]{:S(2)}) async-start(s8[6291456]{0:T(1024)(128)(4,1)} %bitcast.143), calls=%async_computation.13 | async-start | bytes 8388608
  477.5 16.4 %slice-start.1 = ((s8[6291456]{0:T(1024)(128)(4,1)}), s8[2097152]{0:T(1024)(128)(4,1)S(1)}, s32[]{:S(2)}) async-start(s8[6291456]{0:T(1024)(128)(4,1)} %bitcast.143), calls=%async_computation.14 | async-start | bytes 4194304
  477.5 27.3 %slice-start.4 = ((s8[8388608]{0:T(1024)(128)(4,1)}), s8[4194304]{0:T(1024)(128)(4,1)S(1)}, s32[]{:S(2)}) async-start(s8[8388608]{0:T(1024)(128)(4,1)} %bitcast.152), calls=%async_computation.17 | async-start | bytes 8388608
  493.9 10.9 %slice-start.5 = ((s8[8388608]{0:T(1024)(128)(4,1)}), s8[4194304]{0:T(1024)(128)(4,1)S(1)}, s32[]{:S(2)}) async-start(s8[8388608]{0:T(1024)(128)(4,1)} %bitcast.152), calls=%async_computation.18 | async-start | bytes 8388608
  504.4 8.0 collective-permute-start.11
  510.9 239.9 %all-reduce.3.cloned.1.call-start = ((), (), s32[]{:S(2)}) async-start(), calls=%async_computation.12 | async-start | bytes 163840 | tf_op jit(solution)/shard_map/psum | solution.py:582
  516.7 25.7 %copy-start.37 = (f32[2048]{0:T(1024)S(1)}, f32[2048]{0:T(1024)}, u32[]{:S(2)}) copy-start(f32[2048]{0:T(1024)} %param.19) | copy-start | bytes 24580
  516.9 25.6 %collective-permute-start.12 = (bf16[256,2048]{1,0:T(8,128)(2,1)S(1)}, bf16[256,2048]{1,0:T(8,128)(2,1)S(1)}, u32[]{:S(2)}, u32[]{:S(2)}) collective-permute-start(bf16[256,2048]{1,0:T(8,128)(2,1)S(1)} %slice.185), channel_id=1, source_target_pairs={{0,8},{4,12},{8,0},{12,4},{1,9},{5,13},{9,1},{13,5},{2,10},{6,14},... | collective-permute-start | bytes 3145736 | tf_op jit(solution)/shard_map/ppermute | solution.py:407
  546.5 208.5 %reduce-scatter.9.cloned.1.call-start = ((), (), s32[]{:S(2)}) async-start(), calls=%async_computation.7 | async-start | bytes 2359296 | tf_op jit(solution)/shard_map/reduce_scatter | solution.py:562
  553.0 241.2 %reduce-scatter.7.cloned.1.call-start = ((), (), s32[]{:S(2)}) async-start(), calls=%async_computation.6 | async-start | bytes 7077888 | tf_op jit(solution)/shard_map/reduce_scatter | solution.py:562
  570.9 25.2 %collective-permute-start.4 = (bf16[256,2048]{1,0:T(8,128)(2,1)}, bf16[256,2048]{1,0:T(8,128)(2,1)S(1)}, u32[]{:S(2)}, u32[]{:S(2)}) collective-permute-start(bf16[256,2048]{1,0:T(8,128)(2,1)} %get-tuple-element.82), channel_id=1, source_target_pairs={{0,8},{4,12},{8,0},{12,4},{1,9},{5,13},{9,1},{13,5},{2,10},{6,14},... | collective-permute-start | bytes 3145736 | tf_op jit(solution)/shard_map/ppermute | solution.py:407
  572.1 80.4 %collective-permute-start.16 = (bf16[1024,512]{1,0:T(8,128)(2,1)}, bf16[1024,512]{1,0:T(8,128)(2,1)}, u32[]{:S(2)}, u32[]{:S(2)}) collective-permute-start(bf16[1024,512]{1,0:T(8,128)(2,1)} %reduce-scatter.17.cloned.1.call-done), channel_id=1, source_target_pairs={{0,2},{1,3},{2,0},{3,1},{4,6},{5,7},{6,4},{7,5},{8,10},{9,11},{10,... | collective-permute-start | bytes 3145736 | tf_op jit(solution)/shard_map/ppermute | solution.py:407
  576.5 107.2 %collective-permute-start.15 = (bf16[1024,512]{1,0:T(8,128)(2,1)}, bf16[1024,512]{1,0:T(8,128)(2,1)}, u32[]{:S(2)}, u32[]{:S(2)}) collective-permute-start(bf16[1024,512]{1,0:T(8,128)(2,1)} %reduce-scatter.13.cloned.1.call-done), channel_id=1, source_target_pairs={{0,2},{1,3},{2,0},{3,1},{4,6},{5,7},{6,4},{7,5},{8,10},{9,11},{10,... | collective-permute-start | bytes 3145736 | tf_op jit(solution)/shard_map/ppermute | solution.py:407
  599.3 93.5 %collective-permute-start.5 = (bf16[512,2048]{1,0:T(8,128)(2,1)}, bf16[512,2048]{1,0:T(8,128)(2,1)}, u32[]{:S(2)}, u32[]{:S(2)}) collective-permute-start(bf16[512,2048]{1,0:T(8,128)(2,1)} %pad_maximum_fusion.2), channel_id=1, source_target_pairs={{0,4},{4,0},{8,12},{12,8},{1,5},{5,1},{9,13},{13,9},{2,6},{6,2},{1... | collective-permute-start | bytes 6291464 | tf_op jit(solution)/shard_map/ppermute | solution.py:407
  608.0 82.1 %collective-permute-start.13 = (bf16[256,2048]{1,0:T(8,128)(2,1)S(1)}, bf16[256,2048]{1,0:T(8,128)(2,1)}, u32[]{:S(2)}, u32[]{:S(2)}) collective-permute-start(bf16[256,2048]{1,0:T(8,128)(2,1)S(1)} %get-tuple-element.77), channel_id=1, source_target_pairs={{0,8},{4,12},{8,0},{12,4},{1,9},{5,13},{9,1},{13,5},{2,10},{6,14},... | collective-permute-start | bytes 3145736 | tf_op jit(solution)/shard_map/ppermute | solution.py:407
  656.2 32.9 %copy-start.32 = (bf16[256,2048]{1,0:T(8,128)(2,1)S(1)}, bf16[256,2048]{1,0:T(8,128)(2,1)}, u32[]{:S(2)}) copy-start(bf16[256,2048]{1,0:T(8,128)(2,1)} %copy-done.31) | copy-start | bytes 3145732
  692.8 67.0 %collective-permute-start.14 = (bf16[512,2048]{1,0:T(8,128)(2,1)}, bf16[512,2048]{1,0:T(8,128)(2,1)S(1)}, u32[]{:S(2)}, u32[]{:S(2)}) collective-permute-start(bf16[512,2048]{1,0:T(8,128)(2,1)} %pad_maximum_fusion.5), channel_id=1, source_target_pairs={{0,4},{4,0},{8,12},{12,8},{1,5},{5,1},{9,13},{13,9},{2,6},{6,2},{1... | collective-permute-start | bytes 6291464 | tf_op jit(solution)/shard_map/ppermute | solution.py:407
  (37 other events, 165.5 us)
Sparse Core Ops, SparseCore 0:
  316.5 32.9 reduce-scatter.16
  400.9 33.5 reduce-scatter.12
  465.1 33.1 reduce-scatter.14
  511.0 33.2 reduce-scatter.10
  553.2 118.1 reduce-scatter.8
  674.8 119.4 reduce-scatter.6
Sparse Core Ops, SparseCore 1:
  546.6 204.2 all-reduce.2

commit v3 on v2

--- a/solution.py
+++ b/solution.py
@@ -31,11 +31,6 @@
         - normed * jnp.mean(scaled * normed, -1, keepdims=True)
     )
     return inverse * inner, jnp.sum(grad_in * normed, 0), jnp.sum(grad_in, 0)
-
-
-def softmax(scores):
-    expo = jnp.exp(scores - jnp.max(scores, -1, keepdims=True))
-    return expo / jnp.sum(expo, -1, keepdims=True)
 
 
 def layout(lengths_row, tok_rows):
@@ -202,7 +197,7 @@
     n2_ref,
     up_other_ref,
     down_other_ref,
-    near_cot_ref,
+    cots_ref,
     away_ref,
     got_core_ref,
     pass_ref,
@@ -211,6 +206,7 @@
     send_sems,
     recv_sems,
     local_sem,
+    local_sems,
 ):
     t, z, x = lax.axis_index("tensor"), lax.axis_index("bucket"), lax.axis_index("dp")
     rows, own = q_ref.shape
@@ -231,8 +227,14 @@
 
     up_piece = links.start(piece(up_ref, x), piece(up_other_ref, x), far)
     parity = lax.rem(t, 2)
+    keep_cots = [
+        pltpu.make_async_copy(shard(cot_ref, i), cots_ref.at[0, i], local_sems.at[i])
+        for i in range(cots_ref.shape[1])
+    ]
+    for copy in keep_cots:
+        copy.start()
     cots = [
-        links.start(shard(cot_ref, parity + i), shard(near_cot_ref, parity + i), near)
+        links.start(shard(cot_ref, parity + i), cots_ref.at[1, parity + i], near)
         for i in (0, 2)
     ]
     down_piece = links.start(piece(down_ref, x), piece(down_other_ref, x), far)
@@ -296,7 +298,7 @@
         onward.extend(links.start(ref, ref, device) for device in devices)
 
     for i, copy in zip((0, 2), cots):
-        pass_on(copy, shard(near_cot_ref, parity + i), [core])
+        pass_on(copy, cots_ref.at[1, parity + i], [core])
     pass_on(up_piece, piece(up_other_ref, x), twins)
     to_y.wait_recv()
     total = middle_ref[...] + got_y_ref[...].astype(F32)
@@ -316,7 +318,8 @@
     near_y.wait_recv()
     near_y_core = links.start(n2_ref.at[1, t ^ 2], n2_ref.at[1, t ^ 2], core)
     pass_on(down_piece, piece(down_other_ref, x), twins)
-    keep_own.wait()
+    for copy in (keep_own, *keep_cots):
+        copy.wait()
     for copy in (own_core, y_core, near_core, near_y_core, *onward):
         copy.wait_recv()
     for copy in (
@@ -350,7 +353,7 @@
             shape((2, splits, share, width), BF16),
             shape(up.shape, BF16),
             shape(down.shape, BF16),
-            shape(cotangent.shape, BF16),
+            shape((2, splits, share, width), BF16),
         ],
         scratch_shapes=[
             pltpu.VMEM((2, share, width), BF16),
@@ -361,6 +364,7 @@
             pltpu.SemaphoreType.DMA((total,)),
             pltpu.SemaphoreType.DMA((total,)),
             pltpu.SemaphoreType.DMA,
+            pltpu.SemaphoreType.DMA((splits,)),
         ],
         compiler_params=pltpu.CompilerParams(
             vmem_limit_bytes=56 << 20, collective_id=0, has_side_effects=True
@@ -372,6 +376,371 @@
         ),
         name="front",
     )(tokens, *ln1, w3, *tables_, first, keep, w_out, *ln2, up, down, cotangent)
+
+
+def block_at(i, t):
+    late = i // 4
+    near = (1 - late) * (1 - (i // 2) % 2) + late * (1 - i % 2)
+    bit = (1 - late) * (3 - 2 * (i % 2)) + late * (2 - 2 * ((i % 4) // 2))
+    return near, t ^ bit
+
+
+def router_gate(rows, w_router_ref, level):
+    logits = dot(rows, w_router_ref[...], NN)
+    expo = jnp.exp(logits - jnp.max(logits, -1, keepdims=True))
+    probs = expo / jnp.sum(expo, -1, keepdims=True)
+    number = lax.broadcasted_iota(jnp.int32, probs.shape, 1).astype(F32)
+    onehot = (number == level).astype(F32)
+    return jnp.sum(probs * onehot, -1, keepdims=True), probs, onehot
+
+
+def middle_kernel(
+    copies,
+    n2_ref,
+    cot_ref,
+    up_own_ref,
+    up_other_ref,
+    down_own_ref,
+    down_other_ref,
+    router_ref,
+    level_ref,
+    x2_ref,
+    gain2_ref,
+    bias2_ref,
+    mixed_ref,
+    gx2_ref,
+    ga_ref,
+    small_ref,
+    gf_ref,
+    grad_down_ref,
+    grad_up_ref,
+    got_x_ref,
+    n2_in,
+    cot_in,
+    gf_out,
+    hid_ref,
+    gu_ref,
+    part_f,
+    part_g,
+    hold_f,
+    send_ref,
+    core_f,
+    core_g,
+    got_fz,
+    got_fy,
+    got_gy,
+    got_gz,
+    tile_in,
+    tile_out,
+    core_send_sems,
+    core_recv_sems,
+    send_sems,
+    recv_sems,
+    in_sems,
+    out_sems,
+    tile_sems,
+    tile_out_sems,
+):
+    t, z, x = lax.axis_index("tensor"), lax.axis_index("bucket"), lax.axis_index("dp")
+    share, width = gx2_ref.shape
+    half = up_own_ref.shape[1]
+    core, y_side, near = {"tensor": t ^ 1}, {"tensor": t ^ 2}, {"bucket": z ^ 1}
+    twins = [{"dp": lax.rem(x + d, copies)} for d in range(1, copies)]
+    splits = n2_ref.shape[1]
+
+    def load(i, slot):
+        at, s = block_at(i, t)
+        return (
+            pltpu.make_async_copy(n2_ref.at[at, s], n2_in.at[slot], in_sems.at[slot, 0]),
+            pltpu.make_async_copy(cot_ref.at[at, s], cot_in.at[slot], in_sems.at[slot, 1]),
+        )
+
+    def store(i, slot):
+        at, s = block_at(i, t)
+        return pltpu.make_async_copy(gf_out.at[slot], gf_ref.at[at, s], out_sems.at[slot])
+
+    def to_core(i):
+        return [
+            pltpu.make_async_remote_copy(
+                src_ref=send_ref.at[kind * 2 + i % 2],
+                dst_ref=(core_f, core_g)[kind].at[i],
+                send_sem=core_send_sems.at[kind, i],
+                recv_sem=core_recv_sems.at[kind, i],
+                device_id=core,
+                device_id_type=pl.DeviceIdType.MESH,
+            )
+            for kind in (0, 1)
+        ]
+
+    for copy in load(0, 0):
+        copy.start()
+    meet([core, y_side, near] + twins)
+    links = Copies(send_sems, recv_sems)
+    f_near_y = links.make(send_ref.at[0], got_fz.at[0], near)
+    g_near_y = links.make(send_ref.at[1], got_gy.at[0], y_side)
+    g_own_y = links.make(send_ref.at[2], got_gy.at[1], y_side)
+    f_near = links.make(send_ref.at[3], got_fz.at[1], near)
+    f_own_y = links.make(send_ref.at[0], got_fy, y_side)
+    g_near = links.make(send_ref.at[1], got_gz, near)
+
+    def work(i, carry):
+        slot = i % 2
+        at, s = block_at(i, t)
+        for copy in load(i, slot):
+            copy.wait()
+
+        @pl.when(i < 7)
+        def _():
+            for copy in load(i + 1, 1 - slot):
+                copy.start()
+
+        @pl.when(i >= 2)
+        def _():
+            store(i - 2, slot).wait()
+
+        spot = pl.ds(pl.multiple_of((at * splits + s) * share, share), share)
+        rows = n2_in[slot]
+        level = level_ref[spot, :]
+        gate, _, _ = router_gate(rows, router_ref, level)
+        grad = (gate * cot_in[slot].astype(F32)).astype(BF16)
+        gf_out[slot] = grad
+        store(i, slot).start()
+        for part, (up_ref, down_ref, unit_level) in enumerate(
+            ((up_own_ref, down_own_ref, z), (up_other_ref, down_other_ref, z ^ 2))
+        ):
+            lanes = slice(part * half, (part + 1) * half)
+            kept = level >= unit_level.astype(F32)
+            act = jnp.where(kept, jnp.maximum(dot(rows, up_ref[...], NN), 0.0), 0.0)
+            hid_ref[spot, lanes] = (act * act).astype(BF16)
+            back = dot(grad, down_ref[...], NT)
+            gu_ref[spot, lanes] = (back * 2.0 * act).astype(BF16)
+        for lanes in (slice(0, width // 2), slice(width // 2, width)):
+            part_f[:, lanes] = dot(hid_ref[spot, :half], down_own_ref[:, lanes], NN) + dot(
+                hid_ref[spot, half:], down_other_ref[:, lanes], NN
+            )
+            part_g[:, lanes] = dot(gu_ref[spot, :half], up_own_ref[lanes, :], NT) + dot(
+                gu_ref[spot, half:], up_other_ref[lanes, :], NT
+            )
+
+        @pl.when(i < 4)
+        def _():
+            @pl.when(i >= 2)
+            def _():
+                for copy in to_core(i - 2):
+                    copy.wait_send()
+
+            send_ref[slot] = part_f[...].astype(BF16)
+            send_ref[2 + slot] = part_g[...].astype(BF16)
+            for copy in to_core(i):
+                copy.start()
+
+        def with_core(kind, at_i):
+            to_core(at_i)[kind].wait_recv()
+            got = (core_f, core_g)[kind][at_i].astype(F32)
+            return (part_f, part_g)[kind][...] + got
+
+        @pl.when(i == 4)
+        def _():
+            for j in (2, 3):
+                for copy in to_core(j):
+                    copy.wait_send()
+            send_ref[1] = with_core(1, 0).astype(BF16)
+            g_near_y.start()
+            send_ref[0] = with_core(0, 0).astype(BF16)
+            f_near_y.start()
+
+        @pl.when(i == 5)
+        def _():
+            send_ref[2] = with_core(1, 2).astype(BF16)
+            g_own_y.start()
+            hold_f[...] = with_core(0, 2)
+
+        @pl.when(i == 6)
+        def _():
+            send_ref[3] = with_core(0, 1).astype(BF16)
+            f_near.start()
+            gx2_ref[...] = with_core(1, 1)
+
+        @pl.when(i == 7)
+        def _():
+            part_f[...] = with_core(0, 3)
+            part_g[...] = with_core(1, 3)
+
+        return carry
+
+    lax.fori_loop(0, 8, work, 0)
+    store(6, 0).wait()
+    store(7, 1).wait()
+
+    tile = tile_in.shape[-1]
+    tiles = width // tile
+
+    def weight_grads(source_ref, right_ref, result_ref):
+        def fetch(j, slot):
+            lanes = pl.ds(pl.multiple_of(j * tile, tile), tile)
+            return pltpu.make_async_copy(
+                source_ref.at[:, :, :, lanes], tile_in.at[slot], tile_sems.at[slot]
+            )
+
+        def put(j, slot):
+            rows = pl.ds(pl.multiple_of(j * tile, tile), tile)
+            return pltpu.make_async_copy(
+                tile_out.at[slot], result_ref.at[rows, :], tile_out_sems.at[slot]
+            )
+
+        fetch(0, 0).start()
+
+        def step(j, carry):
+            slot = j % 2
+            fetch(j, slot).wait()
+
+            @pl.when(j < tiles - 1)
+            def _():
+                fetch(j + 1, 1 - slot).start()
+
+            @pl.when(j >= 2)
+            def _():
+                put(j - 2, slot).wait()
+
+            left = tile_in[slot].reshape(-1, tile)
+            tile_out[slot] = dot(left, right_ref[...], TN).astype(BF16)
+            put(j, slot).start()
+            return carry
+
+        lax.fori_loop(0, tiles, step, 0)
+        put(tiles - 2, (tiles - 2) % 2).wait()
+        put(tiles - 1, (tiles - 1) % 2).wait()
+
+    weight_grads(gf_ref, hid_ref, grad_down_ref)
+    size = width // copies
+    downs = []
+    for d in range(1, copies):
+        part = pl.ds(pl.multiple_of(lax.rem(x + d, copies) * size, size), size)
+        downs.append(
+            links.start(grad_down_ref.at[part, :], got_x_ref.at[d - 1], twins[d - 1])
+        )
+
+    f_near_y.wait_recv()
+    f_near_y.wait_send()
+    send_ref[0] = (hold_f[...] + got_fz[0].astype(F32)).astype(BF16)
+    f_own_y.start()
+    g_near_y.wait_recv()
+    g_near_y.wait_send()
+    send_ref[1] = (gx2_ref[...] + got_gy[0].astype(F32)).astype(BF16)
+    g_near.start()
+
+    weight_grads(n2_ref, gu_ref, grad_up_ref)
+
+    own = pltpu.make_async_copy(n2_ref.at[0, t], n2_in.at[0], in_sems.at[0, 0])
+    own.start()
+    own_cot = pltpu.make_async_copy(cot_ref.at[0, t], cot_in.at[0], in_sems.at[0, 1])
+    own_cot.start()
+    own.wait()
+    own_cot.wait()
+    for copy in (f_near, f_own_y, g_own_y, g_near):
+        copy.wait_recv()
+    small_ref[...] = jnp.zeros_like(small_ref)
+    few = 64
+
+    def finish(j, carry):
+        at = pl.ds(pl.multiple_of(j * few, few), few)
+        level = level_ref[pl.ds(pl.multiple_of(t * share + j * few, few), few), :]
+        rows = n2_in[0, at, :]
+        gate, probs, onehot = router_gate(rows, router_ref, level)
+        branch = part_f[at, :] + got_fz[1, at, :].astype(F32) + got_fy[at, :].astype(F32)
+        branch = branch.astype(BF16).astype(F32)
+        x2 = x2_ref[at, :]
+        mixed_ref[at, :] = (x2 + gate * branch).astype(BF16)
+        grad_out = cot_in[0, at, :].astype(F32)
+        grad_gate = jnp.sum(grad_out * branch, -1, keepdims=True)
+        grad_logits = grad_gate * gate * (onehot - probs)
+        returned = part_g[at, :] + got_gy[1, at, :].astype(F32) + got_gz[at, :].astype(F32)
+        grad_n2 = returned.astype(BF16).astype(F32)
+        grad_n2 += lax.dot_general(
+            grad_logits,
+            router_ref[...].astype(F32),
+            (NT, ((), ())),
+            precision=HIGH,
+            preferred_element_type=F32,
+        )
+        hat, inverse = norm_parts(x2)
+        back, gain_grad, bias_grad = norm_backward(grad_n2, hat, inverse, gain2_ref[...])
+        gx2 = grad_out + back
+        gx2_ref[at, :] = gx2
+        ga_ref[at, :] = gx2.astype(BF16)
+        small_ref[0:1, :] += gain_grad[None, :]
+        small_ref[1:2, :] += bias_grad[None, :]
+        small_ref[2 : 2 + probs.shape[1], :] += lax.dot_general(
+            grad_logits, rows.astype(F32), (TN, ((), ())), precision=HIGH, preferred_element_type=F32
+        )
+        return carry
+
+    lax.fori_loop(0, share // few, finish, 0)
+    for copy in downs:
+        copy.wait_recv()
+    for copy in (g_own_y, f_near, f_own_y, g_near, *downs):
+        copy.wait_send()
+
+
+def middle_call(n2, cotangents, ups, downs, w_router, levels, middle, ln2):
+    _, splits, share, width = n2.shape
+    copies = lax.axis_size("dp")
+    half = ups[0].shape[1]
+    rows = 2 * splits * share
+    inside = pl.BlockSpec(memory_space=pltpu.VMEM)
+    outside = pl.BlockSpec(memory_space=pl.ANY)
+    shape = jax.ShapeDtypeStruct
+    block = lambda count, dtype=BF16: pltpu.VMEM((*count, share, width), dtype)
+    dma = lambda *count: pltpu.SemaphoreType.DMA(count)
+    return pl.pallas_call(
+        functools.partial(middle_kernel, copies),
+        in_specs=[outside] * 2 + [inside] * 9,
+        out_specs=[inside] * 4 + [outside] * 4,
+        out_shape=[
+            shape((share, width), BF16),
+            shape((share, width), F32),
+            shape((share, width), BF16),
+            shape((2 + w_router.shape[1], width), F32),
+            shape(n2.shape, BF16),
+            shape((width, 2 * half), BF16),
+            shape((width, 2 * half), BF16),
+            shape((copies - 1, width // copies, 2 * half), BF16),
+        ],
+        scratch_shapes=[
+            block((2,)),
+            block((2,)),
+            block((2,)),
+            pltpu.VMEM((rows, 2 * half), BF16),
+            pltpu.VMEM((rows, 2 * half), BF16),
+            block((), F32),
+            block((), F32),
+            block((), F32),
+            block((4,)),
+            block((4,)),
+            block((4,)),
+            block((2,)),
+            block(()),
+            block((2,)),
+            block(()),
+            pltpu.VMEM((2, 2, splits, share, 256), BF16),
+            pltpu.VMEM((2, 256, 2 * half), BF16),
+            dma(2, 4),
+            dma(2, 4),
+            dma(6 + copies - 1),
+            dma(6 + copies - 1),
+            dma(2, 2),
+            dma(2),
+            dma(2),
+            dma(2),
+        ],
+        compiler_params=pltpu.CompilerParams(
+            vmem_limit_bytes=62 << 20, collective_id=1, has_side_effects=True
+        ),
+        cost_estimate=pl.CostEstimate(
+            flops=12 * rows * width * 2 * half, bytes_accessed=80 << 20, transcendentals=0
+        ),
+        name="middle",
+    )(n2, cotangents, *ups, *downs, w_router, levels, middle, *ln2)
 
 
 def qkv_back_kernel(g_ref, w_ref, o_ref):
@@ -457,7 +826,7 @@
         n2,
         up_other,
         down_other,
-        near_cotangent,
+        cotangents,
     ) = front_call(
         tokens,
         (ln1_gain.reshape(1, -1), ln1_bias.reshape(1, -1)),
@@ -472,8 +841,27 @@
         cotangent,
     )
     logs = logs.T[:, :, None]
-    normed2 = lax.dynamic_index_in_dim(n2[0], t, 0, False)
-    n2 = n2.reshape(-1, model_width)
+    level_all = jnp.concatenate([levels.reshape(-1), near_levels.reshape(-1)], 0)[:, None]
+    (
+        mixed_own,
+        grad_middle,
+        grad_attention_own,
+        small,
+        _,
+        down_part,
+        up_part,
+        got_down,
+    ) = middle_call(
+        n2,
+        cotangents,
+        (up_own, up_other),
+        (down_own, down_other),
+        w_router,
+        level_all,
+        middle,
+        (ln2_gain.reshape(1, -1), ln2_bias.reshape(1, -1)),
+    )
+    inputs_own = shard(tokens, 0).astype(F32)
 
     def gather_sum(away, kept):
         both = kept + swap(away.astype(BF16), "tensor", 1).astype(F32)
@@ -491,72 +879,20 @@
             whole = lax.dynamic_update_slice_in_dim(whole, part, (t ^ bit) * share, 0)
         return whole
 
-    inputs_own = shard(tokens, 0).astype(F32)
-    hat2, inverse2 = norm_parts(middle)
-
-    def gate_of(rows, tok_levels):
-        probs = softmax(dot(rows, w_router, NN))
-        onehot = (tok_levels[:, None] == jnp.arange(owners, dtype=F32)[None, :]).astype(F32)
-        return jnp.sum(probs * onehot, -1), probs, onehot
-
-    level_all = jnp.concatenate([levels.reshape(-1), near_levels.reshape(-1)], 0)
-    gate_all, _, _ = gate_of(n2, level_all)
-    grad_all = jnp.concatenate([cotangent, near_cotangent], 0)
-    grad_branch = (gate_all[:, None] * grad_all.astype(F32)).astype(BF16)
-    kept_own = (level_all >= z.astype(F32))[:, None]
-    kept_other = (level_all >= (z ^ 2).astype(F32))[:, None]
-
-    def forward(up, kept):
-        act = jnp.where(kept, jnp.maximum(dot(n2, up, NN), 0.0), 0.0)
-        return act.astype(BF16), jnp.square(act).astype(BF16)
-
-    act_own, hid_own = forward(up_own, kept_own)
-    act_other, hid_other = forward(up_other, kept_other)
-
-    def scatter_sum(total):
-        blocks = total.astype(BF16).reshape(2, splits, share, model_width)
-        pick = lambda bits: jnp.stack(
-            [lax.dynamic_index_in_dim(blocks, t ^ bit, 1, False) for bit in bits], 1
-        )
-        both = pick((0, 2)).astype(F32) + swap(pick((1, 3)), "tensor", 1).astype(F32)
-        one = both[:, 0] + swap(both[:, 1].astype(BF16), "tensor", 2).astype(F32)
-        return one[0] + swap(one[1].astype(BF16), "bucket", 1).astype(F32)
-
-    branch_sum = scatter_sum(dot(hid_own, down_own, NN) + dot(hid_other, down_other, NN))
-
-    def backward(act, down):
-        grad = dot(grad_branch, down, NT)
-        return (grad * 2.0 * act.astype(F32)).astype(BF16)
-
-    gu_own, gu_other = backward(act_own, down_own), backward(act_other, down_other)
-    returned = scatter_sum(dot(gu_own, up_own, NT) + dot(gu_other, up_other, NT))
-
-    def reduce_dp(grad, dim):
-        return lax.psum_scatter(grad.astype(BF16), "dp", scatter_dimension=dim, tiled=True)
-
-    def owner_sum(own, other):
-        return own.astype(F32) + swap(other, "bucket", 2).astype(F32)
-
-    grad_down = owner_sum(
-        reduce_dp(dot(grad_branch, hid_own, TN), 0), reduce_dp(dot(grad_branch, hid_other, TN), 0)
-    ).T
-    grad_up = owner_sum(
-        reduce_dp(dot(n2, gu_own, TN), 0), reduce_dp(dot(n2, gu_other, TN), 0)
-    )
-
-    branch = branch_sum.astype(BF16).astype(F32)
-    level_own = shard(levels.reshape(-1), 0)
-    gate, probs, onehot = gate_of(normed2, level_own)
-    mixed_own = (middle + gate[:, None] * branch).astype(BF16)
+    size = model_width // copies
+    down_sum = lax.dynamic_slice_in_dim(down_part, x * size, size, 0).astype(F32)
+    down_sum += jnp.sum(got_down.astype(F32), 0)
+    up_sum = lax.psum_scatter(up_part, "dp", scatter_dimension=0, tiled=True).astype(F32)
+
+    def owner_sum(total):
+        return total[:, :hidden_width] + swap(
+            total[:, hidden_width:].astype(BF16), "bucket", 2
+        ).astype(F32)
+
+    grad_down = owner_sum(down_sum).T
+    grad_up = owner_sum(up_sum)
     mixed = natural(spread(mixed_own), BF16)
-    grad_output = shard(cotangent, 0).astype(F32)
-    grad_gate = jnp.sum(grad_output * branch, -1)
-    grad_logits = (grad_gate * gate)[:, None] * (onehot - probs)
-    grad_router = dot(normed2.astype(F32), grad_logits, TN)
-    grad_norm2 = returned.astype(BF16).astype(F32) + dot(grad_logits, w_router.astype(F32), NT)
-    grad_in2, grad_ln2_gain, grad_ln2_bias = norm_backward(grad_norm2, hat2, inverse2, ln2_gain)
-    grad_middle = grad_output + grad_in2
-    grad_attention = natural(spread(grad_middle.astype(BF16)), BF16)
+    grad_attention = natural(spread(grad_attention_own), BF16)
 
     def reduce_all(grad):
         return lax.psum_scatter(
@@ -583,7 +919,7 @@
         width = model_width // (copies * owners)
         return lax.dynamic_slice_in_dim(total, (x * owners + z) * width, width, 1)
 
-    small = reduce_small(grad_ln2_gain, grad_ln2_bias, *(grad_router[:, i] for i in range(owners)))
+    small = reduce_small(*(small[i] for i in range(2 + owners)))
     last = reduce_small(grad_ln1_gain, grad_ln1_bias)
     return (
         mixed,

time: 810 us -> 680 us (0.84)
  matrix products: 131 us -> 20 us
  Pallas kernels: 197 us -> 306 us
  waiting for transfers between devices: 293 us -> 228 us
  other arithmetic: 65.7 us -> 32.4 us
  local copies, waits for them, and re-layouts: 88.7 us -> 55.5 us
    ppermute x17 -> x11, waiting for transfers between devices: 208 us -> 86.3 us  [swap(): return lax.ppermute(values, axis, pairs)]
    dot_general x19 -> x3, matrix products: 131 us -> 20 us  [dot(): lax.dot_general(left, right, (dims, ((), ())), preferred_element_type=F32)]
    pallas_call x0 -> x1, Pallas kernels: none -> 109 us  [middle_call(): pl.pallas_call(functools.partial(middle_kernel, copies), in_specs=[outsid...]
    psum x1, waiting for transfers between devices: 53.4 us -> 122 us  [reduce_small(): total = lax.psum(stacked, ('dp', 'tensor', 'bucket'))]
    unnamed x128 -> x59, local copies, waits for them, and re-layouts: 42.8 us -> 18.5 us
    reduce_scatter x2, waiting for transfers between devices: 31.3 us -> 20 us  [reduce_all(): lax.psum_scatter(grad.astype(BF16), ('dp', 'bucket'), scatter_dimension=0...]
    add x4 -> x1, other arithmetic: 13 us -> 3.15 us  [local(): down_sum += jnp.sum(got_down.astype(F32), 0)]
    ppermute x17 -> x11, starting transfers between devices: 11.8 us -> 16.6 us  [swap(): return lax.ppermute(values, axis, pairs)]
  transfers between devices with their start and end apart: 24 -> 15, of which waited for: 10 -> 7; matrix products, arithmetic and copies ran while one was open for 27% -> 13% of each run, Pallas kernels for 24% -> 29%
where the time goes in v3:
time: 680 us; the launch traced here: 675 us
  Pallas kernels  306 us (45%)
  waiting for transfers between devices  228 us (34%)
  local copies, waits for them, and re-layouts  55.5 us (8%)
  other arithmetic  32.4 us (5%)
  matrix products  20 us (3%)
  starting transfers between devices  16.8 us (2%)
  between operations  16 us (2%)
    pallas_call x1, Pallas kernels, front_call(): pl.pallas_call(functools.partial(front_kernel, copies), in_specs=[inside]...  173 us
    psum x1, waiting for transfers between devices, reduce_small(): total = lax.psum(stacked, ('dp', 'tensor', 'bucket'))  122 us
    pallas_call x1, Pallas kernels, middle_call(): pl.pallas_call(functools.partial(middle_kernel, copies), in_specs=[outsid...  109 us
    ppermute x11, waiting for transfers between devices, swap(): return lax.ppermute(values, axis, pairs)  86.3 us
    reduce_scatter x2, waiting for transfers between devices, reduce_all(): lax.psum_scatter(grad.astype(BF16), ('dp', 'bucket'), scatter_dimension=0...  20 us
    dot_general x3, matrix products, dot(): lax.dot_general(left, right, (dims, ((), ())), preferred_element_type=F32)  20 us
    unnamed x59, local copies, waits for them, and re-layouts  18.5 us
    ppermute x11, starting transfers between devices, swap(): return lax.ppermute(values, axis, pairs)  16.6 us
  transfers between devices with their start and end apart: 15, of which 7 were waited for; matrix products, arithmetic and copies ran while one was open for 13% of the time, Pallas kernels for 29%

profile of v3, /device:TPU:0, one launch (start us, length us, event | category | flops | bytes accessed | tf_op | source)
XLA Modules:
  0.0 674.9 jit_solution(12411168559097059260)
XLA Ops:
  8.7 3.0 collective-permute-start
  16.2 1.9 fusion.13
  19.4 173.4 %front.1 = (bf16[1024,2048]{1,0:T(8,128)(2,1)}, bf16[1024,512]{1,0:T(8,128)(2,1)}, bf16[1024,512]{1,0:T(8,128)(2,1)}, bf16[1024,512]{1,0:T(8,128)(2,1)}, bf16[10...) custom-call(bf16[1024,2048]{1,0:T(8,128)(2,1)} %tokens_ref.1, ...), custom_call_target="tpu_custom_call" | custom-call | flops 10737418240 | bytes 62914560 | tf_op jit(solution)/shard_map/front/pallas_call | solution.py:341
  193.9 1.3 copy.46.level_ref
  195.3 108.7 %middle.1 = (bf16[256,2048]{1,0:T(8,128)(2,1)}, f32[256,2048]{1,0:T(8,128)}, bf16[256,2048]{1,0:T(8,128)(2,1)}, f32[6,2048]{1,0:T(8,128)}, bf16[2,4,256,2048]{3,...) custom-call(bf16[2,4,256,2048]{3,2,1,0:T(8,128)(2,1)} %get-tuple-element, ...), custom_call_target="tpu_custom_call" | custom-call | flops 51539607552 | bytes 83886080 | tf_op jit(solution)/shard_map/middle/pallas_call | solution.py:695
  304.0 3.0 collective-permute-start.3
  307.0 22.4 %collective-permute-done.3 = bf16[256,2048]{1,0:T(8,128)(2,1)S(1)} collective-permute-done((bf16[256,2048]{1,0:T(8,128)(2,1)}, bf16[256,2048]{1,0:T(8,128)(2,1)S(1)}, u32[]{:S(2)}, u32[]{:S(2)}) %collective-permute-start.3) | collective-permute-done | bytes 1048608 | tf_op jit(solution)/shard_map/ppermute | solution.py:776
  329.4 2.7 pad_maximum_fusion.1
  332.2 8.5 %copy.49.log_ref = f32[4,1024,1]{2,1,0:T(8,128)S(1)} copy(f32[4,1024,1]{0,1,2:T(8,128)} %bitcast.55) | data formatting | bytes 32768 | tf_op jit(solution)/shard_map/broadcast_in_dim | solution.py:843
  342.2 1.5 slice_dynamic-update-slice_fusion.1
  343.7 1.3 slice_dynamic-update-slice_fusion
  345.1 2.4 multiply_convert_fusion.go_ref
  348.9 16.5 %attend_back.1.g_ref = bf16[1024,1536]{1,0:T(8,128)(2,1)S(1)} custom-call(bf16[1024,512]{1,0:T(8,128)(2,1)S(1)} %copy-done.5, bf16[1024,512]{1,0:T(8,128)(2,1)S(1)} %copy-done.6, bf16[1024,512]{1,0:T(8,128)(2,1)S(1)} %copy-done.7, bf16[1024,512]{1,0:T(8,128)(2,1)S(1)} %multiply_convert_fusion.go_ref, s32[1024,1]{1,0:T(8,128)S(1)} %copy-done.2, ...), custom_call_target="tpu_custom_call" | custom-call | flops 5368709120 | bytes 7340032 | tf_op jit(solution)/shard_map/attend_back/pallas_call | solution.py:121
  365.4 7.3 %qkv_back.1 = bf16[1024,2048]{1,0:T(8,128)(2,1)S(1)} custom-call(bf16[1024,1536]{1,0:T(8,128)(2,1)S(1)} %attend_back.1.g_ref, bf16[3,2048,512]{2,1,0:T(8,128)(2,1)S(1)} %bitcast.53), custom_call_target="tpu_custom_call" | custom-call | flops 6442450944 | bytes 13631488 | tf_op jit(solution)/shard_map/qkv_back/pallas_call | solution.py:757
  374.4 3.8 collective-permute-done.5
  379.2 1.8 collective-permute-start.6
  382.1 22.6 %collective-permute-done.6 = bf16[256,2048]{1,0:T(8,128)(2,1)S(1)} collective-permute-done((bf16[256,2048]{1,0:T(8,128)(2,1)S(1)}, bf16[256,2048]{1,0:T(8,128)(2,1)S(1)}, u32[]{:S(2)}, u32[]{:S(2)}) %collective-permute-start.6) | collective-permute-done | bytes 1048608 | tf_op jit(solution)/shard_map/ppermute | solution.py:776
  406.6 6.3 convolution_convert_fusion.1
  413.0 11.3 %convolution_convert_fusion = bf16[2048,1536]{1,0:T(8,128)(2,1)} fusion(bf16[1024,2048]{1,0:T(8,128)(2,1)} %get-tuple-element.41, bf16[1024,1536]{1,0:T(8,128)(2,1)S(1)} %copy-done.4), kind=kOutput, calls=%fused_computation | convolution fusion | flops 6445596672 | bytes 13631488 | tf_op jit(solution)/shard_map/dot_general | solution.py:55
  425.5 1.7 collective-permute-start.1
  427.2 3.2 convert_add_fusion
  431.7 4.5 collective-permute-start.10
  436.2 14.0 %collective-permute-done.1 = bf16[256,2048]{1,0:T(8,128)(2,1)S(1)} collective-permute-done((bf16[256,2048]{1,0:T(8,128)(2,1)S(1)}, bf16[256,2048]{1,0:T(8,128)(2,1)S(1)}, u32[]{:S(2)}, u32[]{:S(2)}) %collective-permute-start.1) | collective-permute-done | bytes 1048608 | tf_op jit(solution)/shard_map/ppermute | solution.py:776
  450.2 1.6 pad_maximum_fusion
  455.0 2.2 convert_dynamic-update-slice_fusion.3
  457.1 3.4 copy-done.12
  460.5 1.7 collective-permute-start.7
  462.2 2.7 broadcast.42.clone
  465.9 23.5 %collective-permute-done.10 = bf16[1024,512]{1,0:T(8,128)(2,1)} collective-permute-done((bf16[1024,512]{1,0:T(8,128)(2,1)}, bf16[1024,512]{1,0:T(8,128)(2,1)}, u32[]{:S(2)}, u32[]{:S(2)}) %collective-permute-start.10) | collective-permute-done | bytes 1048608 | tf_op jit(solution)/shard_map/ppermute | solution.py:776
  489.5 1.6 fusion.12
  491.1 2.0 copy.54
  493.2 2.3 constant_dynamic-update-slice_fusion.2
  495.5 2.8 pad_maximum_fusion.3
  498.4 2.3 slice_dynamic-update-slice_fusion.3
  500.7 2.3 slice_dynamic-update-slice_fusion.2
  503.0 2.3 slice.91
  505.3 121.8 %all-reduce.3.cloned.1.call-done = (f32[2,2048]{1,0:T(2,128)}, f32[6,2048]{1,0:T(8,128)}) async-done(((f32[2,2048]{1,0:T(2,128)}, f32[6,2048]{1,0:T(8,128)}), (f32[2,2048]{1,0:T(2,128)}, f32[6,2048]{1,0:T(8,128)})) %all-reduce.3.cloned.1.call-update) | async-done | bytes 65552 | tf_op jit(solution)/shard_map/psum | solution.py:918
  627.1 1.4 fusion.17
  628.5 1.4 fusion.18
  629.9 1.4 dynamic-slice_bitcast_fusion
  633.3 2.9 convert_dynamic-update-slice_fusion.2
  636.2 1.6 add_bitcast_fusion
  637.8 3.5 copy.53
  641.3 1.6 convert_dynamic-update-slice_fusion.1
  642.9 1.6 convert_dynamic-update-slice_fusion
  644.4 20.0 %reduce-scatter.4.cloned.1.call-done = bf16[256,1536]{1,0:T(8,128)(2,1)} async-done(((bf16[2048,1536]{1,0:T(8,128)(2,1)}), bf16[256,1536]{1,0:T(8,128)(2,1)}) %reduce-scatter.4.cloned.1.call-update) | async-done | bytes 786448 | tf_op jit(solution)/shard_map/reduce_scatter | solution.py:898
  664.4 1.4 copy.50
  665.8 1.6 copy.51
  (108 shorter events, 24.9 us)
Async XLA Ops:
  8.0 495.0 %reduce-scatter.8.cloned.1.call-start = ((), (), s32[]{:S(2)}) async-start(), calls=%async_computation.5 | async-start | bytes 6291456 | tf_op jit(solution)/shard_map/reduce_scatter | solution.py:885
  8.7 185.2 %collective-permute-start = (f32[8,128]{1,0:T(8,128)S(1)}, f32[8,128]{1,0:T(8,128)S(1)}, u32[]{:S(2)}, u32[]{:S(2)}) collective-permute-start(f32[8,128]{1,0:T(8,128)S(1)} %bitcast.62), channel_id=1, source_target_pairs={{0,1},{1,0},{2,3},{3,2},{4,5},{5,4},{6,7},{7,6},{8,9},{9,8},{10,11... | collective-permute-start | bytes 12296 | tf_op jit(solution)/shard_map/ppermute | solution.py:776
  19.4 173.4 %copy-start.23 = (bf16[2048,4]{0,1:T(4,128)(2,1)S(1)}, bf16[2048,4]{0,1:T(4,128)(2,1)}, u32[]{:S(2)}) copy-start(bf16[2048,4]{0,1:T(4,128)(2,1)} %param.25) | copy-start | bytes 49156
  304.0 25.4 %collective-permute-start.3 = (bf16[256,2048]{1,0:T(8,128)(2,1)}, bf16[256,2048]{1,0:T(8,128)(2,1)S(1)}, u32[]{:S(2)}, u32[]{:S(2)}) collective-permute-start(bf16[256,2048]{1,0:T(8,128)(2,1)} %get-tuple-element.39), channel_id=1, source_target_pairs={{0,8},{4,12},{8,0},{12,4},{1,9},{5,13},{9,1},{13,5},{2,10},{6,14},... | collective-permute-start | bytes 3145736 | tf_op jit(solution)/shard_map/ppermute | solution.py:776
  332.1 10.1 %collective-permute-start.4 = (bf16[512,2048]{1,0:T(8,128)(2,1)}, bf16[512,2048]{1,0:T(8,128)(2,1)}, u32[]{:S(2)}, u32[]{:S(2)}) collective-permute-start(bf16[512,2048]{1,0:T(8,128)(2,1)} %pad_maximum_fusion.1), channel_id=1, source_target_pairs={{0,4},{4,0},{8,12},{12,8},{1,5},{5,1},{9,13},{13,9},{2,6},{6,2},{1... | collective-permute-start | bytes 6291464 | tf_op jit(solution)/shard_map/ppermute | solution.py:776
  332.1 295.0 %all-reduce.3.cloned.1.call-start = ((), (), s32[]{:S(2)}) async-start(), calls=%async_computation.6 | async-start | bytes 163840 | tf_op jit(solution)/shard_map/psum | solution.py:918
  340.7 1.2 copy-start.19
  342.2 2.8 copy-start.24
  345.0 2.5 copy-start.16
  345.0 2.5 copy-start
  345.1 2.5 copy-start.1
  345.1 2.5 copy-start.2
  345.1 3.2 copy-start.5
  345.1 3.5 copy-start.6
  345.1 3.8 copy-start.7
  345.1 20.3 %slice-start = ((s8[6291456]{0:T(1024)(128)(4,1)}), s8[4194304]{0:T(1024)(128)(4,1)S(1)}, s32[]{:S(2)}) async-start(s8[6291456]{0:T(1024)(128)(4,1)} %bitcast.51), calls=%async_computation.7 | async-start | bytes 8388608
  348.9 16.5 %slice-start.1 = ((s8[6291456]{0:T(1024)(128)(4,1)}), s8[2097152]{0:T(1024)(128)(4,1)S(1)}, s32[]{:S(2)}) async-start(s8[6291456]{0:T(1024)(128)(4,1)} %bitcast.51), calls=%async_computation.8 | async-start | bytes 4194304
  365.4 7.3 %copy-start.3 = (bf16[1024,1536]{1,0:T(8,128)(2,1)}, bf16[1024,1536]{1,0:T(8,128)(2,1)S(1)}, u32[]{:S(2)}) copy-start(bf16[1024,1536]{1,0:T(8,128)(2,1)S(1)} %attend_back.1.g_ref) | copy-start | bytes 9437188
  373.6 4.5 collective-permute-start.5
  378.2 3.3 copy-start.15
  379.0 25.7 %copy-start.8 = (f32[512,2048]{1,0:T(8,128)}, f32[512,2048]{1,0:T(8,128)S(1)}, u32[]{:S(2)}) copy-start(f32[512,2048]{1,0:T(8,128)S(1)} %convert_add_fusion.1) | copy-start | bytes 12582916
  379.0 25.7 %copy-start.22 = (f32[2048]{0:T(1024)S(1)}, f32[2048]{0:T(1024)}, u32[]{:S(2)}) copy-start(f32[2048]{0:T(1024)} %param.19) | copy-start | bytes 24580
  379.2 25.5 %collective-permute-start.6 = (bf16[256,2048]{1,0:T(8,128)(2,1)S(1)}, bf16[256,2048]{1,0:T(8,128)(2,1)S(1)}, u32[]{:S(2)}, u32[]{:S(2)}) collective-permute-start(bf16[256,2048]{1,0:T(8,128)(2,1)S(1)} %slice.119), channel_id=1, source_target_pairs={{0,8},{4,12},{8,0},{12,4},{1,9},{5,13},{9,1},{13,5},{2,10},{6,14},... | collective-permute-start | bytes 3145736 | tf_op jit(solution)/shard_map/ppermute | solution.py:776
  404.7 1.2 copy-start.13
  406.5 224.8 %reduce-scatter.6.cloned.1.call-start = ((), (), s32[]{:S(2)}) async-start(), calls=%async_computation.4 | async-start | bytes 2359296 | tf_op jit(solution)/shard_map/reduce_scatter | solution.py:898
  406.6 6.4 copy-start.4
  412.9 251.5 %reduce-scatter.4.cloned.1.call-start = ((), (), s32[]{:S(2)}) async-start(), calls=%async_computation.3 | async-start | bytes 7077888 | tf_op jit(solution)/shard_map/reduce_scatter | solution.py:898
  424.3 1.2 copy-start.17
  425.5 24.7 %collective-permute-start.1 = (bf16[256,2048]{1,0:T(8,128)(2,1)S(1)}, bf16[256,2048]{1,0:T(8,128)(2,1)S(1)}, u32[]{:S(2)}, u32[]{:S(2)}) collective-permute-start(bf16[256,2048]{1,0:T(8,128)(2,1)S(1)} %copy-done.17), channel_id=1, source_target_pairs={{0,8},{4,12},{8,0},{12,4},{1,9},{5,13},{9,1},{13,5},{2,10},{6,14},... | collective-permute-start | bytes 3145736 | tf_op jit(solution)/shard_map/ppermute | solution.py:776
  430.4 21.3 %copy-start.10 = (f32[1024,1024]{1,0:T(8,128)}, f32[1024,1024]{1,0:T(8,128)S(1)}, u32[]{:S(2)}) copy-start(f32[1024,1024]{1,0:T(8,128)S(1)} %convert_add_fusion) | copy-start | bytes 12582916
  431.7 57.8 %collective-permute-start.10 = (bf16[1024,512]{1,0:T(8,128)(2,1)}, bf16[1024,512]{1,0:T(8,128)(2,1)}, u32[]{:S(2)}, u32[]{:S(2)}) collective-permute-start(bf16[1024,512]{1,0:T(8,128)(2,1)} %slice.118), channel_id=1, source_target_pairs={{0,2},{1,3},{2,0},{3,1},{4,6},{5,7},{6,4},{7,5},{8,10},{9,11},{10,... | collective-permute-start | bytes 3145736 | tf_op jit(solution)/shard_map/ppermute | solution.py:776
  450.2 2.7 copy-start.18
  451.7 46.6 %collective-permute-start.2 = (bf16[512,2048]{1,0:T(8,128)(2,1)}, bf16[512,2048]{1,0:T(8,128)(2,1)}, u32[]{:S(2)}, u32[]{:S(2)}) collective-permute-start(bf16[512,2048]{1,0:T(8,128)(2,1)} %pad_maximum_fusion), channel_id=1, source_target_pairs={{0,4},{4,0},{8,12},{12,8},{1,5},{5,1},{9,13},{13,9},{2,6},{6,2},{1... | collective-permute-start | bytes 6291464 | tf_op jit(solution)/shard_map/ppermute | solution.py:776
  451.8 2.2 copy-start.9
  451.8 2.5 copy-start.14
  451.8 3.2 copy-start.20
  457.1 3.4 copy-start.12
  460.5 34.9 %collective-permute-start.7 = (bf16[256,2048]{1,0:T(8,128)(2,1)S(1)}, bf16[256,2048]{1,0:T(8,128)(2,1)}, u32[]{:S(2)}, u32[]{:S(2)}) collective-permute-start(bf16[256,2048]{1,0:T(8,128)(2,1)S(1)} %get-tuple-element.87), channel_id=1, source_target_pairs={{0,8},{4,12},{8,0},{12,4},{1,9},{5,13},{9,1},{13,5},{2,10},{6,14},... | collective-permute-start | bytes 3145736 | tf_op jit(solution)/shard_map/ppermute | solution.py:776
  462.2 27.2 %copy-start.11 = (f32[1024,1024]{1,0:T(8,128)S(1)}, f32[1024,1024]{1,0:T(8,128)}, u32[]{:S(2)}) copy-start(f32[1024,1024]{1,0:T(8,128)} %copy-done.10) | copy-start | bytes 12582916
  498.3 143.1 %collective-permute-start.8 = (bf16[512,2048]{1,0:T(8,128)(2,1)}, bf16[512,2048]{1,0:T(8,128)(2,1)S(1)}, u32[]{:S(2)}, u32[]{:S(2)}) collective-permute-start(bf16[512,2048]{1,0:T(8,128)(2,1)} %pad_maximum_fusion.3), channel_id=1, source_target_pairs={{0,4},{4,0},{8,12},{12,8},{1,5},{5,1},{9,13},{13,9},{2,6},{6,2},{1... | collective-permute-start | bytes 6291464 | tf_op jit(solution)/shard_map/ppermute | solution.py:776
  505.3 131.0 %collective-permute-start.9 = (bf16[1024,512]{1,0:T(8,128)(2,1)}, bf16[1024,512]{1,0:T(8,128)(2,1)}, u32[]{:S(2)}, u32[]{:S(2)}) collective-permute-start(bf16[1024,512]{1,0:T(8,128)(2,1)} %slice.91), channel_id=1, source_target_pairs={{0,2},{1,3},{2,0},{3,1},{4,6},{5,7},{6,4},{7,5},{8,10},{9,11},{10,... | collective-permute-start | bytes 3145736 | tf_op jit(solution)/shard_map/ppermute | solution.py:776
  633.3 2.9 copy-start.21
Sparse Core Ops, SparseCore 0:
  332.3 56.0 reduce-scatter.7
  413.0 93.9 reduce-scatter.5
  511.0 153.3 reduce-scatter.3
Sparse Core Ops, SparseCore 1:
  406.6 220.5 all-reduce.2

commit v4 on v3

--- a/solution.py
+++ b/solution.py
@@ -66,80 +66,6 @@
     row_at = lax.broadcasted_iota(jnp.int32, (QBLOCK, length), 0) + block * QBLOCK
     allowed = (key_at >= first) & (key_at <= row_at)
     return jnp.where(allowed, scores, NEGATIVE)
-
-
-def attend_back_kernel(
-    q_ref, k_ref, v_ref, go_ref, first_ref, log_ref, cos_ref, sin_ref, g_ref, dk_ref, dv_ref
-):
-    head, step = pl.program_id(0), pl.program_id(1)
-    blocks = pl.num_programs(1)
-    own = q_ref.shape[1] * pl.num_programs(0)
-
-    @pl.when(step == 0)
-    def _():
-        dk_ref[...] = jnp.zeros_like(dk_ref)
-        dv_ref[...] = jnp.zeros_like(dv_ref)
-
-    def place(part):
-        return pl.ds(pl.multiple_of(part * own + head * HEAD_DIM, HEAD_DIM), HEAD_DIM)
-
-    def turn_back(grad, rows):
-        grad = grad.astype(BF16).astype(F32)
-        back = grad * cos_ref[rows] - pltpu.roll(grad, HEAD_DIM // 2, 1) * sin_ref[rows]
-        return back.astype(BF16)
-
-    for block in range(blocks):
-
-        @pl.when(step == block)
-        def _():
-            length = (block + 1) * QBLOCK
-            rows = slice(block * QBLOCK, length)
-            query, keys, grad = q_ref[...], k_ref[:length], go_ref[...]
-            scores = masked_scores(query, keys, first_ref[...], block, length)
-            probs = jnp.exp(scores - log_ref[0])
-            grad_probs = dot(grad, v_ref[:length], NT)
-            inner = jnp.sum(probs * grad_probs, -1, keepdims=True)
-            grad_scores = (probs * (grad_probs - inner)).astype(BF16)
-            dq = dot(grad_scores, keys, NN) * HEAD_DIM**-0.5
-            g_ref[rows, place(0)] = turn_back(dq, rows)
-            dk_ref[:length] += dot(grad_scores, query, TN)
-            dv_ref[:length] += dot(probs.astype(BF16), grad, TN)
-
-    @pl.when(step == blocks - 1)
-    def _():
-        g_ref[:, place(1)] = turn_back(dk_ref[...] * HEAD_DIM**-0.5, slice(None))
-        g_ref[:, place(2)] = dv_ref[...].astype(BF16)
-
-
-def attend_back_call(queries, keys, values, grads, first, logs, cosine, sine):
-    rows, own = queries.shape
-    heads, blocks = own // HEAD_DIM, rows // QBLOCK
-    part = pl.BlockSpec((QBLOCK, HEAD_DIM), lambda h, i: (i, h))
-    whole = pl.BlockSpec((rows, HEAD_DIM), lambda h, i: (0, h))
-    column = pl.BlockSpec((QBLOCK, 1), lambda h, i: (i, 0))
-    table = pl.BlockSpec((rows, HEAD_DIM), lambda h, i: (0, 0))
-    return pl.pallas_call(
-        attend_back_kernel,
-        grid=(heads, blocks),
-        in_specs=[
-            part,
-            whole,
-            whole,
-            part,
-            column,
-            pl.BlockSpec((1, QBLOCK, 1), lambda h, i: (h, i, 0)),
-            table,
-            table,
-        ],
-        out_specs=pl.BlockSpec((rows, 3 * own), lambda h, i: (0, 0)),
-        out_shape=jax.ShapeDtypeStruct((rows, 3 * own), BF16),
-        scratch_shapes=[pltpu.VMEM((rows, HEAD_DIM), F32)] * 2,
-        compiler_params=pltpu.CompilerParams(vmem_limit_bytes=40 << 20),
-        cost_estimate=pl.CostEstimate(
-            flops=10 * rows * rows * own, bytes_accessed=14 * rows * own, transcendentals=heads * rows * rows
-        ),
-        name="attend_back",
-    )(queries, keys, values, grads, first, logs, cosine, sine)
 
 
 class Copies:
@@ -743,32 +669,488 @@
     )(n2, cotangents, *ups, *downs, w_router, levels, middle, *ln2)
 
 
-def qkv_back_kernel(g_ref, w_ref, o_ref):
-    own = w_ref.shape[2]
-    total = dot(g_ref[:, :own], w_ref[0], NT)
-    total += dot(g_ref[:, own : 2 * own], w_ref[1], NT)
-    total += dot(g_ref[:, 2 * own :], w_ref[2], NT)
-    o_ref[...] = total.astype(BF16)
-
-
-def qkv_back_call(grads, w3):
-    rows = grads.shape[0]
-    width, own = w3.shape[1], w3.shape[2]
+def back_kernel(
+    copies,
+    q_ref,
+    k_ref,
+    v_ref,
+    heads_ref,
+    log_ref,
+    first_ref,
+    keep_ref,
+    cos_ref,
+    sin_ref,
+    w_out_ref,
+    w_ref,
+    gain1_ref,
+    tokens_ref,
+    gx2_ref,
+    small_in_ref,
+    ga_in_ref,
+    mixed_in_ref,
+    n1_ref,
+    down_ref,
+    got_down_ref,
+    up_ref,
+    sums_ref,
+    small_ref,
+    mixed_ref,
+    tg_ref,
+    down_own_ref,
+    down_got_ref,
+    up_own_ref,
+    up_got_ref,
+    got_up_ref,
+    leave_ref,
+    ga_ref,
+    go_ref,
+    gp_ref,
+    dk_ref,
+    dv_ref,
+    got_core_ref,
+    got_y_ref,
+    part_ref,
+    tg_own_ref,
+    tile_in,
+    tile_out,
+    fold_a,
+    fold_b,
+    fold_send,
+    fold_out,
+    kept_ref,
+    got_x_ref,
+    z_send,
+    z_kept,
+    got_z1,
+    got_z2,
+    got_small,
+    small_send,
+    send_sems,
+    recv_sems,
+    local_sems,
+    tile_sems,
+    tile_out_sems,
+    fold_sems,
+    fold_out_sems,
+):
+    t, z, x = lax.axis_index("tensor"), lax.axis_index("bucket"), lax.axis_index("dp")
+    rows, own = q_ref.shape
+    splits, share, width = ga_ref.shape
+    heads, blocks = own // HEAD_DIM, rows // QBLOCK
+    reach = width // copies
+    part = got_z2.shape[1]
+    core, y_side = {"tensor": t ^ 1}, {"tensor": t ^ 2}
+    near, far = {"bucket": z ^ 1}, {"bucket": z ^ 2}
+    twins = [{"dp": lax.rem(x + d, copies)} for d in range(1, copies)]
+    meet([core, y_side, near, far] + twins)
+    links = Copies(send_sems, recv_sems)
+    begun = []
+
+    def send(source, target, device):
+        copy = links.start(source, target, device)
+        begun.append(copy)
+        return copy
+
+    def span(start, size):
+        return pl.ds(pl.multiple_of(start, size), size)
+
+    ga_y = send(ga_in_ref, ga_ref.at[t], y_side)
+    ga_core = send(ga_in_ref, ga_ref.at[t], core)
+    ga_own = pltpu.make_async_copy(ga_in_ref, ga_ref.at[t], local_sems.at[0])
+    ga_own.start()
+    ups = [
+        send(up_ref.at[span(lax.rem(x + d, copies) * reach, reach)], got_up_ref.at[d - 1], twins[d - 1])
+        for d in range(1, copies)
+    ]
+    mixed_y = send(mixed_in_ref, mixed_ref.at[t], y_side)
+    mixed_core = send(mixed_in_ref, mixed_ref.at[t], core)
+    mixed_own = pltpu.make_async_copy(mixed_in_ref, mixed_ref.at[t], local_sems.at[1])
+    mixed_own.start()
+
+    few = fold_a.shape[1]
+    half = fold_out.shape[2]
+
+    def fold(which, source_ref, got_ref, own_ref, target_ref):
+        def loads(k, slot):
+            mine = pltpu.make_async_copy(
+                source_ref.at[span(x * reach + k * few, few)], fold_a.at[slot], fold_sems.at[0, slot]
+            )
+            theirs = [
+                pltpu.make_async_copy(
+                    got_ref.at[d, span(k * few, few)], fold_b.at[slot, d], fold_sems.at[1 + d, slot]
+                )
+                for d in range(copies - 1)
+            ]
+            return [mine] + theirs
+
+        def put(k, slot):
+            return pltpu.make_async_copy(
+                fold_out.at[slot], own_ref.at[span(k * few, few)], fold_out_sems.at[slot]
+            )
+
+        for copy in loads(0, 0):
+            copy.start()
+        steps = reach // few
+
+        def step(k, carry):
+            slot = k % 2
+            for copy in loads(k, slot):
+                copy.wait()
+
+            @pl.when(k < steps - 1)
+            def _():
+                for copy in loads(k + 1, 1 - slot):
+                    copy.start()
+
+            @pl.when(k >= 2)
+            def _():
+                put(k - 2, slot).wait()
+
+            total = fold_a[slot].astype(F32)
+            for d in range(copies - 1):
+                total += fold_b[slot, d].astype(F32)
+            fold_out[slot] = total[:, :half]
+            fold_send[which, span(k * few, few), :] = total[:, half:].astype(BF16)
+            put(k, slot).start()
+            return carry
+
+        lax.fori_loop(0, steps, step, 0)
+        for k in range(max(0, steps - 2), steps):
+            put(k, k % 2).wait()
+        return send(fold_send.at[which], target_ref, far)
+
+    down_far = fold(0, down_ref, got_down_ref, down_own_ref, down_got_ref)
+
+    def grad_heads(s):
+        at = span(s * share, share)
+        grad = dot(ga_ref[s], w_out_ref[...], NT).astype(BF16).astype(F32)
+        go_ref[at, :] = (grad * keep_ref[at, :]).astype(BF16)
+
+    ga_own.wait()
+    grad_heads(t)
+    ga_core.wait_recv()
+    grad_heads(t ^ 1)
+    ga_y.wait_recv()
+    ga_y_core = send(ga_ref.at[t ^ 2], ga_ref.at[t ^ 2], core)
+    grad_heads(t ^ 2)
+    ga_y_core.wait_recv()
+    grad_heads(t ^ 3)
+
+    tile = tile_in.shape[-1]
+    per = reach // tile
+
+    def put_tile(slot, place, chunk, count):
+        d, k = place
+        return pltpu.make_async_copy(
+            tile_out.at[slot, pl.ds(0, count)],
+            leave_ref.at[d, pl.ds(chunk, count), span(k * tile, tile)],
+            tile_out_sems.at[slot],
+        )
+
+    def store_tile(index, total, chunk, count):
+        slot = index % 2
+        d, k = index // per, index % per
+        leaving = index < per * (copies - 1)
+
+        @pl.when(leaving)
+        def _():
+            @pl.when(index >= 2)
+            def _():
+                put_tile(slot, ((index - 2) // per, (index - 2) % per), chunk, count).wait()
+
+            for c in range(count):
+                tile_out[slot, c] = total[:, c * own : (c + 1) * own].astype(BF16)
+            put_tile(slot, (d, k), chunk, count).start()
+
+        @pl.when(jnp.logical_not(leaving))
+        def _():
+            for c in range(count):
+                kept_ref[chunk + c, span(k * tile, tile), :] = total[
+                    :, c * own : (c + 1) * own
+                ].astype(BF16)
+
+    def tile_row(index):
+        return lax.rem(x + 1 + index // per, copies) * per + index % per
+
+    last = per * (copies - 1)
+
+    def settle(chunk, count):
+        for index in range(max(0, last - 2), last):
+            put_tile(index % 2, (index // per, index % per), chunk, count).wait()
+        return [
+            [
+                send(leave_ref.at[d - 1, chunk + c], got_x_ref.at[d - 1, chunk + c], twins[d - 1])
+                for d in range(1, copies)
+            ]
+            for c in range(count)
+        ]
+
+    def out_tile(index, carry):
+        lanes = span(tile_row(index) * tile, tile)
+        left = ga_ref[:, :, lanes].reshape(rows, tile)
+        store_tile(index, dot(left, heads_ref[...], TN), 0, 1)
+        return carry
+
+    lax.fori_loop(0, last, out_tile, 0)
+    crossing = settle(0, 1)
+    lax.fori_loop(last, last + per, out_tile, 0)
+
+    def turn_back(grad, at):
+        grad = grad.astype(BF16).astype(F32)
+        back = grad * cos_ref[at] - pltpu.roll(grad, HEAD_DIM // 2, 1) * sin_ref[at]
+        return back.astype(BF16)
+
+    for head in range(heads):
+        lanes = slice(head * HEAD_DIM, (head + 1) * HEAD_DIM)
+        for block in reversed(range(blocks)):
+            length = (block + 1) * QBLOCK
+            at = slice(block * QBLOCK, length)
+            query, keys, grad = q_ref[at, lanes], k_ref[:length, lanes], go_ref[at, lanes]
+            scores = masked_scores(query, keys, first_ref[at], block, length)
+            probs = jnp.exp(scores - log_ref[at, head : head + 1])
+            grad_probs = dot(grad, v_ref[:length, lanes], NT)
+            inner = jnp.sum(probs * grad_probs, -1, keepdims=True)
+            grad_scores = (probs * (grad_probs - inner)).astype(BF16)
+            dq = dot(grad_scores, keys, NN) * HEAD_DIM**-0.5
+            gp_ref[at, lanes] = turn_back(dq, at)
+            dk = dot(grad_scores, query, TN)
+            dv = dot(probs.astype(BF16), grad, TN)
+            if block == blocks - 1:
+                dk_ref[...] = dk
+                dv_ref[...] = dv
+            else:
+                dk_ref[:length] += dk
+                dv_ref[:length] += dv
+        gp_ref[:, own + head * HEAD_DIM : own + (head + 1) * HEAD_DIM] = turn_back(
+            dk_ref[...] * HEAD_DIM**-0.5, slice(None)
+        )
+        gp_ref[:, 2 * own + head * HEAD_DIM : 2 * own + (head + 1) * HEAD_DIM] = dv_ref[
+            ...
+        ].astype(BF16)
+
+    ga_y.wait_send()
+    ga_y_core.wait_send()
+
+    def norm1_part(s):
+        at = span(s * share, share)
+        for lanes in (slice(0, width // 2), slice(width // 2, width)):
+            total = dot(gp_ref[at, :own], w_ref[0, lanes, :], NT)
+            total += dot(gp_ref[at, own : 2 * own], w_ref[1, lanes, :], NT)
+            total += dot(gp_ref[at, 2 * own :], w_ref[2, lanes, :], NT)
+            part_ref[:, lanes] = total
+
+    norm1_part(t ^ 3)
+    ga_ref[0] = part_ref[...].astype(BF16)
+    core_pass = send(ga_ref.at[0], got_core_ref.at[0], core)
+    norm1_part(t ^ 1)
+    ga_ref[1] = part_ref[...].astype(BF16)
+    core_own = send(ga_ref.at[1], got_core_ref.at[1], core)
+    norm1_part(t ^ 2)
+    core_pass.wait_recv()
+    ga_ref[2] = (part_ref[...] + got_core_ref[0].astype(F32)).astype(BF16)
+    y_own = send(ga_ref.at[2], got_y_ref, y_side)
+    norm1_part(t)
+
+    mixed_y.wait_recv()
+    mixed_y_core = send(mixed_ref.at[t ^ 2], mixed_ref.at[t ^ 2], core)
+
+    def fetch(index, slot):
+        lanes = span(tile_row(index) * tile, tile)
+        return pltpu.make_async_copy(n1_ref.at[:, lanes], tile_in.at[slot], tile_sems.at[slot])
+
+    fetch(0, 0).start()
+
+    def qkv_tile(index, carry):
+        slot = index % 2
+        fetch(index, slot).wait()
+
+        @pl.when(index < last + per - 1)
+        def _():
+            fetch(index + 1, 1 - slot).start()
+
+        store_tile(index, dot(tile_in[slot], gp_ref[...], TN), 1, 3)
+        return carry
+
+    lax.fori_loop(0, last, qkv_tile, 0)
+    crossing += settle(1, 3)
+    lax.fori_loop(last, last + per, qkv_tile, 0)
+
+    for copy in ups:
+        copy.wait_recv()
+    up_far = fold(1, up_ref, got_up_ref, up_own_ref, up_got_ref)
+
+    def first_step(chunk):
+        for copy in crossing[chunk]:
+            copy.wait_recv()
+
+        def total(index):
+            at = span(index * part, part)
+            value = kept_ref[chunk, at, :].astype(F32)
+            for d in range(copies - 1):
+                value += got_x_ref[d, chunk, at, :].astype(F32)
+            return value
+
+        z_send[chunk, 1] = total(z ^ 3).astype(BF16)
+        one = send(z_send.at[chunk, 1], got_z1.at[chunk, 1], near)
+        z_send[chunk, 0] = total(z ^ 1).astype(BF16)
+        two = send(z_send.at[chunk, 0], got_z1.at[chunk, 0], near)
+        z_kept[chunk] = total(z ^ 2)
+        sums_ref[chunk] = total(z)
+        return one, two
+
+    def second_step(chunk, pair):
+        one, two = pair
+        one.wait_recv()
+        one.wait_send()
+        begun[:] = [copy for copy in begun if copy is not one]
+        z_send[chunk, 1] = (z_kept[chunk] + got_z1[chunk, 1].astype(F32)).astype(BF16)
+        gone = send(z_send.at[chunk, 1], got_z2.at[chunk], far)
+        two.wait_recv()
+        sums_ref[chunk] += got_z1[chunk, 0].astype(F32)
+        return gone
+
+    def third_step(chunk, gone):
+        gone.wait_recv()
+        sums_ref[chunk] += got_z2[chunk].astype(F32)
+
+    core_own.wait_recv()
+    y_own.wait_recv()
+    small_ref[...] = small_in_ref[...]
+    lines = 64
+    count = small_in_ref.shape[0] - 2
+
+    def finish(j, carry):
+        at = span(j * lines, lines)
+        grad = part_ref[at, :] + got_core_ref[1, at, :].astype(F32) + got_y_ref[at, :].astype(F32)
+        hat, inverse = norm_parts(tokens_ref[at, :].astype(F32))
+        back, gain_grad, bias_grad = norm_backward(grad, hat, inverse, gain1_ref[...])
+        tg_own_ref[at, :] = (gx2_ref[at, :] + back).astype(BF16)
+        small_ref[count : count + 1, :] += gain_grad[None, :]
+        small_ref[count + 1 : count + 2, :] += bias_grad[None, :]
+        return carry
+
+    lax.fori_loop(0, share // lines, finish, 0)
+    tg_y = send(tg_own_ref, tg_ref.at[t], y_side)
+    tg_core = send(tg_own_ref, tg_ref.at[t], core)
+    tg_own = pltpu.make_async_copy(tg_own_ref, tg_ref.at[t], local_sems.at[2])
+    tg_own.start()
+
+    for step, devices in enumerate(([core], [y_side], [near], [far], twins)):
+        small_send[step] = small_ref[...]
+        exchanged = [
+            send(small_send.at[step], got_small.at[step + d], device)
+            for d, device in enumerate(devices)
+        ]
+        for d, copy in enumerate(exchanged):
+            copy.wait_recv()
+            small_ref[...] += got_small[step + d]
+        if step == 1:
+            out_first = first_step(0)
+        if step == 3:
+            out_second = second_step(0, out_first)
+
+    tg_y.wait_recv()
+    tg_y_core = send(tg_ref.at[t ^ 2], tg_ref.at[t ^ 2], core)
+    firsts = {1: first_step(1)}
+    third_step(0, out_second)
+    firsts[2] = first_step(2)
+    seconds = {1: second_step(1, firsts[1])}
+    firsts[3] = first_step(3)
+    seconds[2] = second_step(2, firsts[2])
+    third_step(1, seconds[1])
+    seconds[3] = second_step(3, firsts[3])
+    third_step(2, seconds[2])
+    third_step(3, seconds[3])
+    for copy in (core_own, mixed_core, mixed_y_core, tg_core, tg_y_core, down_far, up_far):
+        if copy is not core_own:
+            copy.wait_recv()
+    for copy in (mixed_own, tg_own):
+        copy.wait()
+    for copy in begun:
+        if copy is not ga_y and copy is not ga_y_core:
+            copy.wait_send()
+
+
+def back_call(
+    queries, keys, values, heads, logs, first, keep, tables_, w_out, w3, gain1, tokens_own,
+    grad_middle, small, grad_own, mixed_own, normed1, down_part, got_down, up_part,
+):
+    rows, own = queries.shape
+    share, width = grad_own.shape
+    copies, owners = lax.axis_size("dp"), lax.axis_size("bucket")
+    splits = rows // share
+    reach = width // copies
+    part = reach // owners
+    half = down_part.shape[1] // 2
+    inside = pl.BlockSpec(memory_space=pltpu.VMEM)
+    outside = pl.BlockSpec(memory_space=pl.ANY)
+    shape = jax.ShapeDtypeStruct
+    dma = lambda *count: pltpu.SemaphoreType.DMA(count)
+    vmem = lambda dtype, *size: pltpu.VMEM(size, dtype)
+    others = copies - 1
+    few = 128
+    sends = 3 + 3 + 3 + 2 + 3 + 12 + 4 + 6 * others
     return pl.pallas_call(
-        qkv_back_kernel,
-        grid=(rows // QBLOCK,),
-        in_specs=[
-            pl.BlockSpec((QBLOCK, 3 * own), lambda i: (i, 0)),
-            pl.BlockSpec(w3.shape, lambda i: (0, 0, 0)),
+        functools.partial(back_kernel, copies),
+        in_specs=[inside] * 15 + [outside] * 6,
+        out_specs=[inside] * 2 + [outside] * 8,
+        out_shape=[
+            shape((4, part, own), F32),
+            shape(small.shape, F32),
+            shape((splits, share, width), BF16),
+            shape((splits, share, width), BF16),
+            shape((reach, half), F32),
+            shape((reach, half), BF16),
+            shape((reach, half), F32),
+            shape((reach, half), BF16),
+            shape((others, reach, 2 * half), BF16),
+            shape((others, 4, reach, own), BF16),
         ],
-        out_specs=pl.BlockSpec((QBLOCK, width), lambda i: (i, 0)),
-        out_shape=jax.ShapeDtypeStruct((rows, width), BF16),
-        compiler_params=pltpu.CompilerParams(vmem_limit_bytes=40 << 20),
+        scratch_shapes=[
+            vmem(BF16, splits, share, width),
+            vmem(BF16, rows, own),
+            vmem(BF16, rows, 3 * own),
+            vmem(F32, rows, HEAD_DIM),
+            vmem(F32, rows, HEAD_DIM),
+            vmem(BF16, 2, share, width),
+            vmem(BF16, share, width),
+            vmem(F32, share, width),
+            vmem(BF16, share, width),
+            vmem(BF16, 2, rows, 256),
+            vmem(BF16, 2, 3, 256, own),
+            vmem(BF16, 2, few, 2 * half),
+            vmem(BF16, 2, others, few, 2 * half),
+            vmem(BF16, 2, reach, half),
+            vmem(F32, 2, few, half),
+            vmem(BF16, 4, reach, own),
+            vmem(BF16, others, 4, reach, own),
+            vmem(BF16, 4, 2, part, own),
+            vmem(F32, 4, part, own),
+            vmem(BF16, 4, 2, part, own),
+            vmem(BF16, 4, part, own),
+            vmem(F32, 4 + others, *small.shape),
+            vmem(F32, 5, *small.shape),
+            dma(sends),
+            dma(sends),
+            dma(3),
+            dma(2),
+            dma(2),
+            dma(copies, 2),
+            dma(2),
+        ],
+        compiler_params=pltpu.CompilerParams(
+            vmem_limit_bytes=62 << 20, collective_id=2, has_side_effects=True
+        ),
         cost_estimate=pl.CostEstimate(
-            flops=6 * rows * width * own, bytes_accessed=2 * (rows * width + 3 * width * own + 3 * rows * own), transcendentals=0
+            flops=16 * rows * width * own + 10 * rows * rows * own,
+            bytes_accessed=80 << 20,
+            transcendentals=rows * rows * own // HEAD_DIM,
         ),
-        name="qkv_back",
-    )(grads, w3)
+        name="back",
+    )(
+        queries, keys, values, heads, logs, first, keep, *tables_, w_out, w3, gain1, tokens_own,
+        grad_middle, small, grad_own, mixed_own, normed1, down_part, got_down, up_part,
+    )
 
 
 def swap(values, axis, bit):
@@ -807,8 +1189,6 @@
 
     def shard(values, bit):
         return lax.dynamic_slice_in_dim(values, (t ^ bit) * share, share, 0)
-
-    ORDER = (0, 2, 1, 3)
 
     positions, first = layout(lengths[0], tok_rows)
     first = first[:, None]
@@ -840,7 +1220,6 @@
         down_own,
         cotangent,
     )
-    logs = logs.T[:, :, None]
     level_all = jnp.concatenate([levels.reshape(-1), near_levels.reshape(-1)], 0)[:, None]
     (
         mixed_own,
@@ -861,76 +1240,42 @@
         middle,
         (ln2_gain.reshape(1, -1), ln2_bias.reshape(1, -1)),
     )
-    inputs_own = shard(tokens, 0).astype(F32)
-
-    def gather_sum(away, kept):
-        both = kept + swap(away.astype(BF16), "tensor", 1).astype(F32)
-        half = both.shape[0] // 2
-        return both[:half] + swap(both[half:].astype(BF16), "tensor", 2).astype(F32)
-
-    def spread(piece):
-        both = jnp.concatenate([piece, swap(piece, "tensor", 2)], 0)
-        return jnp.concatenate([both, swap(both, "tensor", 1)], 0)
-
-    def natural(piece, dtype):
-        whole = jnp.zeros((tok_rows, model_width), dtype)
-        for at, bit in enumerate(ORDER):
-            part = lax.slice_in_dim(piece, at * share, (at + 1) * share).astype(dtype)
-            whole = lax.dynamic_update_slice_in_dim(whole, part, (t ^ bit) * share, 0)
-        return whole
-
-    size = model_width // copies
-    down_sum = lax.dynamic_slice_in_dim(down_part, x * size, size, 0).astype(F32)
-    down_sum += jnp.sum(got_down.astype(F32), 0)
-    up_sum = lax.psum_scatter(up_part, "dp", scatter_dimension=0, tiled=True).astype(F32)
-
-    def owner_sum(total):
-        return total[:, :hidden_width] + swap(
-            total[:, hidden_width:].astype(BF16), "bucket", 2
-        ).astype(F32)
-
-    grad_down = owner_sum(down_sum).T
-    grad_up = owner_sum(up_sum)
-    mixed = natural(spread(mixed_own), BF16)
-    grad_attention = natural(spread(grad_attention_own), BF16)
-
-    def reduce_all(grad):
-        return lax.psum_scatter(
-            grad.astype(BF16), ("dp", "bucket"), scatter_dimension=0, tiled=True
-        ).astype(F32)
-
-    grad_w_out = reduce_all(dot(grad_attention, heads_low, TN)).T
-    grad_heads = (dot(grad_attention, w_out, NT).astype(BF16).astype(F32) * keep).astype(BF16)
-    grad_projected = attend_back_call(
-        queries, keys, values, grad_heads, first, logs, cosine, sine
+    sums, small, mixed, tokens_grad, down_own, down_got, up_own, up_got, _, _ = back_call(
+        queries,
+        keys,
+        values,
+        heads_low,
+        logs,
+        first,
+        keep,
+        (cosine, sine),
+        w_out,
+        w3,
+        ln1_gain.reshape(1, -1),
+        shard(tokens, 0),
+        grad_middle,
+        jnp.concatenate([small, jnp.zeros((2, model_width), F32)], 0),
+        grad_attention_own,
+        mixed_own,
+        normed1,
+        down_part,
+        got_down,
+        up_part,
     )
-    partial = qkv_back_call(grad_projected, w3)
-    grad_w_qkv = reduce_all(dot(normed1, grad_projected, TN)).reshape(-1, 3, w3.shape[2])
-    away = jnp.concatenate([shard(partial, 1), shard(partial, 3)], 0)
-    kept = jnp.concatenate([shard(partial, 0), shard(partial, 2)], 0).astype(F32)
-    grad_norm1 = gather_sum(away, kept)
-    hat1, inverse1 = norm_parts(inputs_own)
-    grad_in1, grad_ln1_gain, grad_ln1_bias = norm_backward(grad_norm1, hat1, inverse1, ln1_gain)
-    tokens_grad = natural(spread((grad_middle + grad_in1).astype(BF16)), F32)
-
-    def reduce_small(*grads):
-        stacked = jnp.stack(grads, 0)
-        total = lax.psum(stacked, ("dp", "tensor", "bucket"))
-        width = model_width // (copies * owners)
-        return lax.dynamic_slice_in_dim(total, (x * owners + z) * width, width, 1)
-
-    small = reduce_small(*(small[i] for i in range(2 + owners)))
-    last = reduce_small(grad_ln1_gain, grad_ln1_bias)
+    grad_down = (down_own + down_got.astype(F32)).T
+    grad_up = up_own + up_got.astype(F32)
+    width = model_width // (copies * owners)
+    small = lax.dynamic_slice_in_dim(small, (x * owners + z) * width, width, 1)
     return (
-        mixed,
-        tokens_grad,
-        last[0],
-        last[1],
-        grad_w_qkv,
-        grad_w_out,
+        mixed.reshape(tok_rows, model_width),
+        tokens_grad.reshape(tok_rows, model_width).astype(F32),
+        small[2 + owners],
+        small[3 + owners],
+        jnp.transpose(sums[1:], (1, 0, 2)),
+        sums[0].T,
         small[0],
         small[1],
-        small[2:].T,
+        small[2 : 2 + owners].T,
         grad_up.reshape(-1, 1, hidden_width),
         grad_down.reshape(1, hidden_width, -1),
     )

time: 680 us -> 546 us (0.80)
  waiting for transfers between devices: 228 us -> 0.01 us
  Pallas kernels: 306 us -> 496 us
  local copies, waits for them, and re-layouts: 55.5 us -> 26.3 us
  matrix products: 20 us -> 0 us
  other arithmetic: 32.4 us -> 13.5 us
  between operations: 16 us -> 1.04 us
  starting transfers between devices: 16.8 us -> 3.02 us
    pallas_call x2 -> x1, Pallas kernels: 23.8 us -> 214 us  [back_call(): pl.pallas_call(functools.partial(back_kernel, copies), in_specs=[inside]...]
    psum x1 -> x0, waiting for transfers between devices: 122 us -> none  [reduce_small(): total = lax.psum(stacked, ('dp', 'tensor', 'bucket'))]
    ppermute x11 -> x1, waiting for transfers between devices: 86.3 us -> 0.01 us  [swap(): return lax.ppermute(values, axis, pairs)]
    reduce_scatter x3 -> x0, waiting for transfers between devices: 20 us -> none  [the longest x2 20 us: reduce_all(): lax.psum_scatter(grad.astype(BF16), ('dp', 'bucket'), scatter_dimension=0...]
    dot_general x3 -> x0, matrix products: 20 us -> none  [dot(): lax.dot_general(left, right, (dims, ((), ())), preferred_element_type=F32)]
    ppermute x11 -> x1, starting transfers between devices: 16.6 us -> 3.02 us  [swap(): return lax.ppermute(values, axis, pairs)]
    dynamic_update_slice x8 -> x0, local copies, waits for them, and re-layouts: 11 us -> none  [natural(): whole = lax.dynamic_update_slice_in_dim(whole, part, (t ^ bit) * share, 0)]
    broadcast_in_dim x2 -> x0, local copies, waits for them, and re-layouts: 9.53 us -> none  [the longest x1 8.5 us: local(): logs = logs.T[:, :, None]]
  transfers between devices with their start and end apart: 15 -> 1, of which waited for: 7 -> 0; matrix products, arithmetic and copies ran while one was open for 13% -> 2% of each run, Pallas kernels for 29% -> 32%
where the time goes in v4:
time: 546 us; the launch traced here: 540 us
  Pallas kernels  496 us (91%)
  local copies, waits for them, and re-layouts  26.3 us (5%)
  other arithmetic  13.5 us (2%)
    pallas_call x1, Pallas kernels, back_call(): pl.pallas_call(functools.partial(back_kernel, copies), in_specs=[inside]...  214 us
    pallas_call x1, Pallas kernels, front_call(): pl.pallas_call(functools.partial(front_kernel, copies), in_specs=[inside]...  173 us
    pallas_call x1, Pallas kernels, middle_call(): pl.pallas_call(functools.partial(middle_kernel, copies), in_specs=[outsid...  109 us
    unnamed x13, local copies, waits for them, and re-layouts  12.4 us
  transfers between devices with their start and end apart: 1, of which 0 were waited for; matrix products, arithmetic and copies ran while one was open for 2% of the time, Pallas kernels for 32%

profile of v4, /device:TPU:0, one launch (start us, length us, event | category | flops | bytes accessed | tf_op | source)
XLA Modules:
  0.0 540.3 jit_solution(16271087420609985627)
XLA Ops:
  0.6 0.7 convert_element_type.35
  1.3 3.0 collective-permute-start
  4.4 0.8 reduce-window.4
  5.2 0.7 fusion.1
  5.9 0.1 convert_reduce_fusion
  5.9 0.1 select_reduce_fusion
  6.0 1.0 copy.38.first_ref
  7.1 0.7 compare_convert_fusion
  7.8 1.0 copy.39.keep_ref
  8.8 1.9 fusion
  10.7 1.3 pad_maximum_fusion
  12.0 173.4 %front.1 = (bf16[1024,2048]{1,0:T(8,128)(2,1)}, bf16[1024,512]{1,0:T(8,128)(2,1)}, bf16[1024,512]{1,0:T(8,128)(2,1)}, bf16[1024,512]{1,0:T(8,128)(2,1)}, bf16[10...) custom-call(bf16[1024,2048]{1,0:T(8,128)(2,1)} %tokens_ref.1, ...), custom_call_target="tpu_custom_call" | custom-call | flops 10737418240 | bytes 62914560 | tf_op jit(solution)/shard_map/front/pallas_call | solution.py:267
  185.4 0.0 copy-start.3
  185.4 2.3 constant_dynamic-slice_fusion.1.tokens_ref
  187.7 0.0 copy-done.3
  187.7 1.1 copy.40.router_ref
  188.8 0.0 collective-permute-done
  188.8 1.3 copy.41.level_ref
  190.1 108.7 %middle.1 = (bf16[256,2048]{1,0:T(8,128)(2,1)}, f32[256,2048]{1,0:T(8,128)}, bf16[256,2048]{1,0:T(8,128)(2,1)}, f32[6,2048]{1,0:T(8,128)}, bf16[2,4,256,2048]{3,...) custom-call(bf16[2,4,256,2048]{3,2,1,0:T(8,128)(2,1)} %get-tuple-element, ...), custom_call_target="tpu_custom_call" | custom-call | flops 51539607552 | bytes 83886080 | tf_op jit(solution)/shard_map/middle/pallas_call | solution.py:621
  298.8 1.5 concatenate.15.small_in_ref
  300.3 214.3 %back.1 = (f32[4,256,512]{2,1,0:T(8,128)}, f32[8,2048]{1,0:T(8,128)}, bf16[4,256,2048]{2,1,0:T(8,128)(2,1)}, bf16[4,256,2048]{2,1,0:T(8,128)(2,1)}, f32[1024,512...) custom-call(bf16[1024,512]{1,0:T(8,128)(2,1)} %get-tuple-element.37., ...), custom_call_target="tpu_custom_call" | custom-call | flops 22548578304 | bytes 83886080 | tf_op jit(solution)/shard_map/back/pallas_call | solution.py:1093
  514.6 0.0 copy-start.1
  514.6 0.0 copy-start.2
  514.6 2.8 slice_bitcast_fusion
  517.5 1.1 slice_bitcast_fusion.1
  518.5 0.0 copy-done.1
  518.6 0.0 copy-done.2
  518.6 0.3 add_bitcast_fusion
  518.9 2.0 copy.46
  520.9 2.2 add_bitcast_fusion.1
  523.1 0.0 copy-start
  523.1 3.5 copy.45
  526.6 0.0 copy-done
  526.6 4.7 bitcast_convert_fusion
  531.3 1.0 copy.44
  532.3 1.4 dynamic-slice_bitcast_fusion
  533.7 1.5 fusion.2
  535.2 4.8 copy.48
  (3 shorter events, 0.0 us)
Async XLA Ops:
  1.3 187.4 %collective-permute-start = (f32[8,128]{1,0:T(8,128)S(1)}, f32[8,128]{1,0:T(8,128)S(1)}, u32[]{:S(2)}, u32[]{:S(2)}) collective-permute-start(f32[8,128]{1,0:T(8,128)S(1)} %bitcast.47), channel_id=1, source_target_pairs={{0,1},{1,0},{2,3},{3,2},{4,5},{5,4},{6,7},{7,6},{8,9},{9,8},{10,11... | collective-permute-start | bytes 12296 | tf_op jit(solution)/shard_map/ppermute | solution.py:1158
  185.4 2.3 copy-start.3
  514.6 3.9 copy-start.1
  514.6 3.9 copy-start.2
  523.1 3.5 copy-start

commit v5 on v4

--- a/solution.py
+++ b/solution.py
@@ -39,16 +39,7 @@
     tok_index = jnp.arange(tok_rows, dtype=jnp.int32)
     segments = jnp.sum((tok_index[:, None] >= ends[None, :]).astype(jnp.int32), 1)
     chosen = segments[:, None] == jnp.arange(lengths_row.shape[0], dtype=jnp.int32)[None, :]
-    first = jnp.sum(jnp.where(chosen, starts[None, :], 0), 1)
-    return tok_index - first, first
-
-
-def tables(positions):
-    half_dim = HEAD_DIM // 2
-    freq = jnp.exp(jnp.arange(half_dim, dtype=F32) * (-math.log(10000.0) / half_dim))
-    angle = positions.astype(F32)[:, None] * freq[None, :]
-    cosine, sine = jnp.cos(angle), jnp.sin(angle)
-    return jnp.concatenate([cosine, cosine], -1), jnp.concatenate([-sine, sine], -1)
+    return jnp.sum(jnp.where(chosen, starts[None, :], 0), 1)
 
 
 def dot(left, right, dims):
@@ -99,31 +90,41 @@
 
 def front_kernel(
     copies,
-    tokens_ref,
     gain1_ref,
     bias1_ref,
-    w_ref,
-    cos_ref,
-    sin_ref,
     first_ref,
     keep_ref,
-    w_out_ref,
     gain2_ref,
     bias2_ref,
+    tokens_in,
+    w_in,
+    w_out_in,
     up_ref,
     down_ref,
     cot_ref,
+    level_ref,
+    log_ref,
+    middle_ref,
+    cos_ref,
+    sin_ref,
+    n1_out,
+    q_out,
+    k_out,
+    v_out,
+    heads_out,
+    n2_ref,
+    up_other_ref,
+    down_other_ref,
+    near_cot_ref,
+    near_level_ref,
+    tokens_ref,
+    w_ref,
+    w_out_ref,
     n1_ref,
     q_ref,
     k_ref,
     v_ref,
     heads_ref,
-    log_ref,
-    middle_ref,
-    n2_ref,
-    up_other_ref,
-    down_other_ref,
-    cots_ref,
     away_ref,
     got_core_ref,
     pass_ref,
@@ -131,58 +132,116 @@
     own_ref,
     send_sems,
     recv_sems,
-    local_sem,
-    local_sems,
+    in_sems,
+    out_sems,
 ):
     t, z, x = lax.axis_index("tensor"), lax.axis_index("bucket"), lax.axis_index("dp")
     rows, own = q_ref.shape
     share = own_ref.shape[0]
     heads = own // HEAD_DIM
+    blocks = rows // QBLOCK
     core, y_side = {"tensor": t ^ 1}, {"tensor": t ^ 2}
     near, far = {"bucket": z ^ 1}, {"bucket": z ^ 2}
     twins = [{"dp": lax.rem(x + d, copies)} for d in range(1, copies)]
+
+    def token_block(i):
+        at = pl.ds(pl.multiple_of(i * QBLOCK, QBLOCK), QBLOCK)
+        return pltpu.make_async_copy(tokens_in.at[at], tokens_ref.at[at], in_sems.at[i])
+
+    w_copies = [
+        pltpu.make_async_copy(w_in.at[part], w_ref.at[part], in_sems.at[blocks + part])
+        for part in range(3)
+    ]
+    w_out_copy = pltpu.make_async_copy(w_out_in, w_out_ref, in_sems.at[blocks + 3])
+    token_block(0).start()
+    for copy in w_copies:
+        copy.start()
+    for i in range(1, blocks):
+        token_block(i).start()
+    w_out_copy.start()
+
     meet([core, y_side, near, far] + twins)
     links = Copies(send_sems, recv_sems)
-
-    def piece(ref, of):
-        size = ref.shape[0] // copies
-        return ref.at[pl.ds(pl.multiple_of(of * size, 16), size)]
-
-    def shard(ref, index):
-        return ref.at[pl.ds(pl.multiple_of(index * share, share), share)]
-
-    up_piece = links.start(piece(up_ref, x), piece(up_other_ref, x), far)
-    parity = lax.rem(t, 2)
-    keep_cots = [
-        pltpu.make_async_copy(shard(cot_ref, i), cots_ref.at[0, i], local_sems.at[i])
-        for i in range(cots_ref.shape[1])
+    begun = []
+
+    def send(source, target, device):
+        copy = links.start(source, target, device)
+        begun.append(copy)
+        return copy
+
+    def piece(ref, quarter):
+        size = ref.shape[0] // copies // 4
+        return ref.at[pl.ds(pl.multiple_of((x * 4 + quarter) * size, 16), size)]
+
+    def fetch(ref, other_ref, quarter):
+        return send(piece(ref, quarter), piece(other_ref, quarter), far)
+
+    onward = []
+
+    def pass_on(copy, ref, devices):
+        copy.wait_recv()
+        onward.extend(send(ref, ref, device) for device in devices)
+
+    few = share // 4
+
+    def cot_rows(ref, s, chunk):
+        return ref.at[s, pl.ds(chunk * few, few)]
+
+    cots = [
+        send(cot_rows(cot_ref, t, chunk), cot_rows(near_cot_ref, t, chunk), near)
+        for chunk in range(4)
     ]
-    for copy in keep_cots:
-        copy.start()
-    cots = [
-        links.start(shard(cot_ref, parity + i), cots_ref.at[1, parity + i], near)
-        for i in (0, 2)
-    ]
-    down_piece = links.start(piece(down_ref, x), piece(down_other_ref, x), far)
+    up_copies = [fetch(up_ref, up_other_ref, quarter) for quarter in range(4)]
+    near_level = send(level_ref, near_level_ref, near)
+    cots_y = []
+
+    def pass_cots(chunk):
+        cots[chunk].wait_recv()
+        rows_here = cot_rows(near_cot_ref, t, chunk)
+        cots_y.append(send(rows_here, rows_here, y_side))
+        onward.append(send(rows_here, rows_here, core))
+
+    half = HEAD_DIM // 2
+    lane = lax.broadcasted_iota(jnp.int32, (1, HEAD_DIM), 1)
+    freq = jnp.exp((lane % half).astype(F32) * (-math.log(10000.0) / half))
+    side = jnp.where(lane < half, -1.0, 1.0)
 
     def project(i, carry):
         at = pl.ds(pl.multiple_of(i * QBLOCK, QBLOCK), QBLOCK)
+        token_block(i).wait()
         normed, _ = norm_parts(tokens_ref[at, :].astype(F32))
         low = (normed * gain1_ref[...] + bias1_ref[...]).astype(BF16)
         n1_ref[at, :] = low
-        cosine, sine = cos_ref[at, :], sin_ref[at, :]
+        token = lax.broadcasted_iota(jnp.int32, (QBLOCK, 1), 0) + i * QBLOCK
+        angle = (token - first_ref[at, :]).astype(F32) * freq
+        cosine, sine = jnp.cos(angle), jnp.sin(angle) * side
+        cos_ref[at, :] = cosine
+        sin_ref[at, :] = sine
         for part, out_ref in enumerate((q_ref, k_ref, v_ref)):
+
+            @pl.when(i == 0)
+            def _():
+                w_copies[part].wait()
+
             projected = dot(low, w_ref[part], NN)
             if part == 2:
                 out_ref[at, :] = projected.astype(BF16)
                 continue
-            for lane in range(0, own, HEAD_DIM):
-                head = projected[:, lane : lane + HEAD_DIM]
-                turned = head * cosine + pltpu.roll(head, HEAD_DIM // 2, 1) * sine
-                out_ref[at, lane : lane + HEAD_DIM] = turned.astype(BF16)
+            for start in range(0, own, HEAD_DIM):
+                head = projected[:, start : start + HEAD_DIM]
+                turned = head * cosine + pltpu.roll(head, half, 1) * sine
+                out_ref[at, start : start + HEAD_DIM] = turned.astype(BF16)
         return carry
 
-    lax.fori_loop(0, rows // QBLOCK, project, 0)
+    lax.fori_loop(0, blocks, project, 0)
+    outs = [
+        pltpu.make_async_copy(ref, out, out_sems.at[i])
+        for i, (ref, out) in enumerate(
+            ((n1_ref, n1_out), (q_ref, q_out), (k_ref, k_out), (v_ref, v_out), (heads_ref, heads_out))
+        )
+    ]
+    for copy in outs[:4]:
+        copy.start()
 
     for head in range(heads):
         lanes = slice(head * HEAD_DIM, (head + 1) * HEAD_DIM)
@@ -199,63 +258,70 @@
             out = dot(weights, v_ref[:length, lanes], NN)
             heads_ref[at, lanes] = (out * keep_ref[at]).astype(BF16)
             log_ref[at, head : head + 1] = most + jnp.log(total)
+        if head < 4:
+            pass_cots(head)
+
+    for chunk in range(heads, 4):
+        pass_cots(chunk)
+    outs[4].start()
+    w_out_copy.wait()
 
     def attended(index):
         at = pl.ds(pl.multiple_of(index * share, share), share)
         return dot(heads_ref[at, :], w_out_ref[...], NN)
 
     away_ref[1] = attended(t ^ 3).astype(BF16)
-    to_core1 = links.start(away_ref.at[1], got_core_ref.at[1], core)
+    to_core1 = send(away_ref.at[1], got_core_ref.at[1], core)
     away_ref[0] = attended(t ^ 1).astype(BF16)
-    to_core0 = links.start(away_ref.at[0], got_core_ref.at[0], core)
+    to_core0 = send(away_ref.at[0], got_core_ref.at[0], core)
     passed = attended(t ^ 2)
     to_core1.wait_recv()
     pass_ref[...] = (passed + got_core_ref[1].astype(F32)).astype(BF16)
-    to_y = links.start(pass_ref, got_y_ref, y_side)
+    to_y = send(pass_ref, got_y_ref, y_side)
     middle = attended(t)
     middle += tokens_ref[pl.ds(pl.multiple_of(t * share, share), share), :].astype(F32)
     to_core0.wait_recv()
     middle_ref[...] = middle + got_core_ref[0].astype(F32)
 
-    onward = []
-
-    def pass_on(copy, ref, devices):
-        copy.wait_recv()
-        onward.extend(links.start(ref, ref, device) for device in devices)
-
-    for i, copy in zip((0, 2), cots):
-        pass_on(copy, cots_ref.at[1, parity + i], [core])
-    pass_on(up_piece, piece(up_other_ref, x), twins)
+    for chunk, copy in enumerate(cots_y):
+        pass_on(copy, cot_rows(near_cot_ref, t ^ 2, chunk), [core])
+    down_copies = []
+    for quarter, copy in enumerate(up_copies):
+        pass_on(copy, piece(up_other_ref, quarter), twins)
+        if quarter >= 2:
+            down_copies.append(fetch(down_ref, down_other_ref, quarter - 2))
     to_y.wait_recv()
     total = middle_ref[...] + got_y_ref[...].astype(F32)
     middle_ref[...] = total
     normed, _ = norm_parts(total)
     own_ref[...] = (normed * gain2_ref[...] + bias2_ref[...]).astype(BF16)
-    keep_own = pltpu.make_async_copy(own_ref, n2_ref.at[0, t], local_sem)
+    keep_own = pltpu.make_async_copy(own_ref, n2_ref.at[0, t], in_sems.at[0])
     keep_own.start()
-    to_near = links.start(own_ref, n2_ref.at[1, t], near)
-    own_y = links.start(own_ref, n2_ref.at[0, t], y_side)
-    own_core = links.start(own_ref, n2_ref.at[0, t], core)
+    to_near = send(own_ref, n2_ref.at[1, t], near)
+    own_y = send(own_ref, n2_ref.at[0, t], y_side)
+    own_core = send(own_ref, n2_ref.at[0, t], core)
+    down_copies += [fetch(down_ref, down_other_ref, quarter) for quarter in (2, 3)]
     own_y.wait_recv()
-    y_core = links.start(n2_ref.at[0, t ^ 2], n2_ref.at[0, t ^ 2], core)
+    y_core = send(n2_ref.at[0, t ^ 2], n2_ref.at[0, t ^ 2], core)
     to_near.wait_recv()
-    near_y = links.start(n2_ref.at[1, t], n2_ref.at[1, t], y_side)
-    near_core = links.start(n2_ref.at[1, t], n2_ref.at[1, t], core)
+    near_y = send(n2_ref.at[1, t], n2_ref.at[1, t], y_side)
+    near_core = send(n2_ref.at[1, t], n2_ref.at[1, t], core)
+    for quarter in (0, 1):
+        pass_on(down_copies[quarter], piece(down_other_ref, quarter), twins)
+    pass_on(down_copies[2], piece(down_other_ref, 2), twins)
     near_y.wait_recv()
-    near_y_core = links.start(n2_ref.at[1, t ^ 2], n2_ref.at[1, t ^ 2], core)
-    pass_on(down_piece, piece(down_other_ref, x), twins)
-    for copy in (keep_own, *keep_cots):
+    near_y_core = send(n2_ref.at[1, t ^ 2], n2_ref.at[1, t ^ 2], core)
+    pass_on(down_copies[3], piece(down_other_ref, 3), twins)
+    keep_own.wait()
+    for copy in outs:
         copy.wait()
-    for copy in (own_core, y_core, near_core, near_y_core, *onward):
+    for copy in (near_level, own_core, y_core, near_core, near_y_core, *onward):
         copy.wait_recv()
-    for copy in (
-        up_piece, *cots, down_piece, to_core1, to_core0, to_y,
-        to_near, own_y, own_core, y_core, near_y, near_core, near_y_core, *onward,
-    ):
+    for copy in begun:
         copy.wait_send()
 
 
-def front_call(tokens, ln1, w3, tables_, first, keep, w_out, ln2, up, down, cotangent):
+def front_call(tokens, ln1, w3, first, keep, w_out, ln2, up, down, cotangent, levels):
     rows, width = tokens.shape
     own = w3.shape[2]
     splits, copies = lax.axis_size("tensor"), lax.axis_size("dp")
@@ -263,34 +329,47 @@
     inside = pl.BlockSpec(memory_space=pltpu.VMEM)
     outside = pl.BlockSpec(memory_space=pl.ANY)
     shape = jax.ShapeDtypeStruct
-    total = 14 + 2 * copies
+    vmem = lambda dtype, *size: pltpu.VMEM(size, dtype)
+    total = 35 + 8 * (copies - 1)
+    narrow = shape((rows, own), BF16)
     return pl.pallas_call(
         functools.partial(front_kernel, copies),
-        in_specs=[inside] * 11 + [outside] * 3,
-        out_specs=[inside] * 7 + [outside] * 4,
+        in_specs=[inside] * 6 + [outside] * 7,
+        out_specs=[inside] * 4 + [outside] * 10,
         out_shape=[
-            shape((rows, width), BF16),
-            shape((rows, own), BF16),
-            shape((rows, own), BF16),
-            shape((rows, own), BF16),
-            shape((rows, own), BF16),
             shape((rows, own // HEAD_DIM), F32),
             shape((share, width), F32),
+            shape((rows, HEAD_DIM), F32),
+            shape((rows, HEAD_DIM), F32),
+            shape((rows, width), BF16),
+            narrow,
+            narrow,
+            narrow,
+            narrow,
             shape((2, splits, share, width), BF16),
             shape(up.shape, BF16),
             shape(down.shape, BF16),
-            shape((2, splits, share, width), BF16),
+            shape((splits, share, width), BF16),
+            shape(levels.shape, F32),
         ],
         scratch_shapes=[
-            pltpu.VMEM((2, share, width), BF16),
-            pltpu.VMEM((2, share, width), BF16),
-            pltpu.VMEM((share, width), BF16),
-            pltpu.VMEM((share, width), BF16),
-            pltpu.VMEM((share, width), BF16),
+            vmem(BF16, rows, width),
+            vmem(BF16, *w3.shape),
+            vmem(BF16, *w_out.shape),
+            vmem(BF16, rows, width),
+            vmem(BF16, rows, own),
+            vmem(BF16, rows, own),
+            vmem(BF16, rows, own),
+            vmem(BF16, rows, own),
+            vmem(BF16, 2, share, width),
+            vmem(BF16, 2, share, width),
+            vmem(BF16, share, width),
+            vmem(BF16, share, width),
+            vmem(BF16, share, width),
             pltpu.SemaphoreType.DMA((total,)),
             pltpu.SemaphoreType.DMA((total,)),
-            pltpu.SemaphoreType.DMA,
-            pltpu.SemaphoreType.DMA((splits,)),
+            pltpu.SemaphoreType.DMA((rows // QBLOCK + 4,)),
+            pltpu.SemaphoreType.DMA((5,)),
         ],
         compiler_params=pltpu.CompilerParams(
             vmem_limit_bytes=56 << 20, collective_id=0, has_side_effects=True
@@ -301,7 +380,7 @@
             transcendentals=rows * rows * own // HEAD_DIM,
         ),
         name="front",
-    )(tokens, *ln1, w3, *tables_, first, keep, w_out, *ln2, up, down, cotangent)
+    )(*ln1, first, keep, *ln2, tokens, w3, w_out, up, down, cotangent, levels)
 
 
 def block_at(i, t):
@@ -324,6 +403,7 @@
     copies,
     n2_ref,
     cot_ref,
+    near_cot_ref,
     up_own_ref,
     up_other_ref,
     down_own_ref,
@@ -376,10 +456,15 @@
 
     def load(i, slot):
         at, s = block_at(i, t)
-        return (
-            pltpu.make_async_copy(n2_ref.at[at, s], n2_in.at[slot], in_sems.at[slot, 0]),
-            pltpu.make_async_copy(cot_ref.at[at, s], cot_in.at[slot], in_sems.at[slot, 1]),
-        )
+        return pltpu.make_async_copy(n2_ref.at[at, s], n2_in.at[slot], in_sems.at[slot, 0])
+
+    def load_cot(i, slot, act):
+        at, s = block_at(i, t)
+        for index, ref in enumerate((cot_ref, near_cot_ref)):
+
+            @pl.when(at == index)
+            def _():
+                act(pltpu.make_async_copy(ref.at[s], cot_in.at[slot], in_sems.at[slot, 1]))
 
     def store(i, slot):
         at, s = block_at(i, t)
@@ -398,8 +483,8 @@
             for kind in (0, 1)
         ]
 
-    for copy in load(0, 0):
-        copy.start()
+    load(0, 0).start()
+    load_cot(0, 0, lambda copy: copy.start())
     meet([core, y_side, near] + twins)
     links = Copies(send_sems, recv_sems)
     f_near_y = links.make(send_ref.at[0], got_fz.at[0], near)
@@ -412,13 +497,13 @@
     def work(i, carry):
         slot = i % 2
         at, s = block_at(i, t)
-        for copy in load(i, slot):
-            copy.wait()
+        load(i, slot).wait()
+        load_cot(i, slot, lambda copy: copy.wait())
 
         @pl.when(i < 7)
         def _():
-            for copy in load(i + 1, 1 - slot):
-                copy.start()
+            load(i + 1, 1 - slot).start()
+            load_cot(i + 1, 1 - slot, lambda copy: copy.start())
 
         @pl.when(i >= 2)
         def _():
@@ -559,7 +644,7 @@
 
     own = pltpu.make_async_copy(n2_ref.at[0, t], n2_in.at[0], in_sems.at[0, 0])
     own.start()
-    own_cot = pltpu.make_async_copy(cot_ref.at[0, t], cot_in.at[0], in_sems.at[0, 1])
+    own_cot = pltpu.make_async_copy(cot_ref.at[t], cot_in.at[0], in_sems.at[0, 1])
     own_cot.start()
     own.wait()
     own_cot.wait()
@@ -608,7 +693,7 @@
         copy.wait_send()
 
 
-def middle_call(n2, cotangents, ups, downs, w_router, levels, middle, ln2):
+def middle_call(n2, cotangent, near_cotangent, ups, downs, w_router, levels, middle, ln2):
     _, splits, share, width = n2.shape
     copies = lax.axis_size("dp")
     half = ups[0].shape[1]
@@ -620,7 +705,7 @@
     dma = lambda *count: pltpu.SemaphoreType.DMA(count)
     return pl.pallas_call(
         functools.partial(middle_kernel, copies),
-        in_specs=[outside] * 2 + [inside] * 9,
+        in_specs=[outside] * 3 + [inside] * 9,
         out_specs=[inside] * 4 + [outside] * 4,
         out_shape=[
             shape((share, width), BF16),
@@ -666,26 +751,26 @@
             flops=12 * rows * width * 2 * half, bytes_accessed=80 << 20, transcendentals=0
         ),
         name="middle",
-    )(n2, cotangents, *ups, *downs, w_router, levels, middle, *ln2)
+    )(n2, cotangent.reshape(splits, share, width), near_cotangent, *ups, *downs, w_router, levels, middle, *ln2)
 
 
 def back_kernel(
     copies,
-    q_ref,
-    k_ref,
-    v_ref,
-    heads_ref,
     log_ref,
     first_ref,
     keep_ref,
     cos_ref,
     sin_ref,
     w_out_ref,
-    w_ref,
     gain1_ref,
     tokens_ref,
     gx2_ref,
     small_in_ref,
+    q_in,
+    k_in,
+    v_in,
+    heads_in,
+    w_in,
     ga_in_ref,
     mixed_in_ref,
     n1_ref,
@@ -702,6 +787,11 @@
     up_got_ref,
     got_up_ref,
     leave_ref,
+    q_ref,
+    k_ref,
+    v_ref,
+    heads_ref,
+    w_ref,
     ga_ref,
     go_ref,
     gp_ref,
@@ -732,6 +822,7 @@
     tile_out_sems,
     fold_sems,
     fold_out_sems,
+    in_sems,
 ):
     t, z, x = lax.axis_index("tensor"), lax.axis_index("bucket"), lax.axis_index("dp")
     rows, own = q_ref.shape
@@ -764,8 +855,18 @@
     ]
     mixed_y = send(mixed_in_ref, mixed_ref.at[t], y_side)
     mixed_core = send(mixed_in_ref, mixed_ref.at[t], core)
-    mixed_own = pltpu.make_async_copy(mixed_in_ref, mixed_ref.at[t], local_sems.at[1])
-    mixed_own.start()
+    mixed_take = pltpu.make_async_copy(mixed_in_ref, tg_own_ref, local_sems.at[1])
+    mixed_take.start()
+    mixed_own = pltpu.make_async_copy(tg_own_ref, mixed_ref.at[t], local_sems.at[3])
+
+    loaded = [
+        pltpu.make_async_copy(source, target, in_sems.at[index])
+        for index, (source, target) in enumerate(
+            ((heads_in, heads_ref), (q_in, q_ref), (k_in, k_ref), (v_in, v_ref), (w_in, w_ref))
+        )
+    ]
+    for copy in loaded:
+        copy.start()
 
     few = fold_a.shape[1]
     half = fold_out.shape[2]
@@ -828,6 +929,8 @@
 
     ga_own.wait()
     grad_heads(t)
+    mixed_take.wait()
+    mixed_own.start()
     ga_core.wait_recv()
     grad_heads(t ^ 1)
     ga_y.wait_recv()
@@ -891,9 +994,13 @@
         store_tile(index, dot(left, heads_ref[...], TN), 0, 1)
         return carry
 
+    loaded[0].wait()
     lax.fori_loop(0, last, out_tile, 0)
     crossing = settle(0, 1)
     lax.fori_loop(last, last + per, out_tile, 0)
+
+    for copy in loaded[1:]:
+        copy.wait()
 
     def turn_back(grad, at):
         grad = grad.astype(BF16).astype(F32)
@@ -1013,6 +1120,7 @@
         gone.wait_recv()
         sums_ref[chunk] += got_z2[chunk].astype(F32)
 
+    mixed_own.wait()
     core_own.wait_recv()
     y_own.wait_recv()
     small_ref[...] = small_in_ref[...]
@@ -1035,7 +1143,7 @@
     tg_own = pltpu.make_async_copy(tg_own_ref, tg_ref.at[t], local_sems.at[2])
     tg_own.start()
 
-    for step, devices in enumerate(([core], [y_side], [near], [far], twins)):
+    def small_step(step, devices):
         small_send[step] = small_ref[...]
         exchanged = [
             send(small_send.at[step], got_small.at[step + d], device)
@@ -1044,28 +1152,26 @@
         for d, copy in enumerate(exchanged):
             copy.wait_recv()
             small_ref[...] += got_small[step + d]
-        if step == 1:
-            out_first = first_step(0)
-        if step == 3:
-            out_second = second_step(0, out_first)
-
+
+    small_step(0, [core])
+    pairs = {0: first_step(0)}
+    gone = {0: second_step(0, pairs[0])}
     tg_y.wait_recv()
     tg_y_core = send(tg_ref.at[t ^ 2], tg_ref.at[t ^ 2], core)
-    firsts = {1: first_step(1)}
-    third_step(0, out_second)
-    firsts[2] = first_step(2)
-    seconds = {1: second_step(1, firsts[1])}
-    firsts[3] = first_step(3)
-    seconds[2] = second_step(2, firsts[2])
-    third_step(1, seconds[1])
-    seconds[3] = second_step(3, firsts[3])
-    third_step(2, seconds[2])
-    third_step(3, seconds[3])
+    small_step(1, [y_side])
+    for chunk in (1, 2, 3):
+        pairs[chunk] = first_step(chunk)
+        third_step(chunk - 1, gone[chunk - 1])
+        if chunk == 3:
+            small_step(4, twins)
+        gone[chunk] = second_step(chunk, pairs[chunk])
+    small_step(2, [near])
+    third_step(3, gone[3])
+    small_step(3, [far])
     for copy in (core_own, mixed_core, mixed_y_core, tg_core, tg_y_core, down_far, up_far):
         if copy is not core_own:
             copy.wait_recv()
-    for copy in (mixed_own, tg_own):
-        copy.wait()
+    tg_own.wait()
     for copy in begun:
         if copy is not ga_y and copy is not ga_y_core:
             copy.wait_send()
@@ -1092,7 +1198,7 @@
     sends = 3 + 3 + 3 + 2 + 3 + 12 + 4 + 6 * others
     return pl.pallas_call(
         functools.partial(back_kernel, copies),
-        in_specs=[inside] * 15 + [outside] * 6,
+        in_specs=[inside] * 10 + [outside] * 11,
         out_specs=[inside] * 2 + [outside] * 8,
         out_shape=[
             shape((4, part, own), F32),
@@ -1107,6 +1213,11 @@
             shape((others, 4, reach, own), BF16),
         ],
         scratch_shapes=[
+            vmem(BF16, rows, own),
+            vmem(BF16, rows, own),
+            vmem(BF16, rows, own),
+            vmem(BF16, rows, own),
+            vmem(BF16, *w3.shape),
             vmem(BF16, splits, share, width),
             vmem(BF16, rows, own),
             vmem(BF16, rows, 3 * own),
@@ -1132,11 +1243,12 @@
             vmem(F32, 5, *small.shape),
             dma(sends),
             dma(sends),
-            dma(3),
+            dma(4),
             dma(2),
             dma(2),
             dma(copies, 2),
             dma(2),
+            dma(5),
         ],
         compiler_params=pltpu.CompilerParams(
             vmem_limit_bytes=62 << 20, collective_id=2, has_side_effects=True
@@ -1148,14 +1260,9 @@
         ),
         name="back",
     )(
-        queries, keys, values, heads, logs, first, keep, *tables_, w_out, w3, gain1, tokens_own,
-        grad_middle, small, grad_own, mixed_own, normed1, down_part, got_down, up_part,
+        logs, first, keep, *tables_, w_out, gain1, tokens_own, grad_middle, small,
+        queries, keys, values, heads, w3, grad_own, mixed_own, normed1, down_part, got_down, up_part,
     )
-
-
-def swap(values, axis, bit):
-    pairs = [(i, i ^ bit) for i in range(lax.axis_size(axis))]
-    return lax.ppermute(values, axis, pairs)
 
 
 def local(
@@ -1185,40 +1292,40 @@
     hidden_width = up_own.shape[1]
 
     levels = buckets[:, 0].astype(F32).reshape(-1, HEAD_DIM)
-    near_levels = swap(levels, "bucket", 1)
 
     def shard(values, bit):
         return lax.dynamic_slice_in_dim(values, (t ^ bit) * share, share, 0)
 
-    positions, first = layout(lengths[0], tok_rows)
-    first = first[:, None]
+    first = layout(lengths[0], tok_rows)[:, None]
     keep = (t < head_quarters).astype(F32)[:, None]
-    cosine, sine = tables(positions)
     w3 = jnp.transpose(w_qkv, (1, 0, 2))
     (
+        logs,
+        middle,
+        cosine,
+        sine,
         normed1,
         queries,
         keys,
         values,
         heads_low,
-        logs,
-        middle,
         n2,
         up_other,
         down_other,
-        cotangents,
+        near_cotangent,
+        near_levels,
     ) = front_call(
         tokens,
         (ln1_gain.reshape(1, -1), ln1_bias.reshape(1, -1)),
         w3,
-        (cosine, sine),
         first,
         keep,
         w_out,
         (ln2_gain.reshape(1, -1), ln2_bias.reshape(1, -1)),
         up_own,
         down_own,
-        cotangent,
+        cotangent.reshape(splits, share, model_width),
+        levels,
     )
     level_all = jnp.concatenate([levels.reshape(-1), near_levels.reshape(-1)], 0)[:, None]
     (
@@ -1232,7 +1339,8 @@
         got_down,
     ) = middle_call(
         n2,
-        cotangents,
+        cotangent,
+        near_cotangent,
         (up_own, up_other),
         (down_own, down_other),
         w_router,

time: 546 us -> 492 us (0.901)
  Pallas kernels: 496 us -> 448 us
    pallas_call x1, Pallas kernels: 173 us -> 142 us  [front_call(): pl.pallas_call(functools.partial(front_kernel, copies), in_specs=[inside]...]
    pallas_call x1, Pallas kernels: 214 us -> 194 us  [back_call(): pl.pallas_call(functools.partial(back_kernel, copies), in_specs=[inside]...]
    unnamed x13 -> x11, local copies, waits for them, and re-layouts: 12.4 us -> 12.1 us
  transfers between devices with their start and end apart: 1 -> 0, of which waited for: 0 -> 0; matrix products, arithmetic and copies ran while one was open for 2% -> 0% of each run, Pallas kernels for 32% -> 0%
where the time goes in v5:
time: 492 us; the launch traced here: 487 us
  Pallas kernels  448 us (91%)
  local copies, waits for them, and re-layouts  23.5 us (5%)
  other arithmetic  14.6 us (3%)
    pallas_call x1, Pallas kernels, back_call(): pl.pallas_call(functools.partial(back_kernel, copies), in_specs=[inside]...  194 us
    pallas_call x1, Pallas kernels, front_call(): pl.pallas_call(functools.partial(front_kernel, copies), in_specs=[inside]...  142 us
    pallas_call x1, Pallas kernels, middle_call(): pl.pallas_call(functools.partial(middle_kernel, copies), in_specs=[outsid...  112 us
    unnamed x11, local copies, waits for them, and re-layouts  12.1 us

profile of v5, /device:TPU:0, one launch (start us, length us, event | category | flops | bytes accessed | tf_op | source)
XLA Modules:
  0.0 487.2 jit_solution(16675753861150519931)
XLA Ops:
  0.6 0.7 compare_convert_fusion
  1.3 1.0 copy.39.keep_ref
  2.4 0.8 reduce-window.4
  3.2 0.1 convert_reduce_fusion
  3.3 0.7 fusion
  3.9 0.1 select_reduce_fusion
  4.0 1.0 copy.38.first_ref
  5.1 1.3 convert_element_type.27
  6.3 0.0 copy-start.2
  6.3 0.0 copy-start.1
  6.3 142.4 %front.1 = (f32[1024,4]{1,0:T(8,128)}, f32[256,2048]{1,0:T(8,128)}, f32[1024,128]{1,0:T(8,128)}, f32[1024,128]{1,0:T(8,128)}, bf16[1024,2048]{1,0:T(8,128)(2,1)}...) custom-call(f32[1,2048]{1,0:T(1,128)} %bitcast.69, ...), custom_call_target="tpu_custom_call" | custom-call | flops 10737418240 | bytes 62914560 | tf_op jit(solution)/shard_map/front/pallas_call | solution.py:335
  148.7 0.0 copy-done.2
  148.7 0.7 pad_maximum_fusion
  149.4 1.3 copy.41.level_ref
  150.8 0.0 copy-done.1
  150.8 1.1 copy.40.router_ref
  151.8 111.9 %middle.1 = (bf16[256,2048]{1,0:T(8,128)(2,1)}, f32[256,2048]{1,0:T(8,128)}, bf16[256,2048]{1,0:T(8,128)(2,1)}, f32[6,2048]{1,0:T(8,128)}, bf16[2,4,256,2048]{3,...) custom-call(bf16[2,4,256,2048]{3,2,1,0:T(8,128)(2,1)} %get-tuple-element, ...), custom_call_target="tpu_custom_call" | custom-call | flops 51539607552 | bytes 83886080 | tf_op jit(solution)/shard_map/middle/pallas_call | solution.py:706
  263.7 1.5 concatenate.7.small_in_ref
  265.2 2.3 constant_dynamic-slice_fusion.1.tokens_ref
  267.5 194.0 %back.1 = (f32[4,256,512]{2,1,0:T(8,128)}, f32[8,2048]{1,0:T(8,128)}, bf16[4,256,2048]{2,1,0:T(8,128)(2,1)}, bf16[4,256,2048]{2,1,0:T(8,128)(2,1)}, f32[1024,512...) custom-call(f32[1024,4]{1,0:T(8,128)} %get-tuple-element.40.log_ref,, ...), custom_call_target="tpu_custom_call" | custom-call | flops 22548578304 | bytes 83886080 | tf_op jit(solution)/shard_map/back/pallas_call | solution.py:1199
  461.5 3.4 add_bitcast_fusion
  464.9 3.5 copy.45
  468.4 1.8 copy.46
  470.2 0.0 copy-start
  470.2 6.8 %bitcast_convert_fusion = f32[1024,2048]{1,0:T(8,128)} fusion(bf16[4,256,2048]{2,1,0:T(8,128)(2,1)} %get-tuple-element.62), kind=kLoop, calls=%fused_computation | loop fusion | flops 2097152 | bytes 12582912 | tf_op jit(solution)/shard_map/convert_element_type | solution.py:1379
  477.0 0.0 copy-done
  477.0 1.3 slice_bitcast_fusion
  478.3 1.0 copy.44
  479.3 1.5 fusion.1
  480.8 1.4 dynamic-slice_bitcast_fusion
  482.2 4.8 copy.48
  (1 shorter events, 0.0 us)
Async XLA Ops:
  6.3 142.4 %copy-start.2 = (f32[1024,1]{0,1:T(1,128)S(1)}, f32[1024,1]{0,1:T(1,128)}, u32[]{:S(2)}) copy-start(f32[1024,1]{0,1:T(1,128)} %convert_element_type.27) | copy-start | bytes 12292
  6.3 144.4 %copy-start.1 = (bf16[2048,4]{0,1:T(4,128)(2,1)S(1)}, bf16[2048,4]{0,1:T(4,128)(2,1)}, u32[]{:S(2)}) copy-start(bf16[2048,4]{0,1:T(4,128)(2,1)} %param.25) | copy-start | bytes 49156
  470.2 6.8 %copy-start = (f32[4,256,512]{2,1,0:T(8,128)S(1)}, f32[4,256,512]{2,1,0:T(8,128)}, u32[]{:S(2)}) copy-start(f32[4,256,512]{2,1,0:T(8,128)} %get-tuple-element.64) | copy-start | bytes 6291460

commit v6 on v5

--- a/solution.py
+++ b/solution.py
@@ -174,32 +174,50 @@
         return ref.at[pl.ds(pl.multiple_of((x * 4 + quarter) * size, 16), size)]
 
     def fetch(ref, other_ref, quarter):
-        return send(piece(ref, quarter), piece(other_ref, quarter), far)
-
-    onward = []
-
-    def pass_on(copy, ref, devices):
-        copy.wait_recv()
-        onward.extend(send(ref, ref, device) for device in devices)
-
-    few = share // 4
-
-    def cot_rows(ref, s, chunk):
-        return ref.at[s, pl.ds(chunk * few, few)]
-
+        copy = links.make(piece(ref, quarter), piece(other_ref, quarter), far)
+        begun.append(copy)
+        return copy
+
+    outer = lax.rem(z, 2) == z // 2
+    pieces = [fetch(up_ref, up_other_ref, quarter) for quarter in range(4)]
+    pieces += [fetch(down_ref, down_other_ref, quarter) for quarter in range(4)]
+    parity = lax.rem(t, 2)
     cots = [
-        send(cot_rows(cot_ref, t, chunk), cot_rows(near_cot_ref, t, chunk), near)
-        for chunk in range(4)
+        links.make(cot_ref.at[parity + i], near_cot_ref.at[parity + i], near) for i in (0, 2)
     ]
-    up_copies = [fetch(up_ref, up_other_ref, quarter) for quarter in range(4)]
+    begun.extend(cots)
+    to_twins = [
+        [links.make(ref, ref, device) for device in twins]
+        for ref in [piece(up_other_ref, quarter) for quarter in range(4)]
+        + [piece(down_other_ref, quarter) for quarter in range(4)]
+    ]
+    to_core_cots = [
+        links.make(near_cot_ref.at[parity + i], near_cot_ref.at[parity + i], core) for i in (0, 2)
+    ]
+
+    def begin(copies_):
+        for copy in copies_:
+            copy.start()
+
+    def pass_weights(indices):
+        for index in indices:
+            pieces[index].wait_recv()
+            begin(to_twins[index])
+
+    def pass_cots():
+        for copy, onward_copy in zip(cots, to_core_cots):
+            copy.wait_recv()
+            onward_copy.start()
+
+    @pl.when(outer)
+    def _():
+        begin(pieces)
+
+    @pl.when(jnp.logical_not(outer))
+    def _():
+        begin(cots)
+
     near_level = send(level_ref, near_level_ref, near)
-    cots_y = []
-
-    def pass_cots(chunk):
-        cots[chunk].wait_recv()
-        rows_here = cot_rows(near_cot_ref, t, chunk)
-        cots_y.append(send(rows_here, rows_here, y_side))
-        onward.append(send(rows_here, rows_here, core))
 
     half = HEAD_DIM // 2
     lane = lax.broadcasted_iota(jnp.int32, (1, HEAD_DIM), 1)
@@ -258,11 +276,7 @@
             out = dot(weights, v_ref[:length, lanes], NN)
             heads_ref[at, lanes] = (out * keep_ref[at]).astype(BF16)
             log_ref[at, head : head + 1] = most + jnp.log(total)
-        if head < 4:
-            pass_cots(head)
-
-    for chunk in range(heads, 4):
-        pass_cots(chunk)
+
     outs[4].start()
     w_out_copy.wait()
 
@@ -283,41 +297,47 @@
     to_core0.wait_recv()
     middle_ref[...] = middle + got_core_ref[0].astype(F32)
 
-    for chunk, copy in enumerate(cots_y):
-        pass_on(copy, cot_rows(near_cot_ref, t ^ 2, chunk), [core])
-    down_copies = []
-    for quarter, copy in enumerate(up_copies):
-        pass_on(copy, piece(up_other_ref, quarter), twins)
-        if quarter >= 2:
-            down_copies.append(fetch(down_ref, down_other_ref, quarter - 2))
+    @pl.when(jnp.logical_not(outer))
+    def _():
+        pass_weights(range(8))
+        begin(pieces)
+
+    @pl.when(outer)
+    def _():
+        begin(cots)
+        pass_cots()
+
     to_y.wait_recv()
     total = middle_ref[...] + got_y_ref[...].astype(F32)
     middle_ref[...] = total
     normed, _ = norm_parts(total)
     own_ref[...] = (normed * gain2_ref[...] + bias2_ref[...]).astype(BF16)
-    keep_own = pltpu.make_async_copy(own_ref, n2_ref.at[0, t], in_sems.at[0])
+    own_y = send(own_ref, n2_ref.at[t], y_side)
+    own_core = send(own_ref, n2_ref.at[t], core)
+    keep_own = pltpu.make_async_copy(own_ref, n2_ref.at[t], in_sems.at[0])
     keep_own.start()
-    to_near = send(own_ref, n2_ref.at[1, t], near)
-    own_y = send(own_ref, n2_ref.at[0, t], y_side)
-    own_core = send(own_ref, n2_ref.at[0, t], core)
-    down_copies += [fetch(down_ref, down_other_ref, quarter) for quarter in (2, 3)]
+
+    @pl.when(outer)
+    def _():
+        pass_weights(range(4))
+
     own_y.wait_recv()
-    y_core = send(n2_ref.at[0, t ^ 2], n2_ref.at[0, t ^ 2], core)
-    to_near.wait_recv()
-    near_y = send(n2_ref.at[1, t], n2_ref.at[1, t], y_side)
-    near_core = send(n2_ref.at[1, t], n2_ref.at[1, t], core)
-    for quarter in (0, 1):
-        pass_on(down_copies[quarter], piece(down_other_ref, quarter), twins)
-    pass_on(down_copies[2], piece(down_other_ref, 2), twins)
-    near_y.wait_recv()
-    near_y_core = send(n2_ref.at[1, t ^ 2], n2_ref.at[1, t ^ 2], core)
-    pass_on(down_copies[3], piece(down_other_ref, 3), twins)
+    y_core = send(n2_ref.at[t ^ 2], n2_ref.at[t ^ 2], core)
+
+    @pl.when(outer)
+    def _():
+        pass_weights(range(4, 8))
+
+    @pl.when(jnp.logical_not(outer))
+    def _():
+        pass_cots()
+
     keep_own.wait()
     for copy in outs:
         copy.wait()
-    for copy in (near_level, own_core, y_core, near_core, near_y_core, *onward):
+    for copy in (near_level, own_core, y_core, *to_core_cots, *sum(to_twins, [])):
         copy.wait_recv()
-    for copy in begun:
+    for copy in (*begun, *to_core_cots, *sum(to_twins, [])):
         copy.wait_send()
 
 
@@ -330,7 +350,7 @@
     outside = pl.BlockSpec(memory_space=pl.ANY)
     shape = jax.ShapeDtypeStruct
     vmem = lambda dtype, *size: pltpu.VMEM(size, dtype)
-    total = 35 + 8 * (copies - 1)
+    total = 19 + 8 * (copies - 1)
     narrow = shape((rows, own), BF16)
     return pl.pallas_call(
         functools.partial(front_kernel, copies),
@@ -346,7 +366,7 @@
             narrow,
             narrow,
             narrow,
-            shape((2, splits, share, width), BF16),
+            shape((splits, share, width), BF16),
             shape(up.shape, BF16),
             shape(down.shape, BF16),
             shape((splits, share, width), BF16),
@@ -384,9 +404,9 @@
 
 
 def block_at(i, t):
-    late = i // 4
-    near = (1 - late) * (1 - (i // 2) % 2) + late * (1 - i % 2)
-    bit = (1 - late) * (3 - 2 * (i % 2)) + late * (2 - 2 * ((i % 4) // 2))
+    near, j = i // 4, i % 4
+    own_bit = (1 - j // 2) * (3 - 2 * j) + (j // 2) * (6 - 2 * j)
+    bit = (1 - near) * own_bit + near * (j + 1 - 2 * (j % 2))
     return near, t ^ bit
 
 
@@ -410,17 +430,21 @@
     down_other_ref,
     router_ref,
     level_ref,
-    x2_ref,
     gain2_ref,
     bias2_ref,
+    x2_in,
     mixed_ref,
     gx2_ref,
     ga_ref,
     small_ref,
+    near_n2_ref,
     gf_ref,
-    grad_down_ref,
-    grad_up_ref,
-    got_x_ref,
+    down_own_grad,
+    down_other_grad,
+    up_own_grad,
+    up_other_grad,
+    got_down_ref,
+    got_up_ref,
     n2_in,
     cot_in,
     gf_out,
@@ -446,64 +470,78 @@
     out_sems,
     tile_sems,
     tile_out_sems,
+    x2_sem,
 ):
     t, z, x = lax.axis_index("tensor"), lax.axis_index("bucket"), lax.axis_index("dp")
     share, width = gx2_ref.shape
     half = up_own_ref.shape[1]
     core, y_side, near = {"tensor": t ^ 1}, {"tensor": t ^ 2}, {"bucket": z ^ 1}
     twins = [{"dp": lax.rem(x + d, copies)} for d in range(1, copies)]
-    splits = n2_ref.shape[1]
-
-    def load(i, slot):
+    splits = n2_ref.shape[0]
+
+    def load(i, slot, act):
         at, s = block_at(i, t)
-        return pltpu.make_async_copy(n2_ref.at[at, s], n2_in.at[slot], in_sems.at[slot, 0])
-
-    def load_cot(i, slot, act):
-        at, s = block_at(i, t)
-        for index, ref in enumerate((cot_ref, near_cot_ref)):
+        for index, (rows_ref, grads_ref) in enumerate(
+            ((n2_ref, cot_ref), (near_n2_ref, near_cot_ref))
+        ):
 
             @pl.when(at == index)
             def _():
-                act(pltpu.make_async_copy(ref.at[s], cot_in.at[slot], in_sems.at[slot, 1]))
+                act(pltpu.make_async_copy(rows_ref.at[s], n2_in.at[slot], in_sems.at[slot, 0]))
+                act(pltpu.make_async_copy(grads_ref.at[s], cot_in.at[slot], in_sems.at[slot, 1]))
+
+    def begin(copy):
+        copy.start()
+
+    def finish_load(copy):
+        copy.wait()
 
     def store(i, slot):
         at, s = block_at(i, t)
         return pltpu.make_async_copy(gf_out.at[slot], gf_ref.at[at, s], out_sems.at[slot])
 
-    def to_core(i):
+    def to_core(a):
         return [
             pltpu.make_async_remote_copy(
-                src_ref=send_ref.at[kind * 2 + i % 2],
-                dst_ref=(core_f, core_g)[kind].at[i],
-                send_sem=core_send_sems.at[kind, i],
-                recv_sem=core_recv_sems.at[kind, i],
+                src_ref=send_ref.at[kind * 2 + int(a == 1)],
+                dst_ref=(core_f, core_g)[kind].at[a],
+                send_sem=core_send_sems.at[kind, a],
+                recv_sem=core_recv_sems.at[kind, a],
                 device_id=core,
                 device_id_type=pl.DeviceIdType.MESH,
             )
             for kind in (0, 1)
         ]
 
-    load(0, 0).start()
-    load_cot(0, 0, lambda copy: copy.start())
+    load(0, 0, begin)
     meet([core, y_side, near] + twins)
     links = Copies(send_sems, recv_sems)
-    f_near_y = links.make(send_ref.at[0], got_fz.at[0], near)
-    g_near_y = links.make(send_ref.at[1], got_gy.at[0], y_side)
-    g_own_y = links.make(send_ref.at[2], got_gy.at[1], y_side)
-    f_near = links.make(send_ref.at[3], got_fz.at[1], near)
-    f_own_y = links.make(send_ref.at[0], got_fy, y_side)
-    g_near = links.make(send_ref.at[1], got_gz, near)
+    few = share // 2
+    late = pl.ds(few, few)
+    early = pl.ds(0, few)
+    to_near = [
+        links.start(n2_ref.at[t, late], near_n2_ref.at[t, late], near),
+        links.start(n2_ref.at[t, early], near_n2_ref.at[t, early], near),
+        links.start(n2_ref.at[t ^ 2, early], near_n2_ref.at[t ^ 2, early], near),
+    ]
+    near_y = links.make(near_n2_ref.at[t, late], near_n2_ref.at[t, late], y_side)
+    near_core = links.make(near_n2_ref.at[t], near_n2_ref.at[t], core)
+    near_y_core = links.make(near_n2_ref.at[t ^ 2], near_n2_ref.at[t ^ 2], core)
+    g_own_y = links.make(send_ref.at[4], got_gy.at[1], y_side)
+    f_near = links.make(send_ref.at[1], got_fz.at[1], near)
+    g_near_y = links.make(send_ref.at[0], got_gy.at[0], y_side)
+    f_near_y = links.make(send_ref.at[2], got_fz.at[0], near)
+    f_own_y = links.make(send_ref.at[3], got_fy, y_side)
+    g_near = links.make(send_ref.at[4], got_gz, near)
 
     def work(i, carry):
         slot = i % 2
         at, s = block_at(i, t)
-        load(i, slot).wait()
-        load_cot(i, slot, lambda copy: copy.wait())
-
-        @pl.when(i < 7)
+        load(i, slot, finish_load)
+
+        @pl.when((i != 3) & (i != 5) & (i != 7))
         def _():
-            load(i + 1, 1 - slot).start()
-            load_cot(i + 1, 1 - slot, lambda copy: copy.start())
+            load(i + 1, 1 - slot, begin)
 
         @pl.when(i >= 2)
         def _():
@@ -533,116 +571,160 @@
                 gu_ref[spot, half:], up_other_ref[lanes, :], NT
             )
 
-        @pl.when(i < 4)
+        def leave(a):
+            for before in {2: (0,), 3: (2,)}.get(a, ()):
+                for copy in to_core(before):
+                    copy.wait_send()
+            send_ref[int(a == 1)] = part_f[...].astype(BF16)
+            send_ref[2 + int(a == 1)] = part_g[...].astype(BF16)
+            for copy in to_core(a):
+                copy.start()
+
+        for a, index in enumerate((0, 1, 4, 6)):
+
+            @pl.when(i == index)
+            def _():
+                leave(a)
+
+        def with_core(kind, a):
+            to_core(a)[kind].wait_recv()
+            got = (core_f, core_g)[kind][a].astype(F32)
+            return (part_f, part_g)[kind][...] + got
+
+        @pl.when(i == 1)
         def _():
-            @pl.when(i >= 2)
-            def _():
-                for copy in to_core(i - 2):
-                    copy.wait_send()
-
-            send_ref[slot] = part_f[...].astype(BF16)
-            send_ref[2 + slot] = part_g[...].astype(BF16)
-            for copy in to_core(i):
-                copy.start()
-
-        def with_core(kind, at_i):
-            to_core(at_i)[kind].wait_recv()
-            got = (core_f, core_g)[kind][at_i].astype(F32)
-            return (part_f, part_g)[kind][...] + got
+            to_near[0].wait_recv()
+            near_y.start()
 
         @pl.when(i == 4)
         def _():
-            for j in (2, 3):
-                for copy in to_core(j):
-                    copy.wait_send()
-            send_ref[1] = with_core(1, 0).astype(BF16)
-            g_near_y.start()
-            send_ref[0] = with_core(0, 0).astype(BF16)
-            f_near_y.start()
+            to_near[2].wait_recv()
+            near_y.wait_recv()
+            near_y_core.start()
+
+        @pl.when(i == 2)
+        def _():
+            send_ref[4] = with_core(1, 0).astype(BF16)
+            g_own_y.start()
+            hold_f[...] = with_core(0, 0)
+
+        @pl.when(i == 3)
+        def _():
+            mixed_ref[...] = with_core(0, 1).astype(BF16)
+            ga_ref[...] = with_core(1, 1).astype(BF16)
+            to_near[1].wait_recv()
+            near_core.start()
+            near_core.wait_recv()
+            load(i + 1, 1 - slot, begin)
 
         @pl.when(i == 5)
         def _():
-            send_ref[2] = with_core(1, 2).astype(BF16)
-            g_own_y.start()
-            hold_f[...] = with_core(0, 2)
-
-        @pl.when(i == 6)
-        def _():
-            send_ref[3] = with_core(0, 1).astype(BF16)
+            for copy in to_core(1):
+                copy.wait_send()
+            send_ref[1] = with_core(0, 2).astype(BF16)
             f_near.start()
-            gx2_ref[...] = with_core(1, 1)
+            gx2_ref[...] = with_core(1, 2)
+            near_y_core.wait_recv()
+            load(i + 1, 1 - slot, begin)
 
         @pl.when(i == 7)
         def _():
-            part_f[...] = with_core(0, 3)
-            part_g[...] = with_core(1, 3)
+            for copy in to_core(3):
+                copy.wait_send()
+            send_ref[0] = with_core(1, 3).astype(BF16)
+            g_near_y.start()
+            send_ref[2] = with_core(0, 3).astype(BF16)
+            f_near_y.start()
 
         return carry
 
     lax.fori_loop(0, 8, work, 0)
     store(6, 0).wait()
     store(7, 1).wait()
+    x2_ref = part_f
+    x2_copy = pltpu.make_async_copy(x2_in, x2_ref, x2_sem)
+    x2_copy.start()
 
     tile = tile_in.shape[-1]
     tiles = width // tile
 
-    def weight_grads(source_ref, right_ref, result_ref):
+    def weight_grads(sources, right_ref, results):
         def fetch(j, slot):
             lanes = pl.ds(pl.multiple_of(j * tile, tile), tile)
-            return pltpu.make_async_copy(
-                source_ref.at[:, :, :, lanes], tile_in.at[slot], tile_sems.at[slot]
-            )
+            return [
+                pltpu.make_async_copy(
+                    source.at[:, :, lanes], tile_in.at[slot, index], tile_sems.at[slot, index]
+                )
+                for index, source in enumerate(sources)
+            ]
 
         def put(j, slot):
             rows = pl.ds(pl.multiple_of(j * tile, tile), tile)
-            return pltpu.make_async_copy(
-                tile_out.at[slot], result_ref.at[rows, :], tile_out_sems.at[slot]
-            )
-
-        fetch(0, 0).start()
+            return [
+                pltpu.make_async_copy(
+                    tile_out.at[slot, index], result.at[rows, :], tile_out_sems.at[slot, index]
+                )
+                for index, result in enumerate(results)
+            ]
+
+        for copy in fetch(0, 0):
+            copy.start()
 
         def step(j, carry):
             slot = j % 2
-            fetch(j, slot).wait()
+            for copy in fetch(j, slot):
+                copy.wait()
 
             @pl.when(j < tiles - 1)
             def _():
-                fetch(j + 1, 1 - slot).start()
+                for copy in fetch(j + 1, 1 - slot):
+                    copy.start()
 
             @pl.when(j >= 2)
             def _():
-                put(j - 2, slot).wait()
+                for copy in put(j - 2, slot):
+                    copy.wait()
 
             left = tile_in[slot].reshape(-1, tile)
-            tile_out[slot] = dot(left, right_ref[...], TN).astype(BF16)
-            put(j, slot).start()
+            total = dot(left, right_ref[...], TN).astype(BF16)
+            for index in (0, 1):
+                tile_out[slot, index] = total[:, index * half : (index + 1) * half]
+            for copy in put(j, slot):
+                copy.start()
             return carry
 
         lax.fori_loop(0, tiles, step, 0)
-        put(tiles - 2, (tiles - 2) % 2).wait()
-        put(tiles - 1, (tiles - 1) % 2).wait()
-
-    weight_grads(gf_ref, hid_ref, grad_down_ref)
+        for j in (tiles - 2, tiles - 1):
+            for copy in put(j, j % 2):
+                copy.wait()
+
     size = width // copies
-    downs = []
-    for d in range(1, copies):
-        part = pl.ds(pl.multiple_of(lax.rem(x + d, copies) * size, size), size)
-        downs.append(
-            links.start(grad_down_ref.at[part, :], got_x_ref.at[d - 1], twins[d - 1])
-        )
+
+    def to_twins(grad_ref, got_ref):
+        return [
+            links.start(
+                grad_ref.at[pl.ds(pl.multiple_of(lax.rem(x + d, copies) * size, size), size), :],
+                got_ref.at[d - 1],
+                twins[d - 1],
+            )
+            for d in range(1, copies)
+        ]
+
+    weight_grads((gf_ref.at[0], gf_ref.at[1]), hid_ref, (down_own_grad, down_other_grad))
+    crossing = to_twins(down_other_grad, got_down_ref)
+
+    weight_grads((n2_ref, near_n2_ref), gu_ref, (up_own_grad, up_other_grad))
+    crossing += to_twins(up_other_grad, got_up_ref)
 
     f_near_y.wait_recv()
-    f_near_y.wait_send()
-    send_ref[0] = (hold_f[...] + got_fz[0].astype(F32)).astype(BF16)
+    send_ref[3] = (hold_f[...] + got_fz[0].astype(F32)).astype(BF16)
     f_own_y.start()
     g_near_y.wait_recv()
-    g_near_y.wait_send()
-    send_ref[1] = (gx2_ref[...] + got_gy[0].astype(F32)).astype(BF16)
+    g_own_y.wait_send()
+    send_ref[4] = (gx2_ref[...] + got_gy[0].astype(F32)).astype(BF16)
     g_near.start()
 
-    weight_grads(n2_ref, gu_ref, grad_up_ref)
-
-    own = pltpu.make_async_copy(n2_ref.at[0, t], n2_in.at[0], in_sems.at[0, 0])
+    own = pltpu.make_async_copy(n2_ref.at[t], n2_in.at[0], in_sems.at[0, 0])
     own.start()
     own_cot = pltpu.make_async_copy(cot_ref.at[t], cot_in.at[0], in_sems.at[0, 1])
     own_cot.start()
@@ -650,6 +732,7 @@
     own_cot.wait()
     for copy in (f_near, f_own_y, g_own_y, g_near):
         copy.wait_recv()
+    x2_copy.wait()
     small_ref[...] = jnp.zeros_like(small_ref)
     few = 64
 
@@ -658,14 +741,14 @@
         level = level_ref[pl.ds(pl.multiple_of(t * share + j * few, few), few), :]
         rows = n2_in[0, at, :]
         gate, probs, onehot = router_gate(rows, router_ref, level)
-        branch = part_f[at, :] + got_fz[1, at, :].astype(F32) + got_fy[at, :].astype(F32)
+        branch = mixed_ref[at, :].astype(F32) + got_fz[1, at, :].astype(F32) + got_fy[at, :].astype(F32)
         branch = branch.astype(BF16).astype(F32)
         x2 = x2_ref[at, :]
         mixed_ref[at, :] = (x2 + gate * branch).astype(BF16)
         grad_out = cot_in[0, at, :].astype(F32)
         grad_gate = jnp.sum(grad_out * branch, -1, keepdims=True)
         grad_logits = grad_gate * gate * (onehot - probs)
-        returned = part_g[at, :] + got_gy[1, at, :].astype(F32) + got_gz[at, :].astype(F32)
+        returned = ga_ref[at, :].astype(F32) + got_gy[1, at, :].astype(F32) + got_gz[at, :].astype(F32)
         grad_n2 = returned.astype(BF16).astype(F32)
         grad_n2 += lax.dot_general(
             grad_logits,
@@ -687,14 +770,17 @@
         return carry
 
     lax.fori_loop(0, share // few, finish, 0)
-    for copy in downs:
+    for copy in crossing:
         copy.wait_recv()
-    for copy in (g_own_y, f_near, f_own_y, g_near, *downs):
+    for copy in (
+        *to_near, near_y, near_core, near_y_core, f_near,
+        g_near_y, f_near_y, f_own_y, g_near, *crossing,
+    ):
         copy.wait_send()
 
 
 def middle_call(n2, cotangent, near_cotangent, ups, downs, w_router, levels, middle, ln2):
-    _, splits, share, width = n2.shape
+    splits, share, width = n2.shape
     copies = lax.axis_size("dp")
     half = ups[0].shape[1]
     rows = 2 * splits * share
@@ -705,17 +791,17 @@
     dma = lambda *count: pltpu.SemaphoreType.DMA(count)
     return pl.pallas_call(
         functools.partial(middle_kernel, copies),
-        in_specs=[outside] * 3 + [inside] * 9,
-        out_specs=[inside] * 4 + [outside] * 4,
+        in_specs=[outside] * 3 + [inside] * 8 + [outside],
+        out_specs=[inside] * 4 + [outside] * 8,
         out_shape=[
             shape((share, width), BF16),
             shape((share, width), F32),
             shape((share, width), BF16),
             shape((2 + w_router.shape[1], width), F32),
             shape(n2.shape, BF16),
-            shape((width, 2 * half), BF16),
-            shape((width, 2 * half), BF16),
-            shape((copies - 1, width // copies, 2 * half), BF16),
+            shape((2, *n2.shape), BF16),
+            *[shape((width, half), BF16)] * 4,
+            *[shape((copies - 1, width // copies, half), BF16)] * 2,
         ],
         scratch_shapes=[
             block((2,)),
@@ -726,7 +812,7 @@
             block((), F32),
             block((), F32),
             block((), F32),
-            block((4,)),
+            block((5,)),
             block((4,)),
             block((4,)),
             block((2,)),
@@ -734,15 +820,16 @@
             block((2,)),
             block(()),
             pltpu.VMEM((2, 2, splits, share, 256), BF16),
-            pltpu.VMEM((2, 256, 2 * half), BF16),
+            pltpu.VMEM((2, 2, 256, half), BF16),
             dma(2, 4),
             dma(2, 4),
-            dma(6 + copies - 1),
-            dma(6 + copies - 1),
+            dma(12 + 2 * (copies - 1)),
+            dma(12 + 2 * (copies - 1)),
             dma(2, 2),
             dma(2),
-            dma(2),
-            dma(2),
+            dma(2, 2),
+            dma(2, 2),
+            pltpu.SemaphoreType.DMA,
         ],
         compiler_params=pltpu.CompilerParams(
             vmem_limit_bytes=62 << 20, collective_id=1, has_side_effects=True
@@ -751,7 +838,7 @@
             flops=12 * rows * width * 2 * half, bytes_accessed=80 << 20, transcendentals=0
         ),
         name="middle",
-    )(n2, cotangent.reshape(splits, share, width), near_cotangent, *ups, *downs, w_router, levels, middle, *ln2)
+    )(n2, cotangent.reshape(splits, share, width), near_cotangent, *ups, *downs, w_router, levels, *ln2, middle)
 
 
 def back_kernel(
@@ -777,15 +864,17 @@
     down_ref,
     got_down_ref,
     up_ref,
+    got_up_ref,
+    down_own_ref,
+    up_own_ref,
     sums_ref,
     small_ref,
     mixed_ref,
     tg_ref,
-    down_own_ref,
-    down_got_ref,
-    up_own_ref,
-    up_got_ref,
-    got_up_ref,
+    down_far_ref,
+    up_far_ref,
+    down_twin_ref,
+    up_twin_ref,
     leave_ref,
     q_ref,
     k_ref,
@@ -806,7 +895,6 @@
     fold_a,
     fold_b,
     fold_send,
-    fold_out,
     kept_ref,
     got_x_ref,
     z_send,
@@ -821,7 +909,6 @@
     tile_sems,
     tile_out_sems,
     fold_sems,
-    fold_out_sems,
     in_sems,
 ):
     t, z, x = lax.axis_index("tensor"), lax.axis_index("bucket"), lax.axis_index("dp")
@@ -849,10 +936,14 @@
     ga_core = send(ga_in_ref, ga_ref.at[t], core)
     ga_own = pltpu.make_async_copy(ga_in_ref, ga_ref.at[t], local_sems.at[0])
     ga_own.start()
-    ups = [
-        send(up_ref.at[span(lax.rem(x + d, copies) * reach, reach)], got_up_ref.at[d - 1], twins[d - 1])
-        for d in range(1, copies)
-    ]
+
+    def to_twins(source_ref, target_ref):
+        for d in range(1, copies):
+            rows_there = span(lax.rem(x + d, copies) * reach, reach)
+            twin_copies.append(send(source_ref.at[rows_there], target_ref.at[d - 1], twins[d - 1]))
+
+    twin_copies = []
+    to_twins(up_own_ref, up_twin_ref)
     mixed_y = send(mixed_in_ref, mixed_ref.at[t], y_side)
     mixed_core = send(mixed_in_ref, mixed_ref.at[t], core)
     mixed_take = pltpu.make_async_copy(mixed_in_ref, tg_own_ref, local_sems.at[1])
@@ -869,9 +960,8 @@
         copy.start()
 
     few = fold_a.shape[1]
-    half = fold_out.shape[2]
-
-    def fold(which, source_ref, got_ref, own_ref, target_ref):
+
+    def fold(which, source_ref, got_ref, target_ref):
         def loads(k, slot):
             mine = pltpu.make_async_copy(
                 source_ref.at[span(x * reach + k * few, few)], fold_a.at[slot], fold_sems.at[0, slot]
@@ -884,11 +974,6 @@
             ]
             return [mine] + theirs
 
-        def put(k, slot):
-            return pltpu.make_async_copy(
-                fold_out.at[slot], own_ref.at[span(k * few, few)], fold_out_sems.at[slot]
-            )
-
         for copy in loads(0, 0):
             copy.start()
         steps = reach // few
@@ -903,24 +988,17 @@
                 for copy in loads(k + 1, 1 - slot):
                     copy.start()
 
-            @pl.when(k >= 2)
-            def _():
-                put(k - 2, slot).wait()
-
             total = fold_a[slot].astype(F32)
             for d in range(copies - 1):
                 total += fold_b[slot, d].astype(F32)
-            fold_out[slot] = total[:, :half]
-            fold_send[which, span(k * few, few), :] = total[:, half:].astype(BF16)
-            put(k, slot).start()
+            fold_send[which, span(k * few, few), :] = total.astype(BF16)
             return carry
 
         lax.fori_loop(0, steps, step, 0)
-        for k in range(max(0, steps - 2), steps):
-            put(k, k % 2).wait()
         return send(fold_send.at[which], target_ref, far)
 
-    down_far = fold(0, down_ref, got_down_ref, down_own_ref, down_got_ref)
+    down_far = fold(0, down_ref, got_down_ref, down_far_ref)
+    up_far = fold(1, up_ref, got_up_ref, up_far_ref)
 
     def grad_heads(s):
         at = span(s * share, share)
@@ -1080,11 +1158,8 @@
 
     lax.fori_loop(0, last, qkv_tile, 0)
     crossing += settle(1, 3)
+    to_twins(down_own_ref, down_twin_ref)
     lax.fori_loop(last, last + per, qkv_tile, 0)
-
-    for copy in ups:
-        copy.wait_recv()
-    up_far = fold(1, up_ref, got_up_ref, up_own_ref, up_got_ref)
 
     def first_step(chunk):
         for copy in crossing[chunk]:
@@ -1168,7 +1243,7 @@
     small_step(2, [near])
     third_step(3, gone[3])
     small_step(3, [far])
-    for copy in (core_own, mixed_core, mixed_y_core, tg_core, tg_y_core, down_far, up_far):
+    for copy in (core_own, mixed_core, mixed_y_core, tg_core, tg_y_core, down_far, up_far, *twin_copies):
         if copy is not core_own:
             copy.wait_recv()
     tg_own.wait()
@@ -1179,7 +1254,7 @@
 
 def back_call(
     queries, keys, values, heads, logs, first, keep, tables_, w_out, w3, gain1, tokens_own,
-    grad_middle, small, grad_own, mixed_own, normed1, down_part, got_down, up_part,
+    grad_middle, small, grad_own, mixed_own, normed1, *level_grads,
 ):
     rows, own = queries.shape
     share, width = grad_own.shape
@@ -1187,29 +1262,26 @@
     splits = rows // share
     reach = width // copies
     part = reach // owners
-    half = down_part.shape[1] // 2
+    half = level_grads[0].shape[1]
     inside = pl.BlockSpec(memory_space=pltpu.VMEM)
     outside = pl.BlockSpec(memory_space=pl.ANY)
     shape = jax.ShapeDtypeStruct
     dma = lambda *count: pltpu.SemaphoreType.DMA(count)
     vmem = lambda dtype, *size: pltpu.VMEM(size, dtype)
     others = copies - 1
-    few = 128
-    sends = 3 + 3 + 3 + 2 + 3 + 12 + 4 + 6 * others
+    few = 256
+    sends = 30 + 7 * others
     return pl.pallas_call(
         functools.partial(back_kernel, copies),
-        in_specs=[inside] * 10 + [outside] * 11,
-        out_specs=[inside] * 2 + [outside] * 8,
+        in_specs=[inside] * 10 + [outside] * 14,
+        out_specs=[inside] * 2 + [outside] * 7,
         out_shape=[
             shape((4, part, own), F32),
             shape(small.shape, F32),
             shape((splits, share, width), BF16),
             shape((splits, share, width), BF16),
-            shape((reach, half), F32),
-            shape((reach, half), BF16),
-            shape((reach, half), F32),
-            shape((reach, half), BF16),
-            shape((others, reach, 2 * half), BF16),
+            *[shape((reach, half), BF16)] * 2,
+            *[shape((others, reach, half), BF16)] * 2,
             shape((others, 4, reach, own), BF16),
         ],
         scratch_shapes=[
@@ -1229,10 +1301,9 @@
             vmem(BF16, share, width),
             vmem(BF16, 2, rows, 256),
             vmem(BF16, 2, 3, 256, own),
-            vmem(BF16, 2, few, 2 * half),
-            vmem(BF16, 2, others, few, 2 * half),
+            vmem(BF16, 2, few, half),
+            vmem(BF16, 2, others, few, half),
             vmem(BF16, 2, reach, half),
-            vmem(F32, 2, few, half),
             vmem(BF16, 4, reach, own),
             vmem(BF16, others, 4, reach, own),
             vmem(BF16, 4, 2, part, own),
@@ -1247,7 +1318,6 @@
             dma(2),
             dma(2),
             dma(copies, 2),
-            dma(2),
             dma(5),
         ],
         compiler_params=pltpu.CompilerParams(
@@ -1261,7 +1331,7 @@
         name="back",
     )(
         logs, first, keep, *tables_, w_out, gain1, tokens_own, grad_middle, small,
-        queries, keys, values, heads, w3, grad_own, mixed_own, normed1, down_part, got_down, up_part,
+        queries, keys, values, heads, w3, grad_own, mixed_own, normed1, *level_grads,
     )
 
 
@@ -1334,9 +1404,13 @@
         grad_attention_own,
         small,
         _,
-        down_part,
-        up_part,
+        _,
+        down_own,
+        down_other,
+        up_own,
+        up_other,
         got_down,
+        got_up,
     ) = middle_call(
         n2,
         cotangent,
@@ -1348,7 +1422,7 @@
         middle,
         (ln2_gain.reshape(1, -1), ln2_bias.reshape(1, -1)),
     )
-    sums, small, mixed, tokens_grad, down_own, down_got, up_own, up_got, _, _ = back_call(
+    sums, small, mixed, tokens_grad, down_far, up_far, down_twin, up_twin, _ = back_call(
         queries,
         keys,
         values,
@@ -1366,12 +1440,21 @@
         grad_attention_own,
         mixed_own,
         normed1,
-        down_part,
+        down_other,
         got_down,
-        up_part,
+        up_other,
+        got_up,
+        down_own,
+        up_own,
     )
-    grad_down = (down_own + down_got.astype(F32)).T
-    grad_up = up_own + up_got.astype(F32)
+    size = model_width // copies
+
+    def level_grad(own, twin, distant):
+        mine = lax.dynamic_slice_in_dim(own, x * size, size, 0).astype(F32)
+        return mine + jnp.sum(twin.astype(F32), 0) + distant.astype(F32)
+
+    grad_down = level_grad(down_own, down_twin, down_far).T
+    grad_up = level_grad(up_own, up_twin, up_far)
     width = model_width // (copies * owners)
     small = lax.dynamic_slice_in_dim(small, (x * owners + z) * width, width, 1)
     return (

time: 492 us -> 463 us (0.941)
  Pallas kernels: 448 us -> 420 us
    pallas_call x1, Pallas kernels: 142 us -> 111 us  [front_call(): pl.pallas_call(functools.partial(front_kernel, copies), in_specs=[inside]...]
    pallas_call x1, Pallas kernels: 112 us -> 126 us  [middle_call(): pl.pallas_call(functools.partial(middle_kernel, copies), in_specs=[outsid...]
    pallas_call x1, Pallas kernels: 194 us -> 183 us  [back_call(): pl.pallas_call(functools.partial(back_kernel, copies), in_specs=[inside]...]
where the time goes in v6:
time: 463 us; the launch traced here: 459 us
  Pallas kernels  420 us (91%)
  local copies, waits for them, and re-layouts  23.5 us (5%)
  other arithmetic  14.8 us (3%)
    pallas_call x1, Pallas kernels, back_call(): pl.pallas_call(functools.partial(back_kernel, copies), in_specs=[inside]...  183 us
    pallas_call x1, Pallas kernels, middle_call(): pl.pallas_call(functools.partial(middle_kernel, copies), in_specs=[outsid...  126 us
    pallas_call x1, Pallas kernels, front_call(): pl.pallas_call(functools.partial(front_kernel, copies), in_specs=[inside]...  111 us
    unnamed x11, local copies, waits for them, and re-layouts  12.1 us

profile of v6, /device:TPU:0, one launch (start us, length us, event | category | flops | bytes accessed | tf_op | source)
XLA Modules:
  0.0 458.8 jit_solution(9982220415452582092)
XLA Ops:
  0.6 0.7 compare_convert_fusion
  1.3 1.0 copy.39.keep_ref
  2.4 0.8 reduce-window.4
  3.2 0.1 convert_reduce_fusion
  3.3 0.7 fusion.4
  3.9 0.1 select_reduce_fusion
  4.0 1.0 copy.38.first_ref
  5.1 1.3 convert_element_type.35
  6.3 0.0 copy-start.2
  6.3 0.0 copy-start.1
  6.3 110.5 %front.1 = (f32[1024,4]{1,0:T(8,128)}, f32[256,2048]{1,0:T(8,128)}, f32[1024,128]{1,0:T(8,128)}, f32[1024,128]{1,0:T(8,128)}, bf16[1024,2048]{1,0:T(8,128)(2,1)}...) custom-call(f32[1,2048]{1,0:T(1,128)} %bitcast.75, ...), custom_call_target="tpu_custom_call" | custom-call | flops 10737418240 | bytes 62914560 | tf_op jit(solution)/shard_map/front/pallas_call | solution.py:355
  116.9 0.0 copy-done.2
  116.9 0.7 pad_maximum_fusion
  117.6 1.3 copy.41.level_ref
  118.9 0.0 copy-done.1
  118.9 1.1 copy.40.router_ref
  120.0 126.1 %middle.1 = (bf16[256,2048]{1,0:T(8,128)(2,1)}, f32[256,2048]{1,0:T(8,128)}, bf16[256,2048]{1,0:T(8,128)(2,1)}, f32[6,2048]{1,0:T(8,128)}, bf16[4,256,2048]{2,1,...) custom-call(bf16[4,256,2048]{2,1,0:T(8,128)(2,1)} %get-tuple-element, ...), custom_call_target="tpu_custom_call" | custom-call | flops 51539607552 | bytes 83886080 | tf_op jit(solution)/shard_map/middle/pallas_call | solution.py:792
  246.1 1.5 concatenate.7.small_in_ref
  247.5 2.3 constant_dynamic-slice_fusion.1.tokens_ref
  249.8 183.0 %back.1 = (f32[4,256,512]{2,1,0:T(8,128)}, f32[8,2048]{1,0:T(8,128)}, bf16[4,256,2048]{2,1,0:T(8,128)(2,1)}, bf16[4,256,2048]{2,1,0:T(8,128)(2,1)}, bf16[1024,51...) custom-call(f32[1024,4]{1,0:T(8,128)} %get-tuple-element.43.log_ref,, ...), custom_call_target="tpu_custom_call" | custom-call | flops 22548578304 | bytes 83886080 | tf_op jit(solution)/shard_map/back/pallas_call | solution.py:1274
  432.8 3.7 fusion.1
  436.5 3.5 copy.45
  440.0 1.8 copy.46
  441.8 0.0 copy-start
  441.8 6.8 %bitcast_convert_fusion = f32[1024,2048]{1,0:T(8,128)} fusion(bf16[4,256,2048]{2,1,0:T(8,128)(2,1)} %get-tuple-element.68), kind=kLoop, calls=%fused_computation | loop fusion | flops 2097152 | bytes 12582912 | tf_op jit(solution)/shard_map/convert_element_type | solution.py:1462
  448.6 0.0 copy-done
  448.6 1.3 slice_bitcast_fusion
  449.9 1.0 copy.44
  450.9 1.5 fusion.5
  452.4 1.4 dynamic-slice_bitcast_fusion
  453.8 4.8 %copy.48 = bf16[1024,2048]{1,0:T(8,128)(2,1)} copy(bf16[1024,2048]{1,0:T(8,128)(2,1)} %bitcast.50) | data formatting | bytes 8388608
  (1 shorter events, 0.0 us)
Async XLA Ops:
  6.3 110.5 %copy-start.2 = (f32[1024,1]{0,1:T(1,128)S(1)}, f32[1024,1]{0,1:T(1,128)}, u32[]{:S(2)}) copy-start(f32[1024,1]{0,1:T(1,128)} %convert_element_type.35) | copy-start | bytes 12292
  6.3 112.6 %copy-start.1 = (bf16[2048,4]{0,1:T(4,128)(2,1)S(1)}, bf16[2048,4]{0,1:T(4,128)(2,1)}, u32[]{:S(2)}) copy-start(bf16[2048,4]{0,1:T(4,128)(2,1)} %param.25) | copy-start | bytes 49156
  441.8 6.8 %copy-start = (f32[4,256,512]{2,1,0:T(8,128)S(1)}, f32[4,256,512]{2,1,0:T(8,128)}, u32[]{:S(2)}) copy-start(f32[4,256,512]{2,1,0:T(8,128)} %get-tuple-element.70) | copy-start | bytes 6291460

commit v7 on v6

--- a/solution.py
+++ b/solution.py
@@ -850,9 +850,9 @@
     sin_ref,
     w_out_ref,
     gain1_ref,
-    tokens_ref,
     gx2_ref,
     small_in_ref,
+    tokens_in,
     q_in,
     k_in,
     v_in,
@@ -881,6 +881,7 @@
     v_ref,
     heads_ref,
     w_ref,
+    tokens_ref,
     ga_ref,
     go_ref,
     gp_ref,
@@ -953,7 +954,14 @@
     loaded = [
         pltpu.make_async_copy(source, target, in_sems.at[index])
         for index, (source, target) in enumerate(
-            ((heads_in, heads_ref), (q_in, q_ref), (k_in, k_ref), (v_in, v_ref), (w_in, w_ref))
+            (
+                (heads_in, heads_ref),
+                (q_in, q_ref),
+                (k_in, k_ref),
+                (v_in, v_ref),
+                (w_in, w_ref),
+                (tokens_in.at[t], tokens_ref),
+            )
         )
     ]
     for copy in loaded:
@@ -1198,9 +1206,10 @@
     mixed_own.wait()
     core_own.wait_recv()
     y_own.wait_recv()
-    small_ref[...] = small_in_ref[...]
     lines = 64
-    count = small_in_ref.shape[0] - 2
+    count = small_in_ref.shape[0]
+    small_ref[:count, :] = small_in_ref[...]
+    small_ref[count:, :] = jnp.zeros((2, width), F32)
 
     def finish(j, carry):
         at = span(j * lines, lines)
@@ -1253,7 +1262,7 @@
 
 
 def back_call(
-    queries, keys, values, heads, logs, first, keep, tables_, w_out, w3, gain1, tokens_own,
+    queries, keys, values, heads, logs, first, keep, tables_, w_out, w3, gain1, tokens,
     grad_middle, small, grad_own, mixed_own, normed1, *level_grads,
 ):
     rows, own = queries.shape
@@ -1269,15 +1278,16 @@
     dma = lambda *count: pltpu.SemaphoreType.DMA(count)
     vmem = lambda dtype, *size: pltpu.VMEM(size, dtype)
     others = copies - 1
+    totals = (small.shape[0] + 2, width)
     few = 256
     sends = 30 + 7 * others
     return pl.pallas_call(
         functools.partial(back_kernel, copies),
-        in_specs=[inside] * 10 + [outside] * 14,
+        in_specs=[inside] * 9 + [outside] * 15,
         out_specs=[inside] * 2 + [outside] * 7,
         out_shape=[
             shape((4, part, own), F32),
-            shape(small.shape, F32),
+            shape(totals, F32),
             shape((splits, share, width), BF16),
             shape((splits, share, width), BF16),
             *[shape((reach, half), BF16)] * 2,
@@ -1290,6 +1300,7 @@
             vmem(BF16, rows, own),
             vmem(BF16, rows, own),
             vmem(BF16, *w3.shape),
+            vmem(BF16, share, width),
             vmem(BF16, splits, share, width),
             vmem(BF16, rows, own),
             vmem(BF16, rows, 3 * own),
@@ -1310,15 +1321,15 @@
             vmem(F32, 4, part, own),
             vmem(BF16, 4, 2, part, own),
             vmem(BF16, 4, part, own),
-            vmem(F32, 4 + others, *small.shape),
-            vmem(F32, 5, *small.shape),
+            vmem(F32, 4 + others, *totals),
+            vmem(F32, 5, *totals),
             dma(sends),
             dma(sends),
             dma(4),
             dma(2),
             dma(2),
             dma(copies, 2),
-            dma(5),
+            dma(6),
         ],
         compiler_params=pltpu.CompilerParams(
             vmem_limit_bytes=62 << 20, collective_id=2, has_side_effects=True
@@ -1330,9 +1341,32 @@
         ),
         name="back",
     )(
-        logs, first, keep, *tables_, w_out, gain1, tokens_own, grad_middle, small,
-        queries, keys, values, heads, w3, grad_own, mixed_own, normed1, *level_grads,
+        logs, first, keep, *tables_, w_out, gain1, grad_middle, small,
+        tokens.reshape(splits, share, width), queries, keys, values, heads, w3, grad_own, mixed_own, normed1, *level_grads,
     )
+
+
+def finish_kernel(tg_ref, mixed_ref, tg_out, mixed_out):
+    tg_out[...] = tg_ref[...].astype(F32)
+    mixed_out[...] = mixed_ref[...]
+
+
+def finish_call(tokens_grad, mixed):
+    rows, width = mixed.shape
+    block = pl.BlockSpec((rows // 8, width), lambda i: (i, 0))
+    return pl.pallas_call(
+        finish_kernel,
+        grid=(8,),
+        in_specs=[block] * 2,
+        out_specs=[block] * 2,
+        out_shape=[
+            jax.ShapeDtypeStruct((rows, width), F32),
+            jax.ShapeDtypeStruct((rows, width), BF16),
+        ],
+        compiler_params=pltpu.CompilerParams(vmem_limit_bytes=24 << 20),
+        cost_estimate=pl.CostEstimate(flops=0, bytes_accessed=10 * rows * width, transcendentals=0),
+        name="finish",
+    )(tokens_grad, mixed)
 
 
 def local(
@@ -1362,9 +1396,6 @@
     hidden_width = up_own.shape[1]
 
     levels = buckets[:, 0].astype(F32).reshape(-1, HEAD_DIM)
-
-    def shard(values, bit):
-        return lax.dynamic_slice_in_dim(values, (t ^ bit) * share, share, 0)
 
     first = layout(lengths[0], tok_rows)[:, None]
     keep = (t < head_quarters).astype(F32)[:, None]
@@ -1434,9 +1465,9 @@
         w_out,
         w3,
         ln1_gain.reshape(1, -1),
-        shard(tokens, 0),
+        tokens,
         grad_middle,
-        jnp.concatenate([small, jnp.zeros((2, model_width), F32)], 0),
+        small,
         grad_attention_own,
         mixed_own,
         normed1,
@@ -1455,11 +1486,14 @@
 
     grad_down = level_grad(down_own, down_twin, down_far).T
     grad_up = level_grad(up_own, up_twin, up_far)
+    tokens_grad, mixed = finish_call(
+        tokens_grad.reshape(tok_rows, model_width), mixed.reshape(tok_rows, model_width)
+    )
     width = model_width // (copies * owners)
     small = lax.dynamic_slice_in_dim(small, (x * owners + z) * width, width, 1)
     return (
-        mixed.reshape(tok_rows, model_width),
-        tokens_grad.reshape(tok_rows, model_width).astype(F32),
+        mixed,
+        tokens_grad,
         small[2 + owners],
         small[3 + owners],
         jnp.transpose(sums[1:], (1, 0, 2)),

time: 463 us -> 457 us (0.987)
  other arithmetic: 14.8 us -> 7.99 us
  Pallas kernels: 420 us -> 425 us
    convert_element_type x1 -> x0, other arithmetic: 6.8 us -> none  [local(): tokens_grad.reshape(tok_rows, model_width).astype(F32)]
    pallas_call x0 -> x1, Pallas kernels: none -> 5.39 us  [finish_call(): pl.pallas_call(finish_kernel, grid=(8,), in_specs=[block] * 2, out_specs=...]
    unnamed x11 -> x14, local copies, waits for them, and re-layouts: 12.1 us -> 11.7 us
where the time goes in v7:
time: 457 us; the launch traced here: 453 us
  Pallas kernels  425 us (93%)
  local copies, waits for them, and re-layouts  19.3 us (4%)
  other arithmetic  7.99 us (2%)
    pallas_call x1, Pallas kernels, back_call(): pl.pallas_call(functools.partial(back_kernel, copies), in_specs=[inside]...  183 us
    pallas_call x1, Pallas kernels, middle_call(): pl.pallas_call(functools.partial(middle_kernel, copies), in_specs=[outsid...  126 us
    pallas_call x1, Pallas kernels, front_call(): pl.pallas_call(functools.partial(front_kernel, copies), in_specs=[inside]...  111 us
    unnamed x14, local copies, waits for them, and re-layouts  11.7 us

profile of v7, /device:TPU:0, one launch (start us, length us, event | category | flops | bytes accessed | tf_op | source)
XLA Modules:
  0.0 453.1 jit_solution(16296086882834409138)
XLA Ops:
  0.6 0.8 reduce-window.4
  1.5 0.1 convert_reduce_fusion
  1.6 0.7 fusion.4
  2.2 0.1 select_reduce_fusion
  2.3 1.0 copy.38.first_ref
  3.3 0.7 compare_convert_fusion
  4.0 1.0 copy.39.keep_ref
  5.0 1.3 convert_element_type.29
  6.3 0.0 copy-start.4
  6.3 0.0 copy-start.3
  6.3 110.5 %front.1 = (f32[1024,4]{1,0:T(8,128)}, f32[256,2048]{1,0:T(8,128)}, f32[1024,128]{1,0:T(8,128)}, f32[1024,128]{1,0:T(8,128)}, bf16[1024,2048]{1,0:T(8,128)(2,1)}...) custom-call(f32[1,2048]{1,0:T(1,128)} %bitcast.76, ...), custom_call_target="tpu_custom_call" | custom-call | flops 10737418240 | bytes 62914560 | tf_op jit(solution)/shard_map/front/pallas_call | solution.py:355
  116.9 0.0 copy-done.4
  116.9 0.7 pad_maximum_fusion
  117.5 1.3 copy.41.level_ref
  118.9 0.0 copy-done.3
  118.9 1.1 copy.40.router_ref
  120.0 126.1 %middle.1 = (bf16[256,2048]{1,0:T(8,128)(2,1)}, f32[256,2048]{1,0:T(8,128)}, bf16[256,2048]{1,0:T(8,128)(2,1)}, f32[6,2048]{1,0:T(8,128)}, bf16[4,256,2048]{2,1,...) custom-call(bf16[4,256,2048]{2,1,0:T(8,128)(2,1)} %get-tuple-element, ...), custom_call_target="tpu_custom_call" | custom-call | flops 51539607552 | bytes 83886080 | tf_op jit(solution)/shard_map/middle/pallas_call | solution.py:792
  246.0 182.9 %back.1 = (f32[4,256,512]{2,1,0:T(8,128)}, f32[8,2048]{1,0:T(8,128)}, bf16[4,256,2048]{2,1,0:T(8,128)(2,1)}, bf16[4,256,2048]{2,1,0:T(8,128)(2,1)}, bf16[1024,51...) custom-call(f32[1024,4]{1,0:T(8,128)} %get-tuple-element.45.log_ref,, ...), custom_call_target="tpu_custom_call" | custom-call | flops 22548578304 | bytes 83886080 | tf_op jit(solution)/shard_map/back/pallas_call | solution.py:1284
  428.9 3.7 fusion.1
  432.6 3.5 copy.45
  436.1 1.8 copy.46
  437.9 0.0 copy-start
  437.9 2.2 copy-done
  440.1 0.0 copy-start.1
  440.1 2.2 copy-done.1
  442.2 0.0 copy-start.2
  442.2 5.4 %finish.1 = (f32[1024,2048]{1,0:T(8,128)}, bf16[1024,2048]{1,0:T(8,128)(2,1)}) custom-call(bf16[1024,2048]{1,0:T(8,128)(2,1)S(1)} %bitcast.50, bf16[1024,2048]{1,0:T(8,128)(2,1)S(1)} %bitcast.49), custom_call_target="tpu_custom_call" | custom-call | bytes 20971520 | tf_op jit(solution)/shard_map/finish/pallas_call | solution.py:1357
  447.6 0.0 copy-done.2
  447.6 1.3 slice_bitcast_fusion
  448.9 1.0 copy.44
  449.9 1.5 fusion.5
  451.4 1.4 dynamic-slice_bitcast_fusion
  (1 shorter events, 0.0 us)
Async XLA Ops:
  6.3 110.5 %copy-start.4 = (f32[1024,1]{0,1:T(1,128)S(1)}, f32[1024,1]{0,1:T(1,128)}, u32[]{:S(2)}) copy-start(f32[1024,1]{0,1:T(1,128)} %convert_element_type.29) | copy-start | bytes 12292
  6.3 112.6 %copy-start.3 = (bf16[2048,4]{0,1:T(4,128)(2,1)S(1)}, bf16[2048,4]{0,1:T(4,128)(2,1)}, u32[]{:S(2)}) copy-start(bf16[2048,4]{0,1:T(4,128)(2,1)} %param.25) | copy-start | bytes 49156
  437.9 2.2 copy-start
  440.1 2.2 copy-start.1
  442.2 5.4 %copy-start.2 = (f32[4,256,512]{2,1,0:T(8,128)S(1)}, f32[4,256,512]{2,1,0:T(8,128)}, u32[]{:S(2)}) copy-start(f32[4,256,512]{2,1,0:T(8,128)} %get-tuple-element.74) | copy-start | bytes 6291460

commit v8 on v7

--- a/solution.py
+++ b/solution.py
@@ -1363,7 +1363,7 @@
             jax.ShapeDtypeStruct((rows, width), F32),
             jax.ShapeDtypeStruct((rows, width), BF16),
         ],
-        compiler_params=pltpu.CompilerParams(vmem_limit_bytes=24 << 20),
+        compiler_params=pltpu.CompilerParams(vmem_limit_bytes=62 << 20),
         cost_estimate=pl.CostEstimate(flops=0, bytes_accessed=10 * rows * width, transcendentals=0),
         name="finish",
     )(tokens_grad, mixed)

time: 457 us -> 460 us (level)
    unnamed x14 -> x8, local copies, waits for them, and re-layouts: 11.7 us -> 7.34 us
where the time goes in v8:
time: 460 us; the launch traced here: 455 us
  Pallas kernels  429 us (93%)
  local copies, waits for them, and re-layouts  17.3 us (4%)
  other arithmetic  8.01 us (2%)
    pallas_call x1, Pallas kernels, back_call(): pl.pallas_call(functools.partial(back_kernel, copies), in_specs=[inside]...  183 us
    pallas_call x1, Pallas kernels, middle_call(): pl.pallas_call(functools.partial(middle_kernel, copies), in_specs=[outsid...  126 us
    pallas_call x1, Pallas kernels, front_call(): pl.pallas_call(functools.partial(front_kernel, copies), in_specs=[inside]...  111 us
    pallas_call x1, Pallas kernels, finish_call(): pl.pallas_call(finish_kernel, grid=(8,), in_specs=[block] * 2, out_specs=...  9.58 us

profile of v8, /device:TPU:0, one launch (start us, length us, event | category | flops | bytes accessed | tf_op | source)
XLA Modules:
  0.0 455.4 jit_solution(8571019835592696684)
XLA Ops:
  0.6 0.8 reduce-window.4
  1.5 0.1 convert_reduce_fusion
  1.6 0.7 fusion.4
  2.2 0.1 select_reduce_fusion
  2.3 1.0 copy.38.first_ref
  3.3 0.7 compare_convert_fusion
  4.0 1.0 copy.39.keep_ref
  5.0 1.3 convert_element_type.29
  6.3 0.0 copy-start.1
  6.3 0.0 copy-start
  6.3 110.5 %front.1 = (f32[1024,4]{1,0:T(8,128)}, f32[256,2048]{1,0:T(8,128)}, f32[1024,128]{1,0:T(8,128)}, f32[1024,128]{1,0:T(8,128)}, bf16[1024,2048]{1,0:T(8,128)(2,1)}...) custom-call(f32[1,2048]{1,0:T(1,128)} %bitcast.76, ...), custom_call_target="tpu_custom_call" | custom-call | flops 10737418240 | bytes 62914560 | tf_op jit(solution)/shard_map/front/pallas_call | solution.py:355
  116.8 0.0 copy-done.1
  116.9 0.7 pad_maximum_fusion
  117.5 1.3 copy.41.level_ref
  118.9 0.0 copy-done
  118.9 1.1 copy.40.router_ref
  120.0 126.1 %middle.1 = (bf16[256,2048]{1,0:T(8,128)(2,1)}, f32[256,2048]{1,0:T(8,128)}, bf16[256,2048]{1,0:T(8,128)(2,1)}, f32[6,2048]{1,0:T(8,128)}, bf16[4,256,2048]{2,1,...) custom-call(bf16[4,256,2048]{2,1,0:T(8,128)(2,1)} %get-tuple-element, ...), custom_call_target="tpu_custom_call" | custom-call | flops 51539607552 | bytes 83886080 | tf_op jit(solution)/shard_map/middle/pallas_call | solution.py:792
  246.0 182.9 %back.1 = (f32[4,256,512]{2,1,0:T(8,128)}, f32[8,2048]{1,0:T(8,128)}, bf16[4,256,2048]{2,1,0:T(8,128)(2,1)}, bf16[4,256,2048]{2,1,0:T(8,128)(2,1)}, bf16[1024,51...) custom-call(f32[1024,4]{1,0:T(8,128)} %get-tuple-element.45.log_ref,, ...), custom_call_target="tpu_custom_call" | custom-call | flops 22548578304 | bytes 83886080 | tf_op jit(solution)/shard_map/back/pallas_call | solution.py:1284
  429.0 3.7 fusion.1
  432.7 3.5 copy.45
  436.1 1.8 copy.46
  437.9 9.6 %finish.1 = (f32[1024,2048]{1,0:T(8,128)}, bf16[1024,2048]{1,0:T(8,128)(2,1)}) custom-call(bf16[1024,2048]{1,0:T(8,128)(2,1)} %bitcast.50, bf16[1024,2048]{1,0:T(8,128)(2,1)} %bitcast.49), custom_call_target="tpu_custom_call" | custom-call | bytes 20971520 | tf_op jit(solution)/shard_map/finish/pallas_call | solution.py:1357
  447.5 2.7 slice_bitcast_fusion
  450.2 1.1 slice_bitcast_fusion.1
  451.3 1.0 copy.44
  452.3 1.5 fusion.5
  453.8 1.4 dynamic-slice_bitcast_fusion
Async XLA Ops:
  6.3 110.5 %copy-start.1 = (f32[1024,1]{0,1:T(1,128)S(1)}, f32[1024,1]{0,1:T(1,128)}, u32[]{:S(2)}) copy-start(f32[1024,1]{0,1:T(1,128)} %convert_element_type.29) | copy-start | bytes 12292
  6.3 112.6 %copy-start = (bf16[2048,4]{0,1:T(4,128)(2,1)S(1)}, bf16[2048,4]{0,1:T(4,128)(2,1)}, u32[]{:S(2)}) copy-start(bf16[2048,4]{0,1:T(4,128)(2,1)} %param.25) | copy-start | bytes 49156
